TPU v7x, 512 devices: a whole 4x8x8 slice. The times are simulated.
512 devices in a mesh: ctx: 64 (over x, y_lo, z), head: 8 (over y_hi, core).
Axes of the slice: x: 4, y: 8 (y_hi: 4, y_lo: 2; y = y_hi * 2 + y_lo), z: 8, core: 2. Of those that a mesh axis runs over, the one named last changes fastest.
Arguments:
- queries: bfloat16 [16384, 8192], P(('ctx', 'head')), may hold values from -6 to 6
- grad_out: bfloat16 [16384, 8192], P(('ctx', 'head')), may hold values from -3 to 3
- outputs: bfloat16 [16384, 8192], P(('ctx', 'head')), may hold values from -3 to 3
- keys: bfloat16 [16384, 1024], P(('ctx', 'head')), may hold values from -6 to 6
- values: bfloat16 [16384, 1024], P(('ctx', 'head')), may hold values from -6 to 6
- log_sum_exp: float32 [16384, 64], P(('ctx', 'head')), may hold values from 1 to 4
- doc_start: int32 [16384], P('ctx'), may hold values from 0 to 16383, as said below
Outputs:
- grad_queries: bfloat16 [16384, 8192], P(('ctx', 'head'))
- grad_keys: float32 [16384, 1024], P('ctx', 'head')
- grad_values: float32 [16384, 1024], P('ctx', 'head')
Inputs may be any that keep to these rules, and one draw needn't show every extreme that they name: doc_start never falls along the sequence, doc_start[t] <= t, and doc_start[t] is the position where a document begins (doc_start[doc_start[t]] = doc_start[t]); every document holds at most 1536 tokens and some document holds exactly 1536.
All inputs are finite; a program needn't handle non-finite values.
Results may differ from a plain program's by a relative error of at most 0.0061.
Values may be sent and summed in bfloat16 or wider, within the bound.
No kernel may reach another device: no remote copies, remote signals or barrier semaphores. Data moves between devices by JAX's collectives and lax.ppermute only.
A program may use at most 64 MiB of HBM per device.

v0:
```python
import jax
import jax.numpy as jnp
from jax import lax
from jax.sharding import PartitionSpec as P

REACH = 6


def from_behind(array, axis, by):
    size = lax.axis_size(axis)
    pairs = [(i, i + by) for i in range(size) if 0 <= i + by < size]
    return lax.ppermute(array, axis, pairs)


def pair_grads(query, dout, lse, delta, qpos, start, key, value, kpos, scale):
    allowed = (kpos[None, :] >= start[:, None]) & (kpos[None, :] <= qpos[:, None])
    score = jnp.einsum("tghd,wgd->gthw", query, key, preferred_element_type=jnp.float32) * scale
    prob = jnp.where(allowed[None, :, None, :], jnp.exp(score - lse[..., None]), 0.0)
    grad_prob = jnp.einsum("tghd,wgd->gthw", dout, value, preferred_element_type=jnp.float32)
    grad_score = prob * (grad_prob - delta[..., None])
    prob_half = prob.astype(jnp.bfloat16)
    score_half = grad_score.astype(jnp.bfloat16)
    grad_q = (
        jnp.einsum("gthw,wgd->tghd", score_half, key, preferred_element_type=jnp.float32) * scale
    )
    grad_k = (
        jnp.einsum("gthw,tghd->wgd", score_half, query, preferred_element_type=jnp.float32) * scale
    )
    grad_v = jnp.einsum("gthw,tghd->wgd", prob_half, dout, preferred_element_type=jnp.float32)
    return (grad_q, grad_k, grad_v)


def per_device(queries, grad_out, outputs, keys, values, log_sum_exp, doc_start):
    rows, wide = queries.shape
    heads = log_sum_exp.shape[1]
    size = wide // heads
    kv_heads = keys.shape[1] // size
    per_head = heads // kv_heads
    scale = size ** (-0.5)
    delta = jnp.sum(
        (grad_out.astype(jnp.float32) * outputs.astype(jnp.float32)).reshape(rows, heads, size),
        axis=2,
    )
    query, dout, key_rows, value_rows = (
        lax.all_to_all(queries, "head", split_axis=1, concat_axis=0, tiled=True),
        lax.all_to_all(grad_out, "head", split_axis=1, concat_axis=0, tiled=True),
        lax.all_to_all(keys, "head", split_axis=1, concat_axis=0, tiled=True),
        lax.all_to_all(values, "head", split_axis=1, concat_axis=0, tiled=True),
    )
    lse_rows, delta_rows = (
        lax.all_to_all(log_sum_exp, "head", split_axis=1, concat_axis=0, tiled=True),
        lax.all_to_all(delta, "head", split_axis=1, concat_axis=0, tiled=True),
    )
    block = query.shape[0]
    local = key_rows.shape[1] // size
    query = query.reshape(block, local, per_head, size)
    dout = dout.reshape(block, local, per_head, size)
    key = key_rows.reshape(block, local, size)
    value = value_rows.reshape(block, local, size)
    lse = jnp.transpose(lse_rows.reshape(block, local, per_head), (1, 0, 2))
    dlt = jnp.transpose(delta_rows.reshape(block, local, per_head), (1, 0, 2))
    qpos = lax.axis_index("ctx") * block + jnp.arange(block, dtype=jnp.int32)
    grad_q, grad_k, grad_v = pair_grads(
        query, dout, lse, dlt, qpos, doc_start, key, value, qpos, scale
    )
    for step in range(1, REACH + 1):
        key_far, value_far = from_behind((key, value), "ctx", step)
        kpos = qpos - step * block
        part_q, part_k, part_v = pair_grads(
            query, dout, lse, dlt, qpos, doc_start, key_far, value_far, kpos, scale
        )
        grad_q = grad_q + part_q
        back_k, back_v = from_behind((part_k, part_v), "ctx", -step)
        grad_k = grad_k + back_k
        grad_v = grad_v + back_v
    grad_half = grad_q.astype(jnp.bfloat16).reshape(block, local * per_head * size)
    grad_rows = lax.all_to_all(grad_half, "head", split_axis=0, concat_axis=1, tiled=True)
    return (grad_rows, grad_k.reshape(block, local * size), grad_v.reshape(block, local * size))


def solution(mesh):
    return jax.shard_map(
        per_device,
        mesh=mesh,
        in_specs=(
            P(("ctx", "head"), None),
            P(("ctx", "head"), None),
            P(("ctx", "head"), None),
            P(("ctx", "head"), None),
            P(("ctx", "head"), None),
            P(("ctx", "head"), None),
            P("ctx"),
        ),
        out_specs=(P(("ctx", "head"), None), P("ctx", "head"), P("ctx", "head")),
        check_vma=False,
    )
```

profile of v0, /device:TPU:132, one launch (start us, length us, event | category | flops | bytes accessed | tf_op | source)
XLA Modules:
  0.0 272.2 jit_solution(5711585808853193430)
XLA Ops:
  2.2 7.1 %all-to-all-start.2 = ((f32[8,1,256]{2,1,0:T(1,128)}), f32[8,1,256]{2,1,0:T(1,128)S(1)}, u32[]{:S(2)}, u32[]{:S(2)}) async-start(f32[8,1,256]{2,1,0:T(1,128)} %reshape.786), calls=%async_computation.2 | async-start | bytes 16384 | tf_op jit(solution)/shard_map/all_to_all | solution.py:51
  11.9 5.1 %all-to-all-done.2 = f32[8,1,256]{2,1,0:T(1,128)S(1)} async-done(((f32[8,1,256]{2,1,0:T(1,128)}), f32[8,1,256]{2,1,0:T(1,128)S(1)}, u32[]{:S(2)}, u32[]{:S(2)}) %all-to-all-start.2) | async-done | bytes 8224 | tf_op jit(solution)/shard_map/all_to_all | solution.py:51
  17.0 3.3 %all-to-all-start.5 = ((f32[8,1,256]{2,1,0:T(1,128)}), f32[8,1,256]{2,1,0:T(1,128)S(1)}, u32[]{:S(2)}, u32[]{:S(2)}) async-start(f32[8,1,256]{2,1,0:T(1,128)} %reshape.788), calls=%async_computation.5 | async-start | bytes 16384 | tf_op jit(solution)/shard_map/all_to_all | solution.py:52
  21.0 7.0 %all-to-all-done.5 = f32[8,1,256]{2,1,0:T(1,128)S(1)} async-done(((f32[8,1,256]{2,1,0:T(1,128)}), f32[8,1,256]{2,1,0:T(1,128)S(1)}, u32[]{:S(2)}, u32[]{:S(2)}) %all-to-all-start.5) | async-done | bytes 8224 | tf_op jit(solution)/shard_map/all_to_all | solution.py:52
  28.0 3.4 %all-to-all-start.1 = ((bf16[32,8,128]{2,0,1:T(8,128)(2,1)}), bf16[32,8,128]{2,0,1:T(8,128)(2,1)S(1)}, u32[]{:S(2)}, u32[]{:S(2)}) async-start(bf16[32,8,128]{2,0,1:T(8,128)(2,1)} %copy_bitcast_fusion.3), calls=%async_computation.1 | async-start | bytes 131072 | tf_op jit(solution)/shard_map/all_to_all | solution.py:47
  32.0 7.5 %all-to-all-done.1 = bf16[32,8,128]{2,0,1:T(8,128)(2,1)S(1)} async-done(((bf16[32,8,128]{2,0,1:T(8,128)(2,1)}), bf16[32,8,128]{2,0,1:T(8,128)(2,1)S(1)}, u32[]{:S(2)}, u32[]{:S(2)}) %all-to-all-start.1) | async-done | bytes 65568 | tf_op jit(solution)/shard_map/all_to_all | solution.py:47
  39.5 3.4 %all-to-all-start.4 = ((bf16[32,8,128]{2,0,1:T(8,128)(2,1)}), bf16[32,8,128]{2,0,1:T(8,128)(2,1)S(1)}, u32[]{:S(2)}, u32[]{:S(2)}) async-start(bf16[32,8,128]{2,0,1:T(8,128)(2,1)} %copy_bitcast_fusion.2), calls=%async_computation.4 | async-start | bytes 131072 | tf_op jit(solution)/shard_map/all_to_all | solution.py:48
  43.7 7.4 %all-to-all-done.4 = bf16[32,8,128]{2,0,1:T(8,128)(2,1)S(1)} async-done(((bf16[32,8,128]{2,0,1:T(8,128)(2,1)}), bf16[32,8,128]{2,0,1:T(8,128)(2,1)S(1)}, u32[]{:S(2)}, u32[]{:S(2)}) %all-to-all-start.4) | async-done | bytes 65568 | tf_op jit(solution)/shard_map/all_to_all | solution.py:48
  51.1 3.5 %all-to-all-start = ((bf16[32,8,1024]{2,0,1:T(8,128)(2,1)}), bf16[32,8,1024]{2,0,1:T(8,128)(2,1)S(1)}, u32[]{:S(2)}, u32[]{:S(2)}) async-start(bf16[32,8,1024]{2,0,1:T(8,128)(2,1)} %bitcast.338), calls=%async_computation | async-start | bytes 1048576 | tf_op jit(solution)/shard_map/all_to_all | solution.py:45
  55.5 17.1 %all-to-all-done = bf16[32,8,1024]{2,0,1:T(8,128)(2,1)S(1)} async-done(((bf16[32,8,1024]{2,0,1:T(8,128)(2,1)}), bf16[32,8,1024]{2,0,1:T(8,128)(2,1)S(1)}, u32[]{:S(2)}, u32[]{:S(2)}) %all-to-all-start) | async-done | bytes 524320 | tf_op jit(solution)/shard_map/all_to_all | solution.py:45
  72.6 3.5 %all-to-all-start.3 = ((bf16[32,8,1024]{2,0,1:T(8,128)(2,1)}), bf16[32,8,1024]{2,0,1:T(8,128)(2,1)S(1)}, u32[]{:S(2)}, u32[]{:S(2)}) async-start(bf16[32,8,1024]{2,0,1:T(8,128)(2,1)} %bitcast.337), calls=%async_computation.3 | async-start | bytes 1048576 | tf_op jit(solution)/shard_map/all_to_all | solution.py:46
  78.6 4.3 %collective-permute-start = (bf16[256,1,128]{2,0,1:T(8,128)(2,1)S(1)}, bf16[256,1,128]{2,0,1:T(8,128)(2,1)S(1)}, u32[]{:S(2)}, u32[]{:S(2)}) collective-permute-start(bf16[256,1,128]{2,0,1:T(8,128)(2,1)S(1)} %bitcast.380), channel_id=1, source_target_pairs={{0,8},{8,16},{16,24},{24,32},{32,40},{40,48},{48,56},{56,64},{64,7... | collective-permute-start | bytes 196616 | tf_op jit(solution)/shard_map/ppermute | solution.py:12
  85.0 9.3 %collective-permute-start.9 = (bf16[256,1,128]{2,0,1:T(8,128)(2,1)S(1)}, bf16[256,1,128]{2,0,1:T(8,128)(2,1)S(1)}, u32[]{:S(2)}, u32[]{:S(2)}) collective-permute-start(bf16[256,1,128]{2,0,1:T(8,128)(2,1)S(1)} %bitcast.374), channel_id=1, source_target_pairs={{0,40},{8,48},{16,56},{24,64},{32,72},{40,80},{48,88},{56,96},{64,... | collective-permute-start | bytes 196616 | tf_op jit(solution)/shard_map/ppermute | solution.py:12
  97.4 6.8 %collective-permute-start.5 = (bf16[256,1,128]{2,0,1:T(8,128)(2,1)S(1)}, bf16[256,1,128]{2,0,1:T(8,128)(2,1)S(1)}, u32[]{:S(2)}, u32[]{:S(2)}) collective-permute-start(bf16[256,1,128]{2,0,1:T(8,128)(2,1)S(1)} %bitcast.376), channel_id=1, source_target_pairs={{0,24},{8,32},{16,40},{24,48},{32,56},{40,64},{48,72},{56,80},{64,... | collective-permute-start | bytes 196616 | tf_op jit(solution)/shard_map/ppermute | solution.py:12
  104.4 4.3 %collective-permute-start.2 = (bf16[256,1,128]{2,0,1:T(8,128)(2,1)S(1)}, bf16[256,1,128]{2,0,1:T(8,128)(2,1)S(1)}, u32[]{:S(2)}, u32[]{:S(2)}) collective-permute-start(bf16[256,1,128]{2,0,1:T(8,128)(2,1)S(1)} %bitcast.381), channel_id=1, source_target_pairs={{0,16},{8,24},{16,32},{24,40},{32,48},{40,56},{48,64},{56,72},{64,... | collective-permute-start | bytes 196616 | tf_op jit(solution)/shard_map/ppermute | solution.py:12
  111.7 6.6 %collective-permute-start.4 = (bf16[256,1,128]{2,0,1:T(8,128)(2,1)S(1)}, bf16[256,1,128]{2,0,1:T(8,128)(2,1)S(1)}, u32[]{:S(2)}, u32[]{:S(2)}) collective-permute-start(bf16[256,1,128]{2,0,1:T(8,128)(2,1)S(1)} %bitcast.382), channel_id=1, source_target_pairs={{0,24},{8,32},{16,40},{24,48},{32,56},{40,64},{48,72},{56,80},{64,... | collective-permute-start | bytes 196616 | tf_op jit(solution)/shard_map/ppermute | solution.py:12
  122.7 5.7 %collective-permute-start.6 = (bf16[256,1,128]{2,0,1:T(8,128)(2,1)S(1)}, bf16[256,1,128]{2,0,1:T(8,128)(2,1)S(1)}, u32[]{:S(2)}, u32[]{:S(2)}) collective-permute-start(bf16[256,1,128]{2,0,1:T(8,128)(2,1)S(1)} %bitcast.383), channel_id=1, source_target_pairs={{0,32},{8,40},{16,48},{24,56},{32,64},{40,72},{48,80},{56,88},{64,... | collective-permute-start | bytes 196616 | tf_op jit(solution)/shard_map/ppermute | solution.py:12
  130.3 4.3 %collective-permute-done.6 = bf16[256,1,128]{2,0,1:T(8,128)(2,1)S(1)} collective-permute-done((bf16[256,1,128]{2,0,1:T(8,128)(2,1)S(1)}, bf16[256,1,128]{2,0,1:T(8,128)(2,1)S(1)}, u32[]{:S(2)}, u32[]{:S(2)}) %collective-permute-start.6) | collective-permute-done | bytes 65568 | tf_op jit(solution)/shard_map/ppermute | solution.py:12
  134.5 5.3 %collective-permute-start.8 = (bf16[256,1,128]{2,0,1:T(8,128)(2,1)S(1)}, bf16[256,1,128]{2,0,1:T(8,128)(2,1)S(1)}, u32[]{:S(2)}, u32[]{:S(2)}) collective-permute-start(bf16[256,1,128]{2,0,1:T(8,128)(2,1)S(1)} %bitcast.384), channel_id=1, source_target_pairs={{0,40},{8,48},{16,56},{24,64},{32,72},{40,80},{48,88},{56,96},{64,... | collective-permute-start | bytes 196616 | tf_op jit(solution)/shard_map/ppermute | solution.py:12
  141.8 4.5 %collective-permute-done.8 = bf16[256,1,128]{2,0,1:T(8,128)(2,1)S(1)} collective-permute-done((bf16[256,1,128]{2,0,1:T(8,128)(2,1)S(1)}, bf16[256,1,128]{2,0,1:T(8,128)(2,1)S(1)}, u32[]{:S(2)}, u32[]{:S(2)}) %collective-permute-start.8) | collective-permute-done | bytes 65568 | tf_op jit(solution)/shard_map/ppermute | solution.py:12
  150.8 4.3 %collective-permute-done.1 = bf16[256,1,128]{2,0,1:T(8,128)(2,1)S(1)} collective-permute-done((bf16[256,1,128]{2,0,1:T(8,128)(2,1)S(1)}, bf16[256,1,128]{2,0,1:T(8,128)(2,1)S(1)}, u32[]{:S(2)}, u32[]{:S(2)}) %collective-permute-start.1) | collective-permute-done | bytes 65568 | tf_op jit(solution)/shard_map/ppermute | solution.py:12
  162.2 4.2 %collective-permute-start.12 = (f32[256,1,128]{2,0,1:T(8,128)}, f32[256,1,128]{2,0,1:T(8,128)S(1)}, u32[]{:S(2)}, u32[]{:S(2)}) collective-permute-start(f32[256,1,128]{2,0,1:T(8,128)} %fusion.22), channel_id=1, source_target_pairs={{8,0},{16,8},{24,16},{32,24},{40,32},{48,40},{56,48},{64,56},{72,6... | collective-permute-start | bytes 393224 | tf_op jit(solution)/shard_map/ppermute | solution.py:12
  175.9 5.9 %collective-permute-start.13 = (f32[256,1,128]{2,0,1:T(8,128)}, f32[256,1,128]{2,0,1:T(8,128)}, u32[]{:S(2)}, u32[]{:S(2)}) collective-permute-start(f32[256,1,128]{2,0,1:T(8,128)} %fusion.20), channel_id=1, source_target_pairs={{16,0},{24,8},{32,16},{40,24},{48,32},{56,40},{64,48},{72,56},{80,... | collective-permute-start | bytes 393224 | tf_op jit(solution)/shard_map/ppermute | solution.py:12
  182.8 4.3 %collective-permute-start.14 = (f32[256,1,128]{2,0,1:T(8,128)}, f32[256,1,128]{2,0,1:T(8,128)}, u32[]{:S(2)}, u32[]{:S(2)}) collective-permute-start(f32[256,1,128]{2,0,1:T(8,128)} %fusion.18), channel_id=1, source_target_pairs={{24,0},{32,8},{40,16},{48,24},{56,32},{64,40},{72,48},{80,56},{88,... | collective-permute-start | bytes 393224 | tf_op jit(solution)/shard_map/ppermute | solution.py:12
  189.2 5.7 %collective-permute-start.15 = (f32[256,1,128]{2,0,1:T(8,128)}, f32[256,1,128]{2,0,1:T(8,128)}, u32[]{:S(2)}, u32[]{:S(2)}) collective-permute-start(f32[256,1,128]{2,0,1:T(8,128)} %fusion.16), channel_id=1, source_target_pairs={{32,0},{40,8},{48,16},{56,24},{64,32},{72,40},{80,48},{88,56},{96,... | collective-permute-start | bytes 393224 | tf_op jit(solution)/shard_map/ppermute | solution.py:12
  199.9 7.1 %all-to-all-start.6 = ((bf16[8,32,1024]{2,1,0:T(8,128)(2,1)}), bf16[8,32,1024]{2,1,0:T(8,128)(2,1)}, u32[]{:S(2)}, u32[]{:S(2)}) async-start(bf16[8,32,1024]{2,1,0:T(8,128)(2,1)} %all_to_all.104), calls=%async_computation.6 | async-start | bytes 1048576 | tf_op jit(solution)/shard_map/all_to_all | solution.py:77
  209.8 6.6 %collective-permute-start.17 = (f32[256,1,128]{2,0,1:T(8,128)S(1)}, f32[256,1,128]{2,0,1:T(8,128)S(1)}, u32[]{:S(2)}, u32[]{:S(2)}) collective-permute-start(f32[256,1,128]{2,0,1:T(8,128)S(1)} %fusion.12), channel_id=1, source_target_pairs={{48,0},{56,8},{64,16},{72,24},{80,32},{88,40},{96,48},{104,56},{11... | collective-permute-start | bytes 393224 | tf_op jit(solution)/shard_map/ppermute | solution.py:12
  218.5 4.8 %collective-permute-start.19 = (f32[256,1,128]{2,0,1:T(8,128)S(1)}, f32[256,1,128]{2,0,1:T(8,128)S(1)}, u32[]{:S(2)}, u32[]{:S(2)}) collective-permute-start(f32[256,1,128]{2,0,1:T(8,128)S(1)} %copy-done.6), channel_id=1, source_target_pairs={{16,0},{24,8},{32,16},{40,24},{48,32},{56,40},{64,48},{72,56},{80,... | collective-permute-start | bytes 393224 | tf_op jit(solution)/shard_map/ppermute | solution.py:12
  223.3 4.5 %collective-permute-start.20 = (f32[256,1,128]{2,0,1:T(8,128)S(1)}, f32[256,1,128]{2,0,1:T(8,128)S(1)}, u32[]{:S(2)}, u32[]{:S(2)}) collective-permute-start(f32[256,1,128]{2,0,1:T(8,128)S(1)} %copy-done.7), channel_id=1, source_target_pairs={{24,0},{32,8},{40,16},{48,24},{56,32},{64,40},{72,48},{80,56},{88,... | collective-permute-start | bytes 393224 | tf_op jit(solution)/shard_map/ppermute | solution.py:12
  227.9 4.3 %collective-permute-start.21 = (f32[256,1,128]{2,0,1:T(8,128)S(1)}, f32[256,1,128]{2,0,1:T(8,128)S(1)}, u32[]{:S(2)}, u32[]{:S(2)}) collective-permute-start(f32[256,1,128]{2,0,1:T(8,128)S(1)} %copy-done.8), channel_id=1, source_target_pairs={{32,0},{40,8},{48,16},{56,24},{64,32},{72,40},{80,48},{88,56},{96,... | collective-permute-start | bytes 393224 | tf_op jit(solution)/shard_map/ppermute | solution.py:12
  242.5 4.0 %collective-permute-done.21 = f32[256,1,128]{2,0,1:T(8,128)S(1)} collective-permute-done((f32[256,1,128]{2,0,1:T(8,128)S(1)}, f32[256,1,128]{2,0,1:T(8,128)S(1)}, u32[]{:S(2)}, u32[]{:S(2)}) %collective-permute-start.21) | collective-permute-done | bytes 131104 | tf_op jit(solution)/shard_map/ppermute | solution.py:12
  246.6 22.5 %collective-permute-done.23 = f32[256,1,128]{2,0,1:T(8,128)S(1)} collective-permute-done((f32[256,1,128]{2,0,1:T(8,128)S(1)}, f32[256,1,128]{2,0,1:T(8,128)S(1)}, u32[]{:S(2)}, u32[]{:S(2)}) %collective-permute-start.23) | collective-permute-done | bytes 131104 | tf_op jit(solution)/shard_map/ppermute | solution.py:12
  (127 shorter events, 73.6 us)
Async XLA Ops:
  2.2 14.8 %all-to-all-start.2 = ((f32[8,1,256]{2,1,0:T(1,128)}), f32[8,1,256]{2,1,0:T(1,128)S(1)}, u32[]{:S(2)}, u32[]{:S(2)}) async-start(f32[8,1,256]{2,1,0:T(1,128)} %reshape.786), calls=%async_computation.2 | async-start | bytes 16384 | tf_op jit(solution)/shard_map/all_to_all | solution.py:51
  17.0 11.0 %all-to-all-start.5 = ((f32[8,1,256]{2,1,0:T(1,128)}), f32[8,1,256]{2,1,0:T(1,128)S(1)}, u32[]{:S(2)}, u32[]{:S(2)}) async-start(f32[8,1,256]{2,1,0:T(1,128)} %reshape.788), calls=%async_computation.5 | async-start | bytes 16384 | tf_op jit(solution)/shard_map/all_to_all | solution.py:52
  28.0 11.5 %all-to-all-start.1 = ((bf16[32,8,128]{2,0,1:T(8,128)(2,1)}), bf16[32,8,128]{2,0,1:T(8,128)(2,1)S(1)}, u32[]{:S(2)}, u32[]{:S(2)}) async-start(bf16[32,8,128]{2,0,1:T(8,128)(2,1)} %copy_bitcast_fusion.3), calls=%async_computation.1 | async-start | bytes 131072 | tf_op jit(solution)/shard_map/all_to_all | solution.py:47
  39.5 11.6 %all-to-all-start.4 = ((bf16[32,8,128]{2,0,1:T(8,128)(2,1)}), bf16[32,8,128]{2,0,1:T(8,128)(2,1)S(1)}, u32[]{:S(2)}, u32[]{:S(2)}) async-start(bf16[32,8,128]{2,0,1:T(8,128)(2,1)} %copy_bitcast_fusion.2), calls=%async_computation.4 | async-start | bytes 131072 | tf_op jit(solution)/shard_map/all_to_all | solution.py:48
  51.1 21.4 %all-to-all-start = ((bf16[32,8,1024]{2,0,1:T(8,128)(2,1)}), bf16[32,8,1024]{2,0,1:T(8,128)(2,1)S(1)}, u32[]{:S(2)}, u32[]{:S(2)}) async-start(bf16[32,8,1024]{2,0,1:T(8,128)(2,1)} %bitcast.338), calls=%async_computation | async-start | bytes 1048576 | tf_op jit(solution)/shard_map/all_to_all | solution.py:45
  72.6 31.7 %all-to-all-start.3 = ((bf16[32,8,1024]{2,0,1:T(8,128)(2,1)}), bf16[32,8,1024]{2,0,1:T(8,128)(2,1)S(1)}, u32[]{:S(2)}, u32[]{:S(2)}) async-start(bf16[32,8,1024]{2,0,1:T(8,128)(2,1)} %bitcast.337), calls=%async_computation.3 | async-start | bytes 1048576 | tf_op jit(solution)/shard_map/all_to_all | solution.py:46
  78.6 25.8 %collective-permute-start = (bf16[256,1,128]{2,0,1:T(8,128)(2,1)S(1)}, bf16[256,1,128]{2,0,1:T(8,128)(2,1)S(1)}, u32[]{:S(2)}, u32[]{:S(2)}) collective-permute-start(bf16[256,1,128]{2,0,1:T(8,128)(2,1)S(1)} %bitcast.380), channel_id=1, source_target_pairs={{0,8},{8,16},{16,24},{24,32},{32,40},{40,48},{48,56},{56,64},{64,7... | collective-permute-start | bytes 196616 | tf_op jit(solution)/shard_map/ppermute | solution.py:12
  83.1 106.1 %collective-permute-start.11 = (bf16[256,1,128]{2,0,1:T(8,128)(2,1)S(1)}, bf16[256,1,128]{2,0,1:T(8,128)(2,1)S(1)}, u32[]{:S(2)}, u32[]{:S(2)}) collective-permute-start(bf16[256,1,128]{2,0,1:T(8,128)(2,1)S(1)} %bitcast.373), channel_id=1, source_target_pairs={{0,48},{8,56},{16,64},{24,72},{32,80},{40,88},{48,96},{56,104},{64... | collective-permute-start | bytes 196616 | tf_op jit(solution)/shard_map/ppermute | solution.py:12
  85.0 77.2 %collective-permute-start.9 = (bf16[256,1,128]{2,0,1:T(8,128)(2,1)S(1)}, bf16[256,1,128]{2,0,1:T(8,128)(2,1)S(1)}, u32[]{:S(2)}, u32[]{:S(2)}) collective-permute-start(bf16[256,1,128]{2,0,1:T(8,128)(2,1)S(1)} %bitcast.374), channel_id=1, source_target_pairs={{0,40},{8,48},{16,56},{24,64},{32,72},{40,80},{48,88},{56,96},{64,... | collective-permute-start | bytes 196616 | tf_op jit(solution)/shard_map/ppermute | solution.py:12
  94.3 81.7 %collective-permute-start.7 = (bf16[256,1,128]{2,0,1:T(8,128)(2,1)S(1)}, bf16[256,1,128]{2,0,1:T(8,128)(2,1)S(1)}, u32[]{:S(2)}, u32[]{:S(2)}) collective-permute-start(bf16[256,1,128]{2,0,1:T(8,128)(2,1)S(1)} %bitcast.375), channel_id=1, source_target_pairs={{0,32},{8,40},{16,48},{24,56},{32,64},{40,72},{48,80},{56,88},{64,... | collective-permute-start | bytes 196616 | tf_op jit(solution)/shard_map/ppermute | solution.py:12
  97.4 61.3 %collective-permute-start.5 = (bf16[256,1,128]{2,0,1:T(8,128)(2,1)S(1)}, bf16[256,1,128]{2,0,1:T(8,128)(2,1)S(1)}, u32[]{:S(2)}, u32[]{:S(2)}) collective-permute-start(bf16[256,1,128]{2,0,1:T(8,128)(2,1)S(1)} %bitcast.376), channel_id=1, source_target_pairs={{0,24},{8,32},{16,40},{24,48},{32,56},{40,64},{48,72},{56,80},{64,... | collective-permute-start | bytes 196616 | tf_op jit(solution)/shard_map/ppermute | solution.py:12
  104.4 7.3 %collective-permute-start.2 = (bf16[256,1,128]{2,0,1:T(8,128)(2,1)S(1)}, bf16[256,1,128]{2,0,1:T(8,128)(2,1)S(1)}, u32[]{:S(2)}, u32[]{:S(2)}) collective-permute-start(bf16[256,1,128]{2,0,1:T(8,128)(2,1)S(1)} %bitcast.381), channel_id=1, source_target_pairs={{0,16},{8,24},{16,32},{24,40},{32,48},{40,56},{48,64},{56,72},{64,... | collective-permute-start | bytes 196616 | tf_op jit(solution)/shard_map/ppermute | solution.py:12
  111.7 11.0 %collective-permute-start.4 = (bf16[256,1,128]{2,0,1:T(8,128)(2,1)S(1)}, bf16[256,1,128]{2,0,1:T(8,128)(2,1)S(1)}, u32[]{:S(2)}, u32[]{:S(2)}) collective-permute-start(bf16[256,1,128]{2,0,1:T(8,128)(2,1)S(1)} %bitcast.382), channel_id=1, source_target_pairs={{0,24},{8,32},{16,40},{24,48},{32,56},{40,64},{48,72},{56,80},{64,... | collective-permute-start | bytes 196616 | tf_op jit(solution)/shard_map/ppermute | solution.py:12
  122.7 11.9 %collective-permute-start.6 = (bf16[256,1,128]{2,0,1:T(8,128)(2,1)S(1)}, bf16[256,1,128]{2,0,1:T(8,128)(2,1)S(1)}, u32[]{:S(2)}, u32[]{:S(2)}) collective-permute-start(bf16[256,1,128]{2,0,1:T(8,128)(2,1)S(1)} %bitcast.383), channel_id=1, source_target_pairs={{0,32},{8,40},{16,48},{24,56},{32,64},{40,72},{48,80},{56,88},{64,... | collective-permute-start | bytes 196616 | tf_op jit(solution)/shard_map/ppermute | solution.py:12
  134.5 11.7 %collective-permute-start.8 = (bf16[256,1,128]{2,0,1:T(8,128)(2,1)S(1)}, bf16[256,1,128]{2,0,1:T(8,128)(2,1)S(1)}, u32[]{:S(2)}, u32[]{:S(2)}) collective-permute-start(bf16[256,1,128]{2,0,1:T(8,128)(2,1)S(1)} %bitcast.384), channel_id=1, source_target_pairs={{0,40},{8,48},{16,56},{24,64},{32,72},{40,80},{48,88},{56,96},{64,... | collective-permute-start | bytes 196616 | tf_op jit(solution)/shard_map/ppermute | solution.py:12
  146.3 8.8 %collective-permute-start.1 = (bf16[256,1,128]{2,0,1:T(8,128)(2,1)S(1)}, bf16[256,1,128]{2,0,1:T(8,128)(2,1)S(1)}, u32[]{:S(2)}, u32[]{:S(2)}) collective-permute-start(bf16[256,1,128]{2,0,1:T(8,128)(2,1)S(1)} %bitcast.377), channel_id=1, source_target_pairs={{0,8},{8,16},{16,24},{24,32},{32,40},{40,48},{48,56},{56,64},{64,7... | collective-permute-start | bytes 196616 | tf_op jit(solution)/shard_map/ppermute | solution.py:12
  155.1 15.9 %collective-permute-start.3 = (bf16[256,1,128]{2,0,1:T(8,128)(2,1)S(1)}, bf16[256,1,128]{2,0,1:T(8,128)(2,1)S(1)}, u32[]{:S(2)}, u32[]{:S(2)}) collective-permute-start(bf16[256,1,128]{2,0,1:T(8,128)(2,1)S(1)} %bitcast.378), channel_id=1, source_target_pairs={{0,16},{8,24},{16,32},{24,40},{32,48},{40,56},{48,64},{56,72},{64,... | collective-permute-start | bytes 196616 | tf_op jit(solution)/shard_map/ppermute | solution.py:12
  158.7 24.1 %collective-permute-start.10 = (bf16[256,1,128]{2,0,1:T(8,128)(2,1)S(1)}, bf16[256,1,128]{2,0,1:T(8,128)(2,1)S(1)}, u32[]{:S(2)}, u32[]{:S(2)}) collective-permute-start(bf16[256,1,128]{2,0,1:T(8,128)(2,1)S(1)} %bitcast.385), channel_id=1, source_target_pairs={{0,48},{8,56},{16,64},{24,72},{32,80},{40,88},{48,96},{56,104},{64... | collective-permute-start | bytes 196616 | tf_op jit(solution)/shard_map/ppermute | solution.py:12
  162.2 45.3 %collective-permute-start.12 = (f32[256,1,128]{2,0,1:T(8,128)}, f32[256,1,128]{2,0,1:T(8,128)S(1)}, u32[]{:S(2)}, u32[]{:S(2)}) collective-permute-start(f32[256,1,128]{2,0,1:T(8,128)} %fusion.22), channel_id=1, source_target_pairs={{8,0},{16,8},{24,16},{32,24},{40,32},{48,40},{56,48},{64,56},{72,6... | collective-permute-start | bytes 393224 | tf_op jit(solution)/shard_map/ppermute | solution.py:12
  171.0 38.7 %collective-permute-start.18 = (f32[256,1,128]{2,0,1:T(8,128)}, f32[256,1,128]{2,0,1:T(8,128)S(1)}, u32[]{:S(2)}, u32[]{:S(2)}) collective-permute-start(f32[256,1,128]{2,0,1:T(8,128)} %convolution_bitcast_fusion.5), channel_id=1, source_target_pairs={{8,0},{16,8},{24,16},{32,24},{40,32},{48,40},{56,48},{64,56},{72,6... | collective-permute-start | bytes 393224 | tf_op jit(solution)/shard_map/ppermute | solution.py:12
  175.9 42.5 %collective-permute-start.13 = (f32[256,1,128]{2,0,1:T(8,128)}, f32[256,1,128]{2,0,1:T(8,128)}, u32[]{:S(2)}, u32[]{:S(2)}) collective-permute-start(f32[256,1,128]{2,0,1:T(8,128)} %fusion.20), channel_id=1, source_target_pairs={{16,0},{24,8},{32,16},{40,24},{48,32},{56,40},{64,48},{72,56},{80,... | collective-permute-start | bytes 393224 | tf_op jit(solution)/shard_map/ppermute | solution.py:12
  182.8 40.6 %collective-permute-start.14 = (f32[256,1,128]{2,0,1:T(8,128)}, f32[256,1,128]{2,0,1:T(8,128)}, u32[]{:S(2)}, u32[]{:S(2)}) collective-permute-start(f32[256,1,128]{2,0,1:T(8,128)} %fusion.18), channel_id=1, source_target_pairs={{24,0},{32,8},{40,16},{48,24},{56,32},{64,40},{72,48},{80,56},{88,... | collective-permute-start | bytes 393224 | tf_op jit(solution)/shard_map/ppermute | solution.py:12
  189.2 38.6 %collective-permute-start.15 = (f32[256,1,128]{2,0,1:T(8,128)}, f32[256,1,128]{2,0,1:T(8,128)}, u32[]{:S(2)}, u32[]{:S(2)}) collective-permute-start(f32[256,1,128]{2,0,1:T(8,128)} %fusion.16), channel_id=1, source_target_pairs={{32,0},{40,8},{48,16},{56,24},{64,32},{72,40},{80,48},{88,56},{96,... | collective-permute-start | bytes 393224 | tf_op jit(solution)/shard_map/ppermute | solution.py:12
  199.9 70.4 %all-to-all-start.6 = ((bf16[8,32,1024]{2,1,0:T(8,128)(2,1)}), bf16[8,32,1024]{2,1,0:T(8,128)(2,1)}, u32[]{:S(2)}, u32[]{:S(2)}) async-start(bf16[8,32,1024]{2,1,0:T(8,128)(2,1)} %all_to_all.104), calls=%async_computation.6 | async-start | bytes 1048576 | tf_op jit(solution)/shard_map/all_to_all | solution.py:77
  207.5 61.6 %copy-start.2 = (f32[256,8,256]{2,0,1:T(8,128)S(1)}, f32[256,8,256]{2,0,1:T(8,128)}, u32[]{:S(2)}) copy-start(f32[256,8,256]{2,0,1:T(8,128)} %copy-done.1) | copy-start | bytes 6291460
  207.6 24.6 %collective-permute-start.16 = (f32[256,1,128]{2,0,1:T(8,128)}, f32[256,1,128]{2,0,1:T(8,128)S(1)}, u32[]{:S(2)}, u32[]{:S(2)}) collective-permute-start(f32[256,1,128]{2,0,1:T(8,128)} %fusion.14), channel_id=1, source_target_pairs={{40,0},{48,8},{56,16},{64,24},{72,32},{80,40},{88,48},{96,56},{104... | collective-permute-start | bytes 393224 | tf_op jit(solution)/shard_map/ppermute | solution.py:12
  209.8 25.9 %collective-permute-start.17 = (f32[256,1,128]{2,0,1:T(8,128)S(1)}, f32[256,1,128]{2,0,1:T(8,128)S(1)}, u32[]{:S(2)}, u32[]{:S(2)}) collective-permute-start(f32[256,1,128]{2,0,1:T(8,128)S(1)} %fusion.12), channel_id=1, source_target_pairs={{48,0},{56,8},{64,16},{72,24},{80,32},{88,40},{96,48},{104,56},{11... | collective-permute-start | bytes 393224 | tf_op jit(solution)/shard_map/ppermute | solution.py:12
  218.5 21.3 %collective-permute-start.19 = (f32[256,1,128]{2,0,1:T(8,128)S(1)}, f32[256,1,128]{2,0,1:T(8,128)S(1)}, u32[]{:S(2)}, u32[]{:S(2)}) collective-permute-start(f32[256,1,128]{2,0,1:T(8,128)S(1)} %copy-done.6), channel_id=1, source_target_pairs={{16,0},{24,8},{32,16},{40,24},{48,32},{56,40},{64,48},{72,56},{80,... | collective-permute-start | bytes 393224 | tf_op jit(solution)/shard_map/ppermute | solution.py:12
  223.3 19.2 %collective-permute-start.20 = (f32[256,1,128]{2,0,1:T(8,128)S(1)}, f32[256,1,128]{2,0,1:T(8,128)S(1)}, u32[]{:S(2)}, u32[]{:S(2)}) collective-permute-start(f32[256,1,128]{2,0,1:T(8,128)S(1)} %copy-done.7), channel_id=1, source_target_pairs={{24,0},{32,8},{40,16},{48,24},{56,32},{64,40},{72,48},{80,56},{88,... | collective-permute-start | bytes 393224 | tf_op jit(solution)/shard_map/ppermute | solution.py:12
  227.9 18.6 %collective-permute-start.21 = (f32[256,1,128]{2,0,1:T(8,128)S(1)}, f32[256,1,128]{2,0,1:T(8,128)S(1)}, u32[]{:S(2)}, u32[]{:S(2)}) collective-permute-start(f32[256,1,128]{2,0,1:T(8,128)S(1)} %copy-done.8), channel_id=1, source_target_pairs={{32,0},{40,8},{48,16},{56,24},{64,32},{72,40},{80,48},{88,56},{96,... | collective-permute-start | bytes 393224 | tf_op jit(solution)/shard_map/ppermute | solution.py:12
  232.2 14.5 %collective-permute-start.22 = (f32[256,1,128]{2,0,1:T(8,128)S(1)}, f32[256,1,128]{2,0,1:T(8,128)S(1)}, u32[]{:S(2)}, u32[]{:S(2)}) collective-permute-start(f32[256,1,128]{2,0,1:T(8,128)S(1)} %copy-done.9), channel_id=1, source_target_pairs={{40,0},{48,8},{56,16},{64,24},{72,32},{80,40},{88,48},{96,56},{104... | collective-permute-start | bytes 393224 | tf_op jit(solution)/shard_map/ppermute | solution.py:12
  235.7 33.5 %collective-permute-start.23 = (f32[256,1,128]{2,0,1:T(8,128)S(1)}, f32[256,1,128]{2,0,1:T(8,128)S(1)}, u32[]{:S(2)}, u32[]{:S(2)}) collective-permute-start(f32[256,1,128]{2,0,1:T(8,128)S(1)} %convolution_bitcast_fusion), channel_id=1, source_target_pairs={{48,0},{56,8},{64,16},{72,24},{80,32},{88,40},{96,48},{104,56},{11... | collective-permute-start | bytes 393224 | tf_op jit(solution)/shard_map/ppermute | solution.py:12
  (13 other events, 245.3 us)
where the time goes:
time: 274 us; the launch traced here: 272 us
  starting transfers between devices  134 us (49%)
  waiting for transfers between devices  91.7 us (33%)
  matrix products  29.2 us (11%)
  local copies, waits for them, and re-layouts  12 us (4%)
  other arithmetic  3.44 us (1%)
    ppermute x24, starting transfers between devices, from_behind(): return lax.ppermute(array, axis, pairs)  103 us
    ppermute x24, waiting for transfers between devices, from_behind(): return lax.ppermute(array, axis, pairs)  47.6 us
    all_to_all x1, waiting for transfers between devices, per_device(): lax.all_to_all(queries, 'head', split_axis=1, concat_axis=0, tiled=True)  17.1 us
    dot_general x7, matrix products, pair_grads(): jnp.einsum('gthw,tghd->wgd', prob_half, dout, preferred_element_type=jnp....  8.84 us
    dot_general x7, matrix products, pair_grads(): jnp.einsum('gthw,tghd->wgd', score_half, query, preferred_element_type=jn...  8.52 us
    all_to_all x1, waiting for transfers between devices, per_device(): lax.all_to_all(keys, 'head', split_axis=1, concat_axis=0, tiled=True)  7.53 us
    all_to_all x1, waiting for transfers between devices, per_device(): lax.all_to_all(values, 'head', split_axis=1, concat_axis=0, tiled=True)  7.41 us
    all_to_all x1, starting transfers between devices, per_device(): lax.all_to_all(log_sum_exp, 'head', split_axis=1, concat_axis=0, tiled=True)  7.1 us
  transfers between devices with their start and end apart: 31, of which 15 were waited for; matrix products, arithmetic and copies ran while one was open for 14% of the time, Pallas kernels for 0%

commit v1 on v0

v1 whole, which is shorter than its diff:
```python
import functools
import math

import jax
import jax.numpy as jnp
from jax import lax
from jax.experimental import pallas as pl
from jax.experimental.pallas import tpu as pltpu
from jax.sharding import PartitionSpec as P

REACH = 6
HD = 128
AUX = 16
LOG2E = math.log2(math.e)
F32 = jnp.float32
BF16 = jnp.bfloat16
VMEM_LIMIT = 32 * 1024 * 1024
VMEM = pl.BlockSpec(memory_space=pltpu.VMEM)
LAST = (((1,), (1,)), ((), ()))
FIRST = (((0,), (0,)), ((), ()))


def call(kernel, outs, scratch=(), flops=0, moved=0):
    return pl.pallas_call(
        kernel,
        out_shape=outs,
        scratch_shapes=scratch,
        compiler_params=pltpu.CompilerParams(vmem_limit_bytes=VMEM_LIMIT),
        cost_estimate=pl.CostEstimate(flops=flops, bytes_accessed=moved, transcendentals=0),
    )


def pack_keys(groups, key_ref, value_ref, out_ref):
    rows = key_ref.shape[0]
    for g in range(groups):
        out_ref[g, :rows, :] = key_ref[:, g * HD : (g + 1) * HD]
        out_ref[g, rows:, :] = value_ref[:, g * HD : (g + 1) * HD]


def three_parts(x):
    first = x.astype(BF16)
    rest = x - first.astype(F32)
    second = rest.astype(BF16)
    third = (rest - second.astype(F32)).astype(BF16)
    return first, second, third


def lane_sums(x):
    ones = jnp.ones((8, HD), BF16)
    return sum(lax.dot_general(ones, part, LAST, preferred_element_type=F32) for part in three_parts(x))


def pack_queries(groups, per, query_ref, dout_ref, output_ref, lse_ref, out_ref):
    rows = query_ref.shape[0]
    span = per * rows
    lse = jnp.concatenate([lse_ref[...] * LOG2E, jnp.zeros((rows, HD - groups * per), F32)], axis=1)
    lane = lax.broadcasted_iota(jnp.int32, (rows, HD), 1)
    for g in range(groups):
        products, picked = [], []
        for h in range(per):
            cols = slice((g * per + h) * HD, (g * per + h + 1) * HD)
            dout = dout_ref[:, cols]
            out_ref[g, h * rows : (h + 1) * rows, :] = query_ref[:, cols]
            out_ref[g, span + h * rows : span + (h + 1) * rows, :] = dout
            products.append(dout.astype(F32) * output_ref[:, cols].astype(F32))
            picked.append(jnp.where(lane == g * per + h, lse, 0.0))
        pieces = []
        for sums in (lane_sums(jnp.concatenate(picked, 0)), lane_sums(jnp.concatenate(products, 0))):
            line = sums[:1]
            high = line.astype(BF16).astype(F32)
            for part in (high, line - high):
                pieces += [part[:, k * HD : (k + 1) * HD] for k in range(span // HD)]
        pieces.append(jnp.zeros((AUX - len(pieces), HD), F32))
        out_ref[g, 2 * span :, :] = jnp.concatenate(pieces, 0).astype(BF16)


def attention(scale, chunks, rows, per, low_ref, pos_ref, msg_ref, *refs):
    kv_refs = refs[: REACH + 1]
    dq_ref, own_ref, p1, p2, p3, p4, p5, p6, kv_all, part_all, prob_ref, ds_ref, dqt_ref = refs[REACH + 1 :]
    span = per * rows
    block = chunks * rows
    for s in range(REACH + 1):
        kv_all[s] = kv_refs[s][...]
    dqt_ref[...] = jnp.zeros_like(dqt_ref)
    kappa = lax.broadcasted_iota(jnp.int32, (block, span), 0)

    def one_block(s, diagonal):
        kv = kv_all[s].reshape(chunks, 2, rows, HD)
        key = kv[:, 0].reshape(block, HD)
        value = kv[:, 1].reshape(block, HD)
        key_t = key.T
        kpos = kappa - s * block
        for j in range(chunks):
            cols = slice(j * span, (j + 1) * span)
            query = msg_ref[j, :span, :]
            dout = msg_ref[j, span : 2 * span, :]
            aux = msg_ref[j, 2 * span :, :].astype(F32)
            half = span // HD

            def line(at):
                return jnp.concatenate([aux[at + k : at + k + 1] + aux[at + half + k : at + half + k + 1] for k in range(half)], 1)

            lse, delta = line(0), line(2 * half)
            score = lax.dot_general(key, query, LAST, preferred_element_type=F32)
            allowed = kpos >= low_ref[j : j + 1, :]
            if diagonal:
                allowed = allowed & (kpos <= pos_ref[j : j + 1, :])
            prob = jnp.where(allowed, jnp.exp2(score * (scale * LOG2E) - lse), 0.0)
            grad_prob = lax.dot_general(value, dout, LAST, preferred_element_type=F32)
            ds = (prob * (grad_prob - delta)).astype(BF16)
            prob_ref[:, cols] = prob.astype(BF16)
            ds_ref[:, cols] = ds
            dqt_ref[:, cols] += jnp.dot(key_t, ds, preferred_element_type=F32)
        queries = jnp.concatenate([msg_ref[j, :span, :] for j in range(chunks)], 0)
        douts = jnp.concatenate([msg_ref[j, span : 2 * span, :] for j in range(chunks)], 0)
        part_all[s, :block] = jnp.dot(ds_ref[...], queries, preferred_element_type=F32) * scale
        part_all[s, block:] = jnp.dot(prob_ref[...], douts, preferred_element_type=F32)

    one_block(0, True)

    def step(s, carry):
        one_block(s, False)
        return carry

    lax.fori_loop(1, REACH + 1, step, 0)
    own_ref[...] = part_all[0]
    for s, ref in enumerate((p1, p2, p3, p4, p5, p6), 1):
        ref[...] = part_all[s].astype(ref.dtype)
    for j in range(chunks):
        dq_ref[j] = (dqt_ref[:, j * span : (j + 1) * span] * scale).T.astype(BF16)


def unpack(groups, per, got_ref, out_ref):
    rows = out_ref.shape[0]
    for g in range(groups):
        for h in range(per):
            out_ref[:, (g * per + h) * HD : (g * per + h + 1) * HD] = got_ref[g, h * rows : (h + 1) * rows, :]


def shift(array, by):
    size = lax.axis_size("ctx")
    return lax.ppermute(array, "ctx", [(i, (i + by) % size) for i in range(size)])


def exchange(array):
    groups, rows, cols = array.shape
    flat = array.reshape(groups * rows, cols)
    return lax.all_to_all(flat, "head", split_axis=0, concat_axis=0, tiled=True).reshape(array.shape)


def per_device(queries, grad_out, outputs, keys, values, log_sum_exp, doc_start):
    rows, wide = queries.shape
    heads = log_sum_exp.shape[1]
    groups = keys.shape[1] // HD
    per = heads // groups
    span = per * rows
    block = doc_start.shape[0]
    chunks = block // rows
    scale = HD ** (-0.5)
    shape = jax.ShapeDtypeStruct

    kv_message = call(
        functools.partial(pack_keys, groups), shape((groups, 2 * rows, HD), BF16), moved=4 * rows * groups * HD * 2
    )(keys, values)
    kv_own = exchange(kv_message)
    message = call(
        functools.partial(pack_queries, groups, per),
        shape((groups, 2 * span + AUX, HD), BF16),
        moved=5 * rows * wide * 2,
    )(queries, grad_out, outputs, log_sum_exp)
    message, kv_own = lax.optimization_barrier((message, kv_own))
    kv = [kv_own.reshape(2 * block, HD)]
    got = exchange(message)

    kv1 = shift(kv[0], 1)
    kv6 = shift(kv[0], 6)
    kv2 = shift(kv1, 1)
    kv5 = shift(kv6, -1)
    kv3 = shift(kv2, 1)
    kv4 = shift(kv5, -1)

    first = lax.axis_index("ctx") * block
    low = jnp.tile((doc_start - first).reshape(chunks, 1, rows), (1, per, 1)).reshape(chunks, span)
    pos = jnp.tile(jnp.arange(block, dtype=jnp.int32).reshape(chunks, 1, rows), (1, per, 1)).reshape(chunks, span)

    part32, part16 = shape((2 * block, HD), F32), shape((2 * block, HD), BF16)
    dq, own, g1, g2, g3, g4, g5, g6 = call(
        functools.partial(attention, scale, chunks, rows, per),
        [shape((chunks, span, HD), BF16), part32, part32, part32, part16, part16, part32, part32],
        scratch=[
            pltpu.VMEM((REACH + 1, 2 * block, HD), BF16),
            pltpu.VMEM((REACH + 1, 2 * block, HD), F32),
            pltpu.VMEM((block, chunks * span), BF16),
            pltpu.VMEM((block, chunks * span), BF16),
            pltpu.VMEM((HD, chunks * span), F32),
        ],
        flops=10 * (REACH + 1) * block * chunks * span * HD,
        moved=6 * 1024 * 1024,
    )(low, pos, got, kv[0], kv1, kv2, kv3, kv4, kv5, kv6)

    back_q = exchange(dq)
    near = shift(g3, -1)
    far = shift(g4, 1)
    near = shift((g2 + near.astype(F32)).astype(BF16), -1)
    far = shift((g5 + far.astype(F32)).astype(BF16), 1)
    near = shift((g1 + near.astype(F32)).astype(BF16), -1)
    far = shift((g6 + far.astype(F32)).astype(BF16), -6)
    total = own + near.astype(F32) + far.astype(F32)

    grad_q = call(functools.partial(unpack, groups, per), shape((rows, wide), BF16), moved=4 * rows * wide)(back_q)
    return grad_q, total[:block], total[block:]


def solution(mesh):
    split = P(("ctx", "head"), None)
    return jax.shard_map(
        per_device,
        mesh=mesh,
        in_specs=(split, split, split, split, split, split, P("ctx")),
        out_specs=(split, P("ctx", "head"), P("ctx", "head")),
        check_vma=False,
    )
```

time: 274 us -> 153 us (0.56)
  the two profiles are of different devices: /device:TPU:132 before, /device:TPU:1 now
where the time goes in v1:
time: 153 us; the launch traced here: 150 us
  starting transfers between devices  76.7 us (50%)
  waiting for transfers between devices  43.5 us (28%)
  Pallas kernels  22.2 us (15%)
  local copies, waits for them, and re-layouts  6.47 us (4%)
    ppermute x12, starting transfers between devices, shift(): lax.ppermute(array, 'ctx', [(i, (i + by) % size) for i in range(size)])  52.1 us
    ppermute x12, waiting for transfers between devices, shift(): lax.ppermute(array, 'ctx', [(i, (i + by) % size) for i in range(size)])  40.9 us
    all_to_all x3, starting transfers between devices, exchange(): lax.all_to_all(flat, 'head', split_axis=0, concat_axis=0, tiled=True)  24.6 us
    pallas_call x1, Pallas kernels, per_device(): call(functools.partial(attention, scale, chunks, rows, per), [shape((chun...  18.7 us
    unnamed x14, local copies, waits for them, and re-layouts  5.52 us
  transfers between devices with their start and end apart: 15, of which 8 were waited for; matrix products, arithmetic and copies ran while one was open for 1% of the time, Pallas kernels for 1%

profile of v1, /device:TPU:1, one launch (start us, length us, event | category | flops | bytes accessed | tf_op | source)
XLA Modules:
  0.0 149.9 jit_solution(7196396697847218840)
XLA Ops:
  0.6 0.8 copy-done.3
  1.5 0.8 copy-done.4
  3.0 10.2 %all-to-all-start = ((bf16[8,64,128]{2,1,0:T(8,128)(2,1)}), bf16[8,64,128]{2,1,0:T(8,128)(2,1)S(1)}, u32[]{:S(2)}, u32[]{:S(2)}) async-start(bf16[8,64,128]{2,1,0:T(8,128)(2,1)} %shard_map.95), calls=%async_computation | async-start | bytes 262144 | tf_op jit(solution)/shard_map/all_to_all | solution.py:148
  13.1 1.0 copy-done
  14.2 1.0 copy-done.1
  15.2 1.0 copy-done.2
  17.0 2.0 %shard_map.94 = bf16[8,528,128]{2,1,0:T(8,128)(2,1)} custom-call(bf16[32,8192]{1,0:T(8,128)(2,1)S(1)} %copy-done, bf16[32,8192]{1,0:T(8,128)(2,1)S(1)} %copy-done.1, bf16[32,8192]{1,0:T(8,128)(2,1)S(1)} %copy-done.2, f32[32,64]{1,0:T(8,128)S(1)} %copy-done.5), custom_call_target="tpu_custom_call" | custom-call | bytes 2621440 | tf_op jit(solution)/shard_map/pallas_call | solution.py:166
  19.0 2.5 %all-to-all-done = bf16[8,64,128]{2,1,0:T(8,128)(2,1)S(1)} async-done(((bf16[8,64,128]{2,1,0:T(8,128)(2,1)}), bf16[8,64,128]{2,1,0:T(8,128)(2,1)S(1)}, u32[]{:S(2)}, u32[]{:S(2)}) %all-to-all-start) | async-done | bytes 131104 | tf_op jit(solution)/shard_map/all_to_all | solution.py:148
  21.5 4.8 %all-to-all-start.1 = ((bf16[8,528,128]{2,1,0:T(8,128)(2,1)}), bf16[8,528,128]{2,1,0:T(8,128)(2,1)S(1)}, u32[]{:S(2)}, u32[]{:S(2)}) async-start(bf16[8,528,128]{2,1,0:T(8,128)(2,1)} %shard_map.94), calls=%async_computation.1 | async-start | bytes 2162688 | tf_op jit(solution)/shard_map/all_to_all | solution.py:148
  26.3 9.1 %collective-permute-start.3 = (bf16[512,128]{1,0:T(8,128)(2,1)S(1)}, bf16[512,128]{1,0:T(8,128)(2,1)S(1)}, u32[]{:S(2)}, u32[]{:S(2)}) collective-permute-start(bf16[512,128]{1,0:T(8,128)(2,1)S(1)} %bitcast.9), channel_id=1, source_target_pairs={{0,48},{8,56},{16,64},{24,72},{32,80},{40,88},{48,96},{56,104},{64... | collective-permute-start | bytes 393224 | tf_op jit(solution)/shard_map/ppermute | solution.py:142
  35.4 3.1 %collective-permute-start = (bf16[512,128]{1,0:T(8,128)(2,1)S(1)}, bf16[512,128]{1,0:T(8,128)(2,1)S(1)}, u32[]{:S(2)}, u32[]{:S(2)}) collective-permute-start(bf16[512,128]{1,0:T(8,128)(2,1)S(1)} %bitcast.10), channel_id=1, source_target_pairs={{0,8},{8,16},{16,24},{24,32},{32,40},{40,48},{48,56},{56,64},{64,7... | collective-permute-start | bytes 393224 | tf_op jit(solution)/shard_map/ppermute | solution.py:142
  38.5 20.1 %collective-permute-done.3.refs_6_ = bf16[512,128]{1,0:T(8,128)(2,1)S(1)} collective-permute-done((bf16[512,128]{1,0:T(8,128)(2,1)S(1)}, bf16[512,128]{1,0:T(8,128)(2,1)S(1)}, u32[]{:S(2)}, u32[]{:S(2)}) %collective-permute-start.3) | collective-permute-done | bytes 131104 | tf_op jit(solution)/shard_map/ppermute | solution.py:142
  58.6 5.8 %collective-permute-start.4 = (bf16[512,128]{1,0:T(8,128)(2,1)S(1)}, bf16[512,128]{1,0:T(8,128)(2,1)S(1)}, u32[]{:S(2)}, u32[]{:S(2)}) collective-permute-start(bf16[512,128]{1,0:T(8,128)(2,1)S(1)} %collective-permute-done.3.refs_6_), channel_id=1, source_target_pairs={{0,504},{8,0},{16,8},{24,16},{32,24},{40,32},{48,40},{56,48},{64,5... | collective-permute-start | bytes 393224 | tf_op jit(solution)/shard_map/ppermute | solution.py:142
  64.4 1.6 %collective-permute-done.refs_1_ = bf16[512,128]{1,0:T(8,128)(2,1)S(1)} collective-permute-done((bf16[512,128]{1,0:T(8,128)(2,1)S(1)}, bf16[512,128]{1,0:T(8,128)(2,1)S(1)}, u32[]{:S(2)}, u32[]{:S(2)}) %collective-permute-start) | collective-permute-done | bytes 131104 | tf_op jit(solution)/shard_map/ppermute | solution.py:142
  66.0 1.9 %collective-permute-start.1 = (bf16[512,128]{1,0:T(8,128)(2,1)S(1)}, bf16[512,128]{1,0:T(8,128)(2,1)S(1)}, u32[]{:S(2)}, u32[]{:S(2)}) collective-permute-start(bf16[512,128]{1,0:T(8,128)(2,1)S(1)} %collective-permute-done.refs_1_), channel_id=1, source_target_pairs={{0,8},{8,16},{16,24},{24,32},{32,40},{40,48},{48,56},{56,64},{64,7... | collective-permute-start | bytes 393224 | tf_op jit(solution)/shard_map/ppermute | solution.py:142
  68.0 7.6 %collective-permute-start.5 = (bf16[512,128]{1,0:T(8,128)(2,1)S(1)}, bf16[512,128]{1,0:T(8,128)(2,1)S(1)}, u32[]{:S(2)}, u32[]{:S(2)}) collective-permute-start(bf16[512,128]{1,0:T(8,128)(2,1)S(1)} %collective-permute-done.4.refs_5_), channel_id=1, source_target_pairs={{0,504},{8,0},{16,8},{24,16},{32,24},{40,32},{48,40},{56,48},{64,5... | collective-permute-start | bytes 393224 | tf_op jit(solution)/shard_map/ppermute | solution.py:142
  75.5 1.0 collective-permute-done.1.refs_2_
  76.5 1.9 %collective-permute-start.2 = (bf16[512,128]{1,0:T(8,128)(2,1)S(1)}, bf16[512,128]{1,0:T(8,128)(2,1)S(1)}, u32[]{:S(2)}, u32[]{:S(2)}) collective-permute-start(bf16[512,128]{1,0:T(8,128)(2,1)S(1)} %collective-permute-done.1.refs_2_), channel_id=1, source_target_pairs={{0,8},{8,16},{16,24},{24,32},{32,40},{40,48},{48,56},{56,64},{64,7... | collective-permute-start | bytes 393224 | tf_op jit(solution)/shard_map/ppermute | solution.py:142
  78.7 7.7 %collective-permute-done.2.refs_3_ = bf16[512,128]{1,0:T(8,128)(2,1)S(1)} collective-permute-done((bf16[512,128]{1,0:T(8,128)(2,1)S(1)}, bf16[512,128]{1,0:T(8,128)(2,1)S(1)}, u32[]{:S(2)}, u32[]{:S(2)}) %collective-permute-start.2) | collective-permute-done | bytes 131104 | tf_op jit(solution)/shard_map/ppermute | solution.py:142
  86.5 18.7 %shard_map.96 = (bf16[8,256,128]{2,1,0:T(8,128)(2,1)}, f32[512,128]{1,0:T(8,128)S(1)}, f32[512,128]{1,0:T(8,128)S(1)}, f32[512,128]{1,0:T(8,128)S(1)}, bf16[512,...) custom-call(s32[8,256]{1,0:T(8,128)S(1)} %tile.18.low_ref, ...), custom_call_target="tpu_custom_call" | custom-call | flops 4697620480 | bytes 6291456 | tf_op jit(solution)/shard_map/pallas_call | solution.py:187
  105.1 1.9 %collective-permute-start.6 = (bf16[512,128]{1,0:T(8,128)(2,1)}, bf16[512,128]{1,0:T(8,128)(2,1)S(1)}, u32[]{:S(2)}, u32[]{:S(2)}) collective-permute-start(bf16[512,128]{1,0:T(8,128)(2,1)} %get-tuple-element.19), channel_id=1, source_target_pairs={{0,504},{8,0},{16,8},{24,16},{32,24},{40,32},{48,40},{56,48},{64,5... | collective-permute-start | bytes 393224 | tf_op jit(solution)/shard_map/ppermute | solution.py:142
  107.0 9.6 %all-to-all-start.2 = ((bf16[8,256,128]{2,1,0:T(8,128)(2,1)}), bf16[8,256,128]{2,1,0:T(8,128)(2,1)S(1)}, u32[]{:S(2)}, u32[]{:S(2)}) async-start(bf16[8,256,128]{2,1,0:T(8,128)(2,1)} %get-tuple-element.15), calls=%async_computation.2 | async-start | bytes 1048576 | tf_op jit(solution)/shard_map/all_to_all | solution.py:148
  116.6 3.6 %collective-permute-start.9 = (bf16[512,128]{1,0:T(8,128)(2,1)S(1)}, bf16[512,128]{1,0:T(8,128)(2,1)S(1)}, u32[]{:S(2)}, u32[]{:S(2)}) collective-permute-start(bf16[512,128]{1,0:T(8,128)(2,1)S(1)} %get-tuple-element.22), channel_id=1, source_target_pairs={{0,8},{8,16},{16,24},{24,32},{32,40},{40,48},{48,56},{56,64},{64,7... | collective-permute-start | bytes 393224 | tf_op jit(solution)/shard_map/ppermute | solution.py:142
  120.3 5.9 %collective-permute-start.7 = (bf16[512,128]{1,0:T(8,128)(2,1)S(1)}, bf16[512,128]{1,0:T(8,128)(2,1)S(1)}, u32[]{:S(2)}, u32[]{:S(2)}) collective-permute-start(bf16[512,128]{1,0:T(8,128)(2,1)S(1)} %add_convert_fusion.3), channel_id=1, source_target_pairs={{0,504},{8,0},{16,8},{24,16},{32,24},{40,32},{48,40},{56,48},{64,5... | collective-permute-start | bytes 393224 | tf_op jit(solution)/shard_map/ppermute | solution.py:142
  126.2 3.6 %collective-permute-done.9 = bf16[512,128]{1,0:T(8,128)(2,1)S(1)} collective-permute-done((bf16[512,128]{1,0:T(8,128)(2,1)S(1)}, bf16[512,128]{1,0:T(8,128)(2,1)S(1)}, u32[]{:S(2)}, u32[]{:S(2)}) %collective-permute-start.9) | collective-permute-done | bytes 131104 | tf_op jit(solution)/shard_map/ppermute | solution.py:142
  129.9 1.9 %collective-permute-start.10 = (bf16[512,128]{1,0:T(8,128)(2,1)S(1)}, bf16[512,128]{1,0:T(8,128)(2,1)S(1)}, u32[]{:S(2)}, u32[]{:S(2)}) collective-permute-start(bf16[512,128]{1,0:T(8,128)(2,1)S(1)} %add_convert_fusion.1), channel_id=1, source_target_pairs={{0,8},{8,16},{16,24},{24,32},{32,40},{40,48},{48,56},{56,64},{64,7... | collective-permute-start | bytes 393224 | tf_op jit(solution)/shard_map/ppermute | solution.py:142
  131.8 7.6 %collective-permute-start.8 = (bf16[512,128]{1,0:T(8,128)(2,1)S(1)}, bf16[512,128]{1,0:T(8,128)(2,1)S(1)}, u32[]{:S(2)}, u32[]{:S(2)}) collective-permute-start(bf16[512,128]{1,0:T(8,128)(2,1)S(1)} %add_convert_fusion.2), channel_id=1, source_target_pairs={{0,504},{8,0},{16,8},{24,16},{32,24},{40,32},{48,40},{56,48},{64,5... | collective-permute-start | bytes 393224 | tf_op jit(solution)/shard_map/ppermute | solution.py:142
  139.4 1.0 collective-permute-done.10
  140.4 1.9 %collective-permute-start.11 = (bf16[512,128]{1,0:T(8,128)(2,1)S(1)}, bf16[512,128]{1,0:T(8,128)(2,1)S(1)}, u32[]{:S(2)}, u32[]{:S(2)}) collective-permute-start(bf16[512,128]{1,0:T(8,128)(2,1)S(1)} %add_convert_fusion), channel_id=1, source_target_pairs={{0,464},{8,472},{16,480},{24,488},{32,496},{40,504},{48,0},{56,8},... | collective-permute-start | bytes 393224 | tf_op jit(solution)/shard_map/ppermute | solution.py:142
  142.4 5.9 %collective-permute-done.11 = bf16[512,128]{1,0:T(8,128)(2,1)S(1)} collective-permute-done((bf16[512,128]{1,0:T(8,128)(2,1)S(1)}, bf16[512,128]{1,0:T(8,128)(2,1)S(1)}, u32[]{:S(2)}, u32[]{:S(2)}) %collective-permute-start.11) | collective-permute-done | bytes 131104 | tf_op jit(solution)/shard_map/ppermute | solution.py:142
  148.3 0.7 fusion
  149.0 0.9 shard_map.97
  (29 shorter events, 1.8 us)
Async XLA Ops:
  0.6 0.8 copy-start.3
  1.5 0.8 copy-start.4
  3.0 18.5 %all-to-all-start = ((bf16[8,64,128]{2,1,0:T(8,128)(2,1)}), bf16[8,64,128]{2,1,0:T(8,128)(2,1)S(1)}, u32[]{:S(2)}, u32[]{:S(2)}) async-start(bf16[8,64,128]{2,1,0:T(8,128)(2,1)} %shard_map.95), calls=%async_computation | async-start | bytes 262144 | tf_op jit(solution)/shard_map/all_to_all | solution.py:148
  13.1 1.0 copy-start
  14.2 1.0 copy-start.1
  15.2 1.0 copy-start.2
  16.3 0.7 copy-start.5
  19.0 59.5 %copy-start.6 = (s32[256]{0:T(256)S(1)}, s32[256]{0:T(256)}, u32[]{:S(2)}) copy-start(s32[256]{0:T(256)} %param.13) | copy-start | bytes 3076
  21.5 65.0 %all-to-all-start.1 = ((bf16[8,528,128]{2,1,0:T(8,128)(2,1)}), bf16[8,528,128]{2,1,0:T(8,128)(2,1)S(1)}, u32[]{:S(2)}, u32[]{:S(2)}) async-start(bf16[8,528,128]{2,1,0:T(8,128)(2,1)} %shard_map.94), calls=%async_computation.1 | async-start | bytes 2162688 | tf_op jit(solution)/shard_map/all_to_all | solution.py:148
  26.3 32.3 %collective-permute-start.3 = (bf16[512,128]{1,0:T(8,128)(2,1)S(1)}, bf16[512,128]{1,0:T(8,128)(2,1)S(1)}, u32[]{:S(2)}, u32[]{:S(2)}) collective-permute-start(bf16[512,128]{1,0:T(8,128)(2,1)S(1)} %bitcast.9), channel_id=1, source_target_pairs={{0,48},{8,56},{16,64},{24,72},{32,80},{40,88},{48,96},{56,104},{64... | collective-permute-start | bytes 393224 | tf_op jit(solution)/shard_map/ppermute | solution.py:142
  35.4 30.6 %collective-permute-start = (bf16[512,128]{1,0:T(8,128)(2,1)S(1)}, bf16[512,128]{1,0:T(8,128)(2,1)S(1)}, u32[]{:S(2)}, u32[]{:S(2)}) collective-permute-start(bf16[512,128]{1,0:T(8,128)(2,1)S(1)} %bitcast.10), channel_id=1, source_target_pairs={{0,8},{8,16},{16,24},{24,32},{32,40},{40,48},{48,56},{56,64},{64,7... | collective-permute-start | bytes 393224 | tf_op jit(solution)/shard_map/ppermute | solution.py:142
  58.6 9.3 %collective-permute-start.4 = (bf16[512,128]{1,0:T(8,128)(2,1)S(1)}, bf16[512,128]{1,0:T(8,128)(2,1)S(1)}, u32[]{:S(2)}, u32[]{:S(2)}) collective-permute-start(bf16[512,128]{1,0:T(8,128)(2,1)S(1)} %collective-permute-done.3.refs_6_), channel_id=1, source_target_pairs={{0,504},{8,0},{16,8},{24,16},{32,24},{40,32},{48,40},{56,48},{64,5... | collective-permute-start | bytes 393224 | tf_op jit(solution)/shard_map/ppermute | solution.py:142
  66.0 10.5 %collective-permute-start.1 = (bf16[512,128]{1,0:T(8,128)(2,1)S(1)}, bf16[512,128]{1,0:T(8,128)(2,1)S(1)}, u32[]{:S(2)}, u32[]{:S(2)}) collective-permute-start(bf16[512,128]{1,0:T(8,128)(2,1)S(1)} %collective-permute-done.refs_1_), channel_id=1, source_target_pairs={{0,8},{8,16},{16,24},{24,32},{32,40},{40,48},{48,56},{56,64},{64,7... | collective-permute-start | bytes 393224 | tf_op jit(solution)/shard_map/ppermute | solution.py:142
  68.0 10.8 %collective-permute-start.5 = (bf16[512,128]{1,0:T(8,128)(2,1)S(1)}, bf16[512,128]{1,0:T(8,128)(2,1)S(1)}, u32[]{:S(2)}, u32[]{:S(2)}) collective-permute-start(bf16[512,128]{1,0:T(8,128)(2,1)S(1)} %collective-permute-done.4.refs_5_), channel_id=1, source_target_pairs={{0,504},{8,0},{16,8},{24,16},{32,24},{40,32},{48,40},{56,48},{64,5... | collective-permute-start | bytes 393224 | tf_op jit(solution)/shard_map/ppermute | solution.py:142
  76.5 9.9 %collective-permute-start.2 = (bf16[512,128]{1,0:T(8,128)(2,1)S(1)}, bf16[512,128]{1,0:T(8,128)(2,1)S(1)}, u32[]{:S(2)}, u32[]{:S(2)}) collective-permute-start(bf16[512,128]{1,0:T(8,128)(2,1)S(1)} %collective-permute-done.1.refs_2_), channel_id=1, source_target_pairs={{0,8},{8,16},{16,24},{24,32},{32,40},{40,48},{48,56},{56,64},{64,7... | collective-permute-start | bytes 393224 | tf_op jit(solution)/shard_map/ppermute | solution.py:142
  105.1 15.2 %collective-permute-start.6 = (bf16[512,128]{1,0:T(8,128)(2,1)}, bf16[512,128]{1,0:T(8,128)(2,1)S(1)}, u32[]{:S(2)}, u32[]{:S(2)}) collective-permute-start(bf16[512,128]{1,0:T(8,128)(2,1)} %get-tuple-element.19), channel_id=1, source_target_pairs={{0,504},{8,0},{16,8},{24,16},{32,24},{40,32},{48,40},{56,48},{64,5... | collective-permute-start | bytes 393224 | tf_op jit(solution)/shard_map/ppermute | solution.py:142
  107.0 42.0 %all-to-all-start.2 = ((bf16[8,256,128]{2,1,0:T(8,128)(2,1)}), bf16[8,256,128]{2,1,0:T(8,128)(2,1)S(1)}, u32[]{:S(2)}, u32[]{:S(2)}) async-start(bf16[8,256,128]{2,1,0:T(8,128)(2,1)} %get-tuple-element.15), calls=%async_computation.2 | async-start | bytes 1048576 | tf_op jit(solution)/shard_map/all_to_all | solution.py:148
  116.6 13.2 %collective-permute-start.9 = (bf16[512,128]{1,0:T(8,128)(2,1)S(1)}, bf16[512,128]{1,0:T(8,128)(2,1)S(1)}, u32[]{:S(2)}, u32[]{:S(2)}) collective-permute-start(bf16[512,128]{1,0:T(8,128)(2,1)S(1)} %get-tuple-element.22), channel_id=1, source_target_pairs={{0,8},{8,16},{16,24},{24,32},{32,40},{40,48},{48,56},{56,64},{64,7... | collective-permute-start | bytes 393224 | tf_op jit(solution)/shard_map/ppermute | solution.py:142
  120.3 11.5 %collective-permute-start.7 = (bf16[512,128]{1,0:T(8,128)(2,1)S(1)}, bf16[512,128]{1,0:T(8,128)(2,1)S(1)}, u32[]{:S(2)}, u32[]{:S(2)}) collective-permute-start(bf16[512,128]{1,0:T(8,128)(2,1)S(1)} %add_convert_fusion.3), channel_id=1, source_target_pairs={{0,504},{8,0},{16,8},{24,16},{32,24},{40,32},{48,40},{56,48},{64,5... | collective-permute-start | bytes 393224 | tf_op jit(solution)/shard_map/ppermute | solution.py:142
  129.9 10.5 %collective-permute-start.10 = (bf16[512,128]{1,0:T(8,128)(2,1)S(1)}, bf16[512,128]{1,0:T(8,128)(2,1)S(1)}, u32[]{:S(2)}, u32[]{:S(2)}) collective-permute-start(bf16[512,128]{1,0:T(8,128)(2,1)S(1)} %add_convert_fusion.1), channel_id=1, source_target_pairs={{0,8},{8,16},{16,24},{24,32},{32,40},{40,48},{48,56},{56,64},{64,7... | collective-permute-start | bytes 393224 | tf_op jit(solution)/shard_map/ppermute | solution.py:142
  131.8 10.5 %collective-permute-start.8 = (bf16[512,128]{1,0:T(8,128)(2,1)S(1)}, bf16[512,128]{1,0:T(8,128)(2,1)S(1)}, u32[]{:S(2)}, u32[]{:S(2)}) collective-permute-start(bf16[512,128]{1,0:T(8,128)(2,1)S(1)} %add_convert_fusion.2), channel_id=1, source_target_pairs={{0,504},{8,0},{16,8},{24,16},{32,24},{40,32},{48,40},{56,48},{64,5... | collective-permute-start | bytes 393224 | tf_op jit(solution)/shard_map/ppermute | solution.py:142
  140.4 7.8 %collective-permute-start.11 = (bf16[512,128]{1,0:T(8,128)(2,1)S(1)}, bf16[512,128]{1,0:T(8,128)(2,1)S(1)}, u32[]{:S(2)}, u32[]{:S(2)}) collective-permute-start(bf16[512,128]{1,0:T(8,128)(2,1)S(1)} %add_convert_fusion), channel_id=1, source_target_pairs={{0,464},{8,472},{16,480},{24,488},{32,496},{40,504},{48,0},{56,8},... | collective-permute-start | bytes 393224 | tf_op jit(solution)/shard_map/ppermute | solution.py:142

commit v2 on v1

v2 whole, which is shorter than its diff:
```python
import functools
import math

import jax
import jax.numpy as jnp
from jax import lax
from jax.experimental import pallas as pl
from jax.experimental.pallas import tpu as pltpu
from jax.sharding import Mesh
from jax.sharding import PartitionSpec as P

REACH = 6
HD = 128
RING = 8
AUX = 16
LOG2E = math.log2(math.e)
F32 = jnp.float32
BF16 = jnp.bfloat16
VMEM_LIMIT = 32 * 1024 * 1024
PACK_LIMIT = 60 * 1024 * 1024
LAST = (((1,), (1,)), ((), ()))


def call(kernel, outs, scratch=(), flops=0, moved=0, limit=VMEM_LIMIT, **specs):
    return pl.pallas_call(
        kernel,
        out_shape=outs,
        scratch_shapes=scratch,
        compiler_params=pltpu.CompilerParams(vmem_limit_bytes=limit),
        cost_estimate=pl.CostEstimate(flops=flops, bytes_accessed=moved, transcendentals=0),
        **specs,
    )


def pack_keys(groups, key_ref, value_ref, out_ref, sems):
    rows = key_ref.shape[0]
    copies = []
    for g in range(groups):
        for k, ref in enumerate((key_ref, value_ref)):
            copy = pltpu.make_async_copy(
                ref.at[:, g * HD : (g + 1) * HD], out_ref.at[g, k * rows : (k + 1) * rows, :], sems.at[g, k]
            )
            copy.start()
            copies.append(copy)
    for copy in copies:
        copy.wait()


def three_parts(x):
    first = x.astype(BF16)
    rest = x - first.astype(F32)
    second = rest.astype(BF16)
    third = (rest - second.astype(F32)).astype(BF16)
    return first, second, third


def lane_sums(x):
    ones = jnp.ones((8, HD), BF16)
    return sum(lax.dot_general(ones, part, LAST, preferred_element_type=F32) for part in three_parts(x))


def fetch(pairs, sems):
    copies = []
    for n, (source, target) in enumerate(pairs):
        half = source.shape[0] // 2
        for k in range(2):
            rows = slice(k * half, (k + 1) * half)
            copies.append(pltpu.make_async_copy(source.at[rows], target.at[rows], sems.at[n, k]))
    for copy in copies:
        copy.start()
    for copy in copies:
        copy.wait()


def pack_queries(groups, per, query_hbm, dout_hbm, output_hbm, lse_hbm, out_ref, q_ref, d_ref, o_ref, l_ref, sems):
    rows = q_ref.shape[0]
    span = per * rows
    fetch(((query_hbm, q_ref), (dout_hbm, d_ref), (output_hbm, o_ref), (lse_hbm, l_ref)), sems)
    lse = jnp.concatenate([l_ref[...] * LOG2E, jnp.zeros((rows, HD - groups * per), F32)], axis=1)
    lane = lax.broadcasted_iota(jnp.int32, (rows, HD), 1)
    for g in range(groups):
        products, picked = [], []
        for h in range(per):
            cols = slice((g * per + h) * HD, (g * per + h + 1) * HD)
            dout = d_ref[:, cols]
            out_ref[g, h * rows : (h + 1) * rows, :] = q_ref[:, cols]
            out_ref[g, span + h * rows : span + (h + 1) * rows, :] = dout
            products.append(dout.astype(F32) * o_ref[:, cols].astype(F32))
            picked.append(jnp.where(lane == g * per + h, lse, 0.0))
        pieces = []
        for sums in (lane_sums(jnp.concatenate(picked, 0)), lane_sums(jnp.concatenate(products, 0))):
            line = sums[:1]
            high = line.astype(BF16).astype(F32)
            for part in (high, line - high):
                pieces += [part[:, k * HD : (k + 1) * HD] for k in range(span // HD)]
        pieces.append(jnp.zeros((AUX - len(pieces), HD), F32))
        out_ref[g, 2 * span :, :] = jnp.concatenate(pieces, 0).astype(BF16)


def attention(scale, chunks, rows, per, blocks, sources, sinks, first, last, low_ref, pos_ref, msg_ref, *refs):
    count = len(blocks)
    operands = 1 + max(n for n, _ in sources)
    kv_refs, refs = refs[:operands], refs[operands:]
    if not first:
        before_ref, refs = refs[0], refs[1:]
    dq_ref, part_refs, refs = refs[0], refs[1 : len(sinks) + 1], refs[len(sinks) + 1 :]
    k_all, v_all, kt_all, dk_ref, dv_ref = refs[:5]
    bufs = (refs[5:9], refs[9:13])
    span = per * rows
    block = chunks * rows
    half = span // HD
    total = count * block
    for n, (operand, slot) in enumerate(sources):
        at = slice(n * block, (n + 1) * block)
        kv = kv_refs[operand][slot * 2 * block : (slot + 1) * 2 * block].reshape(chunks, 2, rows, HD)
        key = kv[:, 0].reshape(block, HD)
        k_all[at] = key
        v_all[at] = kv[:, 1].reshape(block, HD)
        kt_all[:, at] = key.T
    dk_ref[...] = jnp.zeros_like(dk_ref)
    dv_ref[...] = jnp.zeros_like(dv_ref)

    def window_of(j):
        begin = j * rows if blocks[0] == REACH else 0
        end = total - block + (j + 1) * rows if blocks[-1] == 0 else total
        return begin, end

    def scores(j, sc, gp):
        begin, end = window_of(j)
        sc[: end - begin] = lax.dot_general(k_all[begin:end], msg_ref[j, :span, :], LAST, preferred_element_type=F32)
        gp[: end - begin] = lax.dot_general(
            v_all[begin:end], msg_ref[j, span : 2 * span, :], LAST, preferred_element_type=F32
        )

    def middle(j, sc, gp, pb, ds):
        aux = msg_ref[j, 2 * span :, :].astype(F32)

        def line(at):
            return jnp.concatenate([aux[at + k : at + k + 1] + aux[at + half + k : at + half + k + 1] for k in range(half)], 1)

        lse, delta = line(0), line(2 * half)
        low, pos = low_ref[j : j + 1, :], pos_ref[j : j + 1, :]
        begin, end = window_of(j)
        old_begin, old_end = window_of(j - 2) if j >= 2 else (0, total)
        for a, b in ((old_begin, begin), (end, old_end)):
            if a < b:
                ds[a:b] = jnp.zeros((b - a, span), BF16)
        for n in range(count):
            start, stop = max(begin, n * block), min(end, (n + 1) * block)
            if start >= stop:
                continue
            size = stop - start
            at = slice(start - begin, stop - begin)
            kpos = lax.broadcasted_iota(jnp.int32, (size, span), 0) + (start - n * block - blocks[n] * block)
            allowed = kpos >= low
            if blocks[n] == 0:
                allowed = allowed & (kpos <= pos)
            prob = jnp.where(allowed, jnp.exp2(sc[at] * (scale * LOG2E) - lse), 0.0)
            pb[at] = prob.astype(BF16)
            ds[start:stop] = (prob * (gp[at] - delta)).astype(BF16)

    def sums(j, pb, ds):
        begin, end = window_of(j)
        dv_ref[begin:end] += jnp.dot(pb[: end - begin], msg_ref[j, span : 2 * span, :], preferred_element_type=F32)
        dk_ref[begin:end] += jnp.dot(ds[begin:end], msg_ref[j, :span, :], preferred_element_type=F32)
        dqt = jnp.dot(kt_all[...], ds[...], preferred_element_type=F32)
        cols = slice(j * span, (j + 1) * span)
        if not first:
            dqt = dqt + before_ref[:, cols]
        if last:
            dq_ref[j] = (dqt * scale).T.astype(BF16)
        else:
            dq_ref[:, cols] = dqt

    scores(0, *bufs[0][:2])
    for j in range(chunks):
        sc, gp, pb, ds = bufs[j % 2]
        if j + 1 < chunks:
            scores(j + 1, *bufs[(j + 1) % 2][:2])
        middle(j, sc, gp, pb, ds)
        sums(j, pb, ds)
    for ref, held in zip(part_refs, sinks):
        for slot, s in enumerate(held):
            n = blocks.index(s)
            at = slice(n * block, (n + 1) * block)
            row = slot * 2 * block
            ref[row : row + block] = (dk_ref[at] * scale).astype(ref.dtype)
            ref[row + block : row + 2 * block] = dv_ref[at].astype(ref.dtype)


def attend(scale, chunks, rows, per, low, pos, got, blocks, kv, sources, sinks, before=None, last=False):
    shape = jax.ShapeDtypeStruct
    vmem = pl.BlockSpec(memory_space=pltpu.VMEM)
    span, block = per * rows, chunks * rows
    total = len(blocks) * block
    buffers = [
        pltpu.VMEM((total, span), F32),
        pltpu.VMEM((total, span), F32),
        pltpu.VMEM((total, span), BF16),
        pltpu.VMEM((total, span), BF16),
    ]
    dq = shape((chunks, span, HD), BF16) if last else shape((HD, chunks * span), F32)
    operands = [low, pos, got, *kv] + ([] if before is None else [before])
    return call(
        functools.partial(
            attention, scale, chunks, rows, per, blocks, sources, [held for _, held in sinks], before is None, last
        ),
        [dq] + [shape((len(held) * 2 * block, HD), kind) for kind, held in sinks],
        scratch=[
            pltpu.VMEM((total, HD), BF16),
            pltpu.VMEM((total, HD), BF16),
            pltpu.VMEM((HD, total), BF16),
            pltpu.VMEM((total, HD), F32),
            pltpu.VMEM((total, HD), F32),
            *buffers,
            *buffers,
        ],
        flops=10 * total * chunks * span * HD,
        moved=4 * 1024 * 1024,
        in_specs=[vmem] * len(operands),
        out_specs=[vmem] * (1 + len(sinks)),
    )(*operands)


def unpack(groups, per, got_ref, out_ref):
    rows = out_ref.shape[0]
    for g in range(groups):
        for h in range(per):
            out_ref[:, (g * per + h) * HD : (g * per + h + 1) * HD] = got_ref[g, h * rows : (h + 1) * rows, :]


def turn(array, axis, by):
    size = lax.axis_size(axis)
    return lax.ppermute(array, axis, [(i, (i + by) % size) for i in range(size)])


def hop(array, by):
    axes = ("ring", "z")
    size = lax.axis_size(axes)
    return lax.ppermute(array, axes, [(i, (i + by) % size) for i in range(size)])


def exchange(array):
    groups, rows, cols = array.shape
    flat = array.reshape(groups * rows, cols)
    return lax.all_to_all(flat, "head", split_axis=0, concat_axis=0, tiled=True).reshape(array.shape)


def per_device(queries, grad_out, outputs, keys, values, log_sum_exp, doc_start):
    rows, wide = queries.shape
    heads = log_sum_exp.shape[1]
    groups = keys.shape[1] // HD
    per = heads // groups
    span = per * rows
    block = doc_start.shape[0]
    chunks = block // rows
    scale = HD ** (-0.5)
    shape = jax.ShapeDtypeStruct
    hbm = pl.BlockSpec(memory_space=pltpu.HBM)
    vmem = pl.BlockSpec(memory_space=pltpu.VMEM)

    kv_own = call(
        functools.partial(pack_keys, groups),
        shape((groups, 2 * rows, HD), BF16),
        scratch=[pltpu.SemaphoreType.DMA((groups, 2))],
        moved=4 * rows * groups * HD * 2,
        in_specs=[hbm] * 2,
        out_specs=vmem,
        limit=PACK_LIMIT,
    )(keys, values)
    kv_own = exchange(kv_own)
    message = call(
        functools.partial(pack_queries, groups, per),
        shape((groups, 2 * span + AUX, HD), BF16),
        scratch=[pltpu.VMEM((rows, wide), BF16)] * 3
        + [pltpu.VMEM((rows, heads), F32), pltpu.SemaphoreType.DMA((4, 2))],
        moved=5 * rows * wide * 2,
        in_specs=[hbm] * 4,
        out_specs=vmem,
        limit=PACK_LIMIT,
    )(queries, grad_out, outputs, log_sum_exp)
    message, kv_own = lax.optimization_barrier((message, kv_own))
    kv_own = kv_own.reshape(2 * block, HD)
    kv_older = turn(kv_own, "ring", 1)
    message, kv_older = lax.optimization_barrier((message, kv_older))
    got = exchange(message)
    z = lax.axis_index("z")

    def behind(s):
        return turn(jnp.where(z + s < RING, kv_own, kv_older), "z", s)

    kv = {0: kv_own}
    for s in (3, 4, 5, 2, 6, 1):
        kv[s] = behind(s)

    first = (lax.axis_index("ring") * RING + z) * block
    low = jnp.tile((doc_start - first).reshape(chunks, 1, rows), (1, per, 1)).reshape(chunks, span)
    pos = jnp.tile(jnp.arange(block, dtype=jnp.int32).reshape(chunks, 1, rows), (1, per, 1)).reshape(chunks, span)

    run = functools.partial(attend, scale, chunks, rows, per, low, pos, got)

    dq, g14, g25 = run(
        (5, 4, 2, 1), [kv[s] for s in (5, 4, 2, 1)], [(n, 0) for n in range(4)], [(BF16, (1, 4)), (BF16, (2, 5))]
    )
    from_next = hop(g14, -1).astype(F32)
    from_last = hop(g25, 1).astype(F32)
    dq, g6, g3, g0 = run(
        (6, 3, 0),
        [kv[s] for s in (6, 3, 0)],
        [(n, 0) for n in range(3)],
        [(F32, (6,)), (F32, (3,)), (F32, (0,))],
        before=dq,
        last=True,
    )
    back_q = exchange(dq)
    size = 2 * block
    g3 = hop((g3 + from_next[size:] + from_last[:size]).astype(BF16), -3)
    g6 = hop((g6 + from_last[size:]).astype(BF16), -6)
    total = g0 + from_next[:size] + g3.astype(F32) + g6.astype(F32)

    grad_q = call(functools.partial(unpack, groups, per), shape((rows, wide), BF16), moved=4 * rows * wide)(back_q)
    return grad_q, total[:block], total[block:]


def solution(mesh):
    ctx, head = mesh.devices.shape
    fine = Mesh(mesh.devices.reshape(ctx // RING, RING, head), ("ring", "z", "head"))
    split = P(("ring", "z", "head"), None)
    return jax.shard_map(
        per_device,
        mesh=fine,
        in_specs=(split, split, split, split, split, split, P(("ring", "z"))),
        out_specs=(split, P(("ring", "z"), "head"), P(("ring", "z"), "head")),
        check_vma=False,
    )
```

time: 153 us -> 113 us (0.74)
  the two profiles are of different devices: /device:TPU:1 before, /device:TPU:113 now
where the time goes in v2:
time: 113 us; the launch traced here: 112 us
  starting transfers between devices  70 us (62%)
  waiting for transfers between devices  24.2 us (21%)
  Pallas kernels  15.1 us (13%)
  other arithmetic  1.21 us (1%)
    ppermute x7, starting transfers between devices, turn(): lax.ppermute(array, axis, [(i, (i + by) % size) for i in range(size)])  30.4 us
    all_to_all x3, starting transfers between devices, exchange(): lax.all_to_all(flat, 'head', split_axis=0, concat_axis=0, tiled=True)  27.7 us
    ppermute x4, waiting for transfers between devices, hop(): lax.ppermute(array, axes, [(i, (i + by) % size) for i in range(size)])  13.3 us
    ppermute x4, starting transfers between devices, hop(): lax.ppermute(array, axes, [(i, (i + by) % size) for i in range(size)])  11.9 us
    pallas_call x2, Pallas kernels, attend(): call(functools.partial(attention, scale, chunks, rows, per, blocks, sourc...  9.22 us
    ppermute x7, waiting for transfers between devices, turn(): lax.ppermute(array, axis, [(i, (i + by) % size) for i in range(size)])  9.01 us
    pallas_call x1, Pallas kernels, per_device(): call(functools.partial(pack_queries, groups, per), shape((groups, 2 * spa...  3.38 us
  transfers between devices with their start and end apart: 14, of which 5 were waited for; matrix products, arithmetic and copies ran while one was open for 2% of the time, Pallas kernels for 11%

profile of v2, /device:TPU:113, one launch (start us, length us, event | category | flops | bytes accessed | tf_op | source)
XLA Modules:
  0.0 112.3 jit_solution(16318698819848495361)
XLA Ops:
  0.6 1.7 %shard_map.95 = bf16[8,64,128]{2,1,0:T(8,128)(2,1)} custom-call(bf16[32,1024]{1,0:T(8,128)(2,1)} %key_ref.1, bf16[32,1024]{1,0:T(8,128)(2,1)} %value_ref.1), custom_call_target="tpu_custom_call" | custom-call | bytes 262144 | tf_op jit(solution)/shard_map/pallas_call | solution.py:262
  2.3 7.3 %all-to-all-start = ((bf16[8,64,128]{2,1,0:T(8,128)(2,1)}), bf16[8,64,128]{2,1,0:T(8,128)(2,1)S(1)}, u32[]{:S(2)}, u32[]{:S(2)}) async-start(bf16[8,64,128]{2,1,0:T(8,128)(2,1)} %shard_map.95), calls=%async_computation | async-start | bytes 262144 | tf_op jit(solution)/shard_map/all_to_all | solution.py:246
  9.6 3.4 %shard_map.94 = bf16[8,528,128]{2,1,0:T(8,128)(2,1)} custom-call(bf16[32,8192]{1,0:T(8,128)(2,1)} %query_hbm.1, bf16[32,8192]{1,0:T(8,128)(2,1)} %dout_hbm.1, bf16[32,8192]{1,0:T(8,128)(2,1)} %output_hbm.1, f32[32,64]{1,0:T(8,128)} %lse_hbm.1), custom_call_target="tpu_custom_call" | custom-call | bytes 2621440 | tf_op jit(solution)/shard_map/pallas_call | solution.py:272
  13.0 1.9 %all-to-all-done = bf16[8,64,128]{2,1,0:T(8,128)(2,1)S(1)} async-done(((bf16[8,64,128]{2,1,0:T(8,128)(2,1)}), bf16[8,64,128]{2,1,0:T(8,128)(2,1)S(1)}, u32[]{:S(2)}, u32[]{:S(2)}) %all-to-all-start) | async-done | bytes 131104 | tf_op jit(solution)/shard_map/all_to_all | solution.py:246
  14.9 1.9 %collective-permute-start = (bf16[512,128]{1,0:T(8,128)(2,1)S(1)}, bf16[512,128]{1,0:T(8,128)(2,1)S(1)}, u32[]{:S(2)}, u32[]{:S(2)}) collective-permute-start(bf16[512,128]{1,0:T(8,128)(2,1)S(1)} %bitcast.15), channel_id=1, source_target_pairs={{0,64},{64,128},{128,192},{192,256},{256,320},{320,384},{384,448},... | collective-permute-start | bytes 393224 | tf_op jit(solution)/shard_map/ppermute | solution.py:234
  16.8 6.2 %collective-permute-done = bf16[512,128]{1,0:T(8,128)(2,1)S(1)} collective-permute-done((bf16[512,128]{1,0:T(8,128)(2,1)S(1)}, bf16[512,128]{1,0:T(8,128)(2,1)S(1)}, u32[]{:S(2)}, u32[]{:S(2)}) %collective-permute-start) | collective-permute-done | bytes 131104 | tf_op jit(solution)/shard_map/ppermute | solution.py:234
  23.0 8.1 %all-to-all-start.1 = ((bf16[8,528,128]{2,1,0:T(8,128)(2,1)}), bf16[8,528,128]{2,1,0:T(8,128)(2,1)S(1)}, u32[]{:S(2)}, u32[]{:S(2)}) async-start(bf16[8,528,128]{2,1,0:T(8,128)(2,1)} %shard_map.94), calls=%async_computation.1 | async-start | bytes 2162688 | tf_op jit(solution)/shard_map/all_to_all | solution.py:246
  31.1 0.1 broadcast_select_fusion
  31.2 4.0 %collective-permute-start.6 = (bf16[512,128]{1,0:T(8,128)(2,1)S(1)}, bf16[512,128]{1,0:T(8,128)(2,1)S(1)}, u32[]{:S(2)}, u32[]{:S(2)}) collective-permute-start(bf16[512,128]{1,0:T(8,128)(2,1)S(1)} %get-tuple-element.29), channel_id=1, source_target_pairs={{0,8},{8,16},{16,24},{24,32},{32,40},{40,48},{48,56},{56,0},{1,9},... | collective-permute-start | bytes 393224 | tf_op jit(solution)/shard_map/ppermute | solution.py:234
  35.2 7.0 %collective-permute-start.5 = (bf16[512,128]{1,0:T(8,128)(2,1)S(1)}, bf16[512,128]{1,0:T(8,128)(2,1)S(1)}, u32[]{:S(2)}, u32[]{:S(2)}) collective-permute-start(bf16[512,128]{1,0:T(8,128)(2,1)S(1)} %get-tuple-element.30), channel_id=1, source_target_pairs={{0,16},{8,24},{16,32},{24,40},{32,48},{40,56},{48,0},{56,8},{1,17}... | collective-permute-start | bytes 393224 | tf_op jit(solution)/shard_map/ppermute | solution.py:234
  42.2 4.6 %collective-permute-start.4 = (bf16[512,128]{1,0:T(8,128)(2,1)S(1)}, bf16[512,128]{1,0:T(8,128)(2,1)S(1)}, u32[]{:S(2)}, u32[]{:S(2)}) collective-permute-start(bf16[512,128]{1,0:T(8,128)(2,1)S(1)} %get-tuple-element.31), channel_id=1, source_target_pairs={{0,32},{8,40},{16,48},{24,56},{32,0},{40,8},{48,16},{56,24},{1,33}... | collective-permute-start | bytes 393224 | tf_op jit(solution)/shard_map/ppermute | solution.py:234
  46.9 4.6 %collective-permute-start.3 = (bf16[512,128]{1,0:T(8,128)(2,1)S(1)}, bf16[512,128]{1,0:T(8,128)(2,1)S(1)}, u32[]{:S(2)}, u32[]{:S(2)}) collective-permute-start(bf16[512,128]{1,0:T(8,128)(2,1)S(1)} %get-tuple-element.32), channel_id=1, source_target_pairs={{0,40},{8,48},{16,56},{24,0},{32,8},{40,16},{48,24},{56,32},{1,41}... | collective-permute-start | bytes 393224 | tf_op jit(solution)/shard_map/ppermute | solution.py:234
  51.5 0.1 tile.20
  51.6 0.1 tile.24.pos_ref
  51.6 0.1 tile.22.low_ref
  51.7 3.7 %collective-permute-start.2 = (bf16[512,128]{1,0:T(8,128)(2,1)S(1)}, bf16[512,128]{1,0:T(8,128)(2,1)S(1)}, u32[]{:S(2)}, u32[]{:S(2)}) collective-permute-start(bf16[512,128]{1,0:T(8,128)(2,1)S(1)} %get-tuple-element.33), channel_id=1, source_target_pairs={{0,24},{8,32},{16,40},{24,48},{32,56},{40,0},{48,8},{56,16},{1,25}... | collective-permute-start | bytes 393224 | tf_op jit(solution)/shard_map/ppermute | solution.py:234
  55.5 4.6 %collective-permute-start.1 = (bf16[512,128]{1,0:T(8,128)(2,1)S(1)}, bf16[512,128]{1,0:T(8,128)(2,1)S(1)}, u32[]{:S(2)}, u32[]{:S(2)}) collective-permute-start(bf16[512,128]{1,0:T(8,128)(2,1)S(1)} %get-tuple-element.34), channel_id=1, source_target_pairs={{0,48},{8,56},{16,0},{24,8},{32,16},{40,24},{48,32},{56,40},{1,49}... | collective-permute-start | bytes 393224 | tf_op jit(solution)/shard_map/ppermute | solution.py:234
  60.1 0.0 collective-permute-done.4.refs_1_
  60.1 2.8 %collective-permute-done.3.refs_0_ = bf16[512,128]{1,0:T(8,128)(2,1)S(1)} collective-permute-done((bf16[512,128]{1,0:T(8,128)(2,1)S(1)}, bf16[512,128]{1,0:T(8,128)(2,1)S(1)}, u32[]{:S(2)}, u32[]{:S(2)}) %collective-permute-start.3) | collective-permute-done | bytes 131104 | tf_op jit(solution)/shard_map/ppermute | solution.py:234
  62.8 5.2 %shard_map.96 = (f32[128,2048]{1,0:T(8,128)S(1)}, bf16[1024,128]{1,0:T(8,128)(2,1)S(1)}, bf16[1024,128]{1,0:T(8,128)(2,1)S(1)}) custom-call(s32[8,256]{1,0:T(8,128)S(1)} %tile.22.low_ref, s32[8,256]{1,0:T(8,128)S(1)} %tile.24.pos_ref, bf16[8,528,128]{2,1,0:T(8,128)(2,1)S(1)} %all-to-all-done.1.msg_ref, bf16[512,128]{1,0:T(8,128)(2,1)S(1)} %collective-permute-done.3.refs_0_, ...), custom_call_target="tpu_custom_call" | custom-call | flops 2684354560 | bytes 4194304 | tf_op jit(solution)/shard_map/pallas_call | solution.py:204
  68.1 1.9 %collective-permute-start.7 = (bf16[1024,128]{1,0:T(8,128)(2,1)S(1)}, bf16[1024,128]{1,0:T(8,128)(2,1)}, u32[]{:S(2)}, u32[]{:S(2)}) collective-permute-start(bf16[1024,128]{1,0:T(8,128)(2,1)S(1)} %get-tuple-element.21), channel_id=1, source_target_pairs={{0,504},{8,0},{16,8},{24,16},{32,24},{40,32},{48,40},{56,48},{64,5... | collective-permute-start | bytes 786440 | tf_op jit(solution)/shard_map/ppermute | solution.py:240
  70.0 3.4 %collective-permute-start.8 = (bf16[1024,128]{1,0:T(8,128)(2,1)S(1)}, bf16[1024,128]{1,0:T(8,128)(2,1)S(1)}, u32[]{:S(2)}, u32[]{:S(2)}) collective-permute-start(bf16[1024,128]{1,0:T(8,128)(2,1)S(1)} %get-tuple-element.23), channel_id=1, source_target_pairs={{0,8},{8,16},{16,24},{24,32},{32,40},{40,48},{48,56},{56,64},{64,7... | collective-permute-start | bytes 786440 | tf_op jit(solution)/shard_map/ppermute | solution.py:240
  73.4 4.0 %shard_map.97 = (bf16[8,256,128]{2,1,0:T(8,128)(2,1)}, f32[512,128]{1,0:T(8,128)S(1)}, f32[512,128]{1,0:T(8,128)S(1)}, f32[512,128]{1,0:T(8,128)S(1)}) custom-call(s32[8,256]{1,0:T(8,128)S(1)} %tile.22.low_ref, s32[8,256]{1,0:T(8,128)S(1)} %tile.24.pos_ref, bf16[8,528,128]{2,1,0:T(8,128)(2,1)S(1)} %all-to-all-done.1.msg_ref, ...), custom_call_target="tpu_custom_call" | custom-call | flops 2013265920 | bytes 4194304 | tf_op jit(solution)/shard_map/pallas_call | solution.py:204
  77.4 12.3 %all-to-all-start.2 = ((bf16[8,256,128]{2,1,0:T(8,128)(2,1)}), bf16[8,256,128]{2,1,0:T(8,128)(2,1)S(1)}, u32[]{:S(2)}, u32[]{:S(2)}) async-start(bf16[8,256,128]{2,1,0:T(8,128)(2,1)} %get-tuple-element.19), calls=%async_computation.2 | async-start | bytes 1048576 | tf_op jit(solution)/shard_map/all_to_all | solution.py:246
  89.7 1.0 convert_element_type.18
  90.7 0.1 fusion.1
  90.8 2.2 %collective-permute-start.9 = (bf16[512,128]{1,0:T(8,128)(2,1)S(1)}, bf16[512,128]{1,0:T(8,128)(2,1)S(1)}, u32[]{:S(2)}, u32[]{:S(2)}) collective-permute-start(bf16[512,128]{1,0:T(8,128)(2,1)S(1)} %get-tuple-element.25), channel_id=1, source_target_pairs={{0,488},{8,496},{16,504},{24,0},{32,8},{40,16},{48,24},{56,32},{64... | collective-permute-start | bytes 393224 | tf_op jit(solution)/shard_map/ppermute | solution.py:240
  93.0 4.4 %collective-permute-start.10 = (bf16[512,128]{1,0:T(8,128)(2,1)S(1)}, bf16[512,128]{1,0:T(8,128)(2,1)S(1)}, u32[]{:S(2)}, u32[]{:S(2)}) collective-permute-start(bf16[512,128]{1,0:T(8,128)(2,1)S(1)} %get-tuple-element.26), channel_id=1, source_target_pairs={{0,464},{8,472},{16,480},{24,488},{32,496},{40,504},{48,0},{56,8},... | collective-permute-start | bytes 393224 | tf_op jit(solution)/shard_map/ppermute | solution.py:240
  97.4 10.4 %collective-permute-done.9 = bf16[512,128]{1,0:T(8,128)(2,1)S(1)} collective-permute-done((bf16[512,128]{1,0:T(8,128)(2,1)S(1)}, bf16[512,128]{1,0:T(8,128)(2,1)S(1)}, u32[]{:S(2)}, u32[]{:S(2)}) %collective-permute-start.9) | collective-permute-done | bytes 131104 | tf_op jit(solution)/shard_map/ppermute | solution.py:240
  107.8 2.9 %collective-permute-done.10 = bf16[512,128]{1,0:T(8,128)(2,1)S(1)} collective-permute-done((bf16[512,128]{1,0:T(8,128)(2,1)S(1)}, bf16[512,128]{1,0:T(8,128)(2,1)S(1)}, u32[]{:S(2)}, u32[]{:S(2)}) %collective-permute-start.10) | collective-permute-done | bytes 131104 | tf_op jit(solution)/shard_map/ppermute | solution.py:240
  110.7 0.7 fusion.4
  111.5 0.9 shard_map.98
  (16 shorter events, 0.1 us)
Async XLA Ops:
  2.3 12.6 %all-to-all-start = ((bf16[8,64,128]{2,1,0:T(8,128)(2,1)}), bf16[8,64,128]{2,1,0:T(8,128)(2,1)S(1)}, u32[]{:S(2)}, u32[]{:S(2)}) async-start(bf16[8,64,128]{2,1,0:T(8,128)(2,1)} %shard_map.95), calls=%async_computation | async-start | bytes 262144 | tf_op jit(solution)/shard_map/all_to_all | solution.py:246
  14.9 8.1 %collective-permute-start = (bf16[512,128]{1,0:T(8,128)(2,1)S(1)}, bf16[512,128]{1,0:T(8,128)(2,1)S(1)}, u32[]{:S(2)}, u32[]{:S(2)}) collective-permute-start(bf16[512,128]{1,0:T(8,128)(2,1)S(1)} %bitcast.15), channel_id=1, source_target_pairs={{0,64},{64,128},{128,192},{192,256},{256,320},{320,384},{384,448},... | collective-permute-start | bytes 393224 | tf_op jit(solution)/shard_map/ppermute | solution.py:234
  23.0 39.8 %all-to-all-start.1 = ((bf16[8,528,128]{2,1,0:T(8,128)(2,1)}), bf16[8,528,128]{2,1,0:T(8,128)(2,1)S(1)}, u32[]{:S(2)}, u32[]{:S(2)}) async-start(bf16[8,528,128]{2,1,0:T(8,128)(2,1)} %shard_map.94), calls=%async_computation.1 | async-start | bytes 2162688 | tf_op jit(solution)/shard_map/all_to_all | solution.py:246
  31.1 20.3 %copy-start = (s32[256]{0:T(256)S(1)}, s32[256]{0:T(256)}, u32[]{:S(2)}) copy-start(s32[256]{0:T(256)} %param.13) | copy-start | bytes 3076
  31.2 24.3 %collective-permute-start.6 = (bf16[512,128]{1,0:T(8,128)(2,1)S(1)}, bf16[512,128]{1,0:T(8,128)(2,1)S(1)}, u32[]{:S(2)}, u32[]{:S(2)}) collective-permute-start(bf16[512,128]{1,0:T(8,128)(2,1)S(1)} %get-tuple-element.29), channel_id=1, source_target_pairs={{0,8},{8,16},{16,24},{24,32},{32,40},{40,48},{48,56},{56,0},{1,9},... | collective-permute-start | bytes 393224 | tf_op jit(solution)/shard_map/ppermute | solution.py:234
  35.2 24.8 %collective-permute-start.5 = (bf16[512,128]{1,0:T(8,128)(2,1)S(1)}, bf16[512,128]{1,0:T(8,128)(2,1)S(1)}, u32[]{:S(2)}, u32[]{:S(2)}) collective-permute-start(bf16[512,128]{1,0:T(8,128)(2,1)S(1)} %get-tuple-element.30), channel_id=1, source_target_pairs={{0,16},{8,24},{16,32},{24,40},{32,48},{40,56},{48,0},{56,8},{1,17}... | collective-permute-start | bytes 393224 | tf_op jit(solution)/shard_map/ppermute | solution.py:234
  42.2 17.8 %collective-permute-start.4 = (bf16[512,128]{1,0:T(8,128)(2,1)S(1)}, bf16[512,128]{1,0:T(8,128)(2,1)S(1)}, u32[]{:S(2)}, u32[]{:S(2)}) collective-permute-start(bf16[512,128]{1,0:T(8,128)(2,1)S(1)} %get-tuple-element.31), channel_id=1, source_target_pairs={{0,32},{8,40},{16,48},{24,56},{32,0},{40,8},{48,16},{56,24},{1,33}... | collective-permute-start | bytes 393224 | tf_op jit(solution)/shard_map/ppermute | solution.py:234
  46.9 15.9 %collective-permute-start.3 = (bf16[512,128]{1,0:T(8,128)(2,1)S(1)}, bf16[512,128]{1,0:T(8,128)(2,1)S(1)}, u32[]{:S(2)}, u32[]{:S(2)}) collective-permute-start(bf16[512,128]{1,0:T(8,128)(2,1)S(1)} %get-tuple-element.32), channel_id=1, source_target_pairs={{0,40},{8,48},{16,56},{24,0},{32,8},{40,16},{48,24},{56,32},{1,41}... | collective-permute-start | bytes 393224 | tf_op jit(solution)/shard_map/ppermute | solution.py:234
  51.7 21.6 %collective-permute-start.2 = (bf16[512,128]{1,0:T(8,128)(2,1)S(1)}, bf16[512,128]{1,0:T(8,128)(2,1)S(1)}, u32[]{:S(2)}, u32[]{:S(2)}) collective-permute-start(bf16[512,128]{1,0:T(8,128)(2,1)S(1)} %get-tuple-element.33), channel_id=1, source_target_pairs={{0,24},{8,32},{16,40},{24,48},{32,56},{40,0},{48,8},{56,16},{1,25}... | collective-permute-start | bytes 393224 | tf_op jit(solution)/shard_map/ppermute | solution.py:234
  55.5 17.9 %collective-permute-start.1 = (bf16[512,128]{1,0:T(8,128)(2,1)S(1)}, bf16[512,128]{1,0:T(8,128)(2,1)S(1)}, u32[]{:S(2)}, u32[]{:S(2)}) collective-permute-start(bf16[512,128]{1,0:T(8,128)(2,1)S(1)} %get-tuple-element.34), channel_id=1, source_target_pairs={{0,48},{8,56},{16,0},{24,8},{32,16},{40,24},{48,32},{56,40},{1,49}... | collective-permute-start | bytes 393224 | tf_op jit(solution)/shard_map/ppermute | solution.py:234
  68.1 21.6 %collective-permute-start.7 = (bf16[1024,128]{1,0:T(8,128)(2,1)S(1)}, bf16[1024,128]{1,0:T(8,128)(2,1)}, u32[]{:S(2)}, u32[]{:S(2)}) collective-permute-start(bf16[1024,128]{1,0:T(8,128)(2,1)S(1)} %get-tuple-element.21), channel_id=1, source_target_pairs={{0,504},{8,0},{16,8},{24,16},{32,24},{40,32},{48,40},{56,48},{64,5... | collective-permute-start | bytes 786440 | tf_op jit(solution)/shard_map/ppermute | solution.py:240
  70.0 20.7 %collective-permute-start.8 = (bf16[1024,128]{1,0:T(8,128)(2,1)S(1)}, bf16[1024,128]{1,0:T(8,128)(2,1)S(1)}, u32[]{:S(2)}, u32[]{:S(2)}) collective-permute-start(bf16[1024,128]{1,0:T(8,128)(2,1)S(1)} %get-tuple-element.23), channel_id=1, source_target_pairs={{0,8},{8,16},{16,24},{24,32},{32,40},{40,48},{48,56},{56,64},{64,7... | collective-permute-start | bytes 786440 | tf_op jit(solution)/shard_map/ppermute | solution.py:240
  77.4 34.1 %all-to-all-start.2 = ((bf16[8,256,128]{2,1,0:T(8,128)(2,1)}), bf16[8,256,128]{2,1,0:T(8,128)(2,1)S(1)}, u32[]{:S(2)}, u32[]{:S(2)}) async-start(bf16[8,256,128]{2,1,0:T(8,128)(2,1)} %get-tuple-element.19), calls=%async_computation.2 | async-start | bytes 1048576 | tf_op jit(solution)/shard_map/all_to_all | solution.py:246
  90.8 17.0 %collective-permute-start.9 = (bf16[512,128]{1,0:T(8,128)(2,1)S(1)}, bf16[512,128]{1,0:T(8,128)(2,1)S(1)}, u32[]{:S(2)}, u32[]{:S(2)}) collective-permute-start(bf16[512,128]{1,0:T(8,128)(2,1)S(1)} %get-tuple-element.25), channel_id=1, source_target_pairs={{0,488},{8,496},{16,504},{24,0},{32,8},{40,16},{48,24},{56,32},{64... | collective-permute-start | bytes 393224 | tf_op jit(solution)/shard_map/ppermute | solution.py:240
  93.0 17.7 %collective-permute-start.10 = (bf16[512,128]{1,0:T(8,128)(2,1)S(1)}, bf16[512,128]{1,0:T(8,128)(2,1)S(1)}, u32[]{:S(2)}, u32[]{:S(2)}) collective-permute-start(bf16[512,128]{1,0:T(8,128)(2,1)S(1)} %get-tuple-element.26), channel_id=1, source_target_pairs={{0,464},{8,472},{16,480},{24,488},{32,496},{40,504},{48,0},{56,8},... | collective-permute-start | bytes 393224 | tf_op jit(solution)/shard_map/ppermute | solution.py:240

commit v3 on v2

--- a/solution.py
+++ b/solution.py
@@ -13,10 +13,11 @@
 HD = 128
 RING = 8
 AUX = 16
+CHOOSE_FLOPS = 70_000_000_000
 LOG2E = math.log2(math.e)
 F32 = jnp.float32
 BF16 = jnp.bfloat16
-VMEM_LIMIT = 32 * 1024 * 1024
+VMEM_LIMIT = 16 * 1024 * 1024
 PACK_LIMIT = 60 * 1024 * 1024
 LAST = (((1,), (1,)), ((), ()))
 
@@ -32,18 +33,13 @@
     )
 
 
-def pack_keys(groups, key_ref, value_ref, out_ref, sems):
-    rows = key_ref.shape[0]
-    copies = []
+def pack_keys(groups, key_hbm, value_hbm, out_ref, k_ref, v_ref, sems):
+    rows = k_ref.shape[0]
+    fetch(((key_hbm, k_ref), (value_hbm, v_ref)), sems)
     for g in range(groups):
-        for k, ref in enumerate((key_ref, value_ref)):
-            copy = pltpu.make_async_copy(
-                ref.at[:, g * HD : (g + 1) * HD], out_ref.at[g, k * rows : (k + 1) * rows, :], sems.at[g, k]
-            )
-            copy.start()
-            copies.append(copy)
-    for copy in copies:
-        copy.wait()
+        cols = slice(g * HD, (g + 1) * HD)
+        out_ref[g, :rows, :] = k_ref[:, cols]
+        out_ref[g, rows:, :] = v_ref[:, cols]
 
 
 def three_parts(x):
@@ -222,11 +218,35 @@
     )(*operands)
 
 
-def unpack(groups, per, got_ref, out_ref):
-    rows = out_ref.shape[0]
+def choose(reach, z_ref, own_ref, older_ref, *out_refs):
+    for s, ref in zip(reach, out_refs):
+        ref[...] = jnp.where(z_ref[0] + s < RING, own_ref[...], older_ref[...])
+
+
+def join(last_ref, next_ref, five_ref, two_ref, five_out, two_out):
+    size = five_ref.shape[0]
+    for ref, out, part in ((five_ref, five_out, slice(size, 2 * size)), (two_ref, two_out, slice(0, size))):
+        out[...] = (ref[...] + last_ref[part].astype(F32) + next_ref[part].astype(F32)).astype(BF16)
+
+
+def finish(groups, per, got_ref, own_ref, near_ref, far_ref, q_out, k_out, v_out, q_ref, k_ref, v_ref, sems):
+    rows, block = q_ref.shape[0], k_ref.shape[0]
+    copies = []
+    for n, (ref, out, at) in enumerate(((k_ref, k_out, 0), (v_ref, v_out, block))):
+        part = slice(at, at + block)
+        ref[...] = own_ref[part] + near_ref[part].astype(F32) + far_ref[part].astype(F32)
+        copies.append(pltpu.make_async_copy(ref, out, sems.at[n]))
+        copies[-1].start()
     for g in range(groups):
         for h in range(per):
-            out_ref[:, (g * per + h) * HD : (g * per + h + 1) * HD] = got_ref[g, h * rows : (h + 1) * rows, :]
+            q_ref[:, (g * per + h) * HD : (g * per + h + 1) * HD] = got_ref[g, h * rows : (h + 1) * rows, :]
+    half = rows // 2
+    for n in range(2):
+        part = slice(n * half, (n + 1) * half)
+        copies.append(pltpu.make_async_copy(q_ref.at[part], q_out.at[part], sems.at[2 + n]))
+        copies[-1].start()
+    for copy in copies:
+        copy.wait()
 
 
 def turn(array, axis, by):
@@ -262,7 +282,7 @@
     kv_own = call(
         functools.partial(pack_keys, groups),
         shape((groups, 2 * rows, HD), BF16),
-        scratch=[pltpu.SemaphoreType.DMA((groups, 2))],
+        scratch=[pltpu.VMEM((rows, groups * HD), BF16)] * 2 + [pltpu.SemaphoreType.DMA((2, 2))],
         moved=4 * rows * groups * HD * 2,
         in_specs=[hbm] * 2,
         out_specs=vmem,
@@ -282,16 +302,20 @@
     message, kv_own = lax.optimization_barrier((message, kv_own))
     kv_own = kv_own.reshape(2 * block, HD)
     kv_older = turn(kv_own, "ring", 1)
-    message, kv_older = lax.optimization_barrier((message, kv_older))
+    kv = {}
     got = exchange(message)
     z = lax.axis_index("z")
 
-    def behind(s):
-        return turn(jnp.where(z + s < RING, kv_own, kv_older), "z", s)
-
-    kv = {0: kv_own}
-    for s in (3, 4, 5, 2, 6, 1):
-        kv[s] = behind(s)
+    reach = (6, 4, 3, 1, 5, 2)
+    sent = call(
+        functools.partial(choose, reach),
+        [shape((2 * block, HD), BF16)] * REACH,
+        flops=CHOOSE_FLOPS,
+        in_specs=[pl.BlockSpec(memory_space=pltpu.SMEM), vmem, vmem],
+        out_specs=[vmem] * REACH,
+    )(z.reshape(1), kv_own, kv_older)
+    kv = {s: turn(array, "z", s) for s, array in zip(reach, sent)}
+    kv[0] = kv_own
 
     first = (lax.axis_index("ring") * RING + z) * block
     low = jnp.tile((doc_start - first).reshape(chunks, 1, rows), (1, per, 1)).reshape(chunks, span)
@@ -299,27 +323,39 @@
 
     run = functools.partial(attend, scale, chunks, rows, per, low, pos, got)
 
-    dq, g14, g25 = run(
-        (5, 4, 2, 1), [kv[s] for s in (5, 4, 2, 1)], [(n, 0) for n in range(4)], [(BF16, (1, 4)), (BF16, (2, 5))]
+    dq, g14, g36 = run(
+        (6, 4, 3, 1), [kv[s] for s in (6, 4, 3, 1)], [(n, 0) for n in range(4)], [(BF16, (1, 4)), (BF16, (3, 6))]
     )
-    from_next = hop(g14, -1).astype(F32)
-    from_last = hop(g25, 1).astype(F32)
-    dq, g6, g3, g0 = run(
-        (6, 3, 0),
-        [kv[s] for s in (6, 3, 0)],
+    from_last, from_next = hop(g14, 1), hop(g36, -1)
+    dq, g5, g2, g0 = run(
+        (5, 2, 0),
+        [kv[s] for s in (5, 2, 0)],
         [(n, 0) for n in range(3)],
-        [(F32, (6,)), (F32, (3,)), (F32, (0,))],
+        [(F32, (5,)), (F32, (2,)), (F32, (0,))],
         before=dq,
         last=True,
     )
     back_q = exchange(dq)
     size = 2 * block
-    g3 = hop((g3 + from_next[size:] + from_last[:size]).astype(BF16), -3)
-    g6 = hop((g6 + from_last[size:]).astype(BF16), -6)
-    total = g0 + from_next[:size] + g3.astype(F32) + g6.astype(F32)
-
-    grad_q = call(functools.partial(unpack, groups, per), shape((rows, wide), BF16), moved=4 * rows * wide)(back_q)
-    return grad_q, total[:block], total[block:]
+    g5, g2 = call(
+        join, [shape((size, HD), BF16)] * 2, flops=CHOOSE_FLOPS, in_specs=[vmem] * 4, out_specs=[vmem] * 2
+    )(from_last, from_next, g5, g2)
+    g5, g2 = hop(g5, -5), hop(g2, -2)
+
+    grad_q, grad_k, grad_v = call(
+        functools.partial(finish, groups, per),
+        [shape((rows, wide), BF16), shape((block, HD), F32), shape((block, HD), F32)],
+        scratch=[
+            pltpu.VMEM((rows, wide), BF16),
+            pltpu.VMEM((block, HD), F32),
+            pltpu.VMEM((block, HD), F32),
+            pltpu.SemaphoreType.DMA((4,)),
+        ],
+        moved=4 * rows * wide,
+        in_specs=[vmem] * 4,
+        out_specs=[hbm] * 3,
+    )(back_q, g0, g2, g5)
+    return grad_q, grad_k, grad_v
 
 
 def solution(mesh):

time: 113 us -> 109 us (0.965)
  the two profiles are of different devices: /device:TPU:113 before, /device:TPU:1 now
where the time goes in v3:
time: 109 us; the launch traced here: 108 us
  starting transfers between devices  65.1 us (60%)
  waiting for transfers between devices  26.4 us (24%)
  Pallas kernels  15.3 us (14%)
    ppermute x7, starting transfers between devices, turn(): lax.ppermute(array, axis, [(i, (i + by) % size) for i in range(size)])  28.3 us
    all_to_all x3, starting transfers between devices, exchange(): lax.all_to_all(flat, 'head', split_axis=0, concat_axis=0, tiled=True)  23.5 us
    ppermute x4, waiting for transfers between devices, hop(): lax.ppermute(array, axes, [(i, (i + by) % size) for i in range(size)])  13.6 us
    ppermute x4, starting transfers between devices, hop(): lax.ppermute(array, axes, [(i, (i + by) % size) for i in range(size)])  13.3 us
    pallas_call x2, Pallas kernels, attend(): call(functools.partial(attention, scale, chunks, rows, per, blocks, sourc...  9.22 us
    ppermute x7, waiting for transfers between devices, turn(): lax.ppermute(array, axis, [(i, (i + by) % size) for i in range(size)])  7.91 us
    all_to_all x3, waiting for transfers between devices, exchange(): lax.all_to_all(flat, 'head', split_axis=0, concat_axis=0, tiled=True)  4.97 us
    pallas_call x1, Pallas kernels, per_device(): call(functools.partial(pack_queries, groups, per), shape((groups, 2 * spa...  3.38 us
  transfers between devices with their start and end apart: 14, of which 6 were waited for; matrix products, arithmetic and copies ran while one was open for 0% of the time, Pallas kernels for 12%

profile of v3, /device:TPU:1, one launch (start us, length us, event | category | flops | bytes accessed | tf_op | source)
XLA Modules:
  0.0 108.0 jit_solution(3943557874234728558)
XLA Ops:
  0.6 1.5 %shard_map.95 = bf16[8,64,128]{2,1,0:T(8,128)(2,1)} custom-call(bf16[32,1024]{1,0:T(8,128)(2,1)} %key_hbm.1, bf16[32,1024]{1,0:T(8,128)(2,1)} %value_hbm.1), custom_call_target="tpu_custom_call" | custom-call | bytes 262144 | tf_op jit(solution)/shard_map/pallas_call | solution.py:282
  2.2 10.2 %all-to-all-start = ((bf16[8,64,128]{2,1,0:T(8,128)(2,1)}), bf16[8,64,128]{2,1,0:T(8,128)(2,1)S(1)}, u32[]{:S(2)}, u32[]{:S(2)}) async-start(bf16[8,64,128]{2,1,0:T(8,128)(2,1)} %shard_map.95), calls=%async_computation | async-start | bytes 262144 | tf_op jit(solution)/shard_map/all_to_all | solution.py:266
  12.3 3.4 %shard_map.94 = bf16[8,528,128]{2,1,0:T(8,128)(2,1)} custom-call(bf16[32,8192]{1,0:T(8,128)(2,1)} %query_hbm.1, bf16[32,8192]{1,0:T(8,128)(2,1)} %dout_hbm.1, bf16[32,8192]{1,0:T(8,128)(2,1)} %output_hbm.1, f32[32,64]{1,0:T(8,128)} %lse_hbm.1), custom_call_target="tpu_custom_call" | custom-call | bytes 2621440 | tf_op jit(solution)/shard_map/pallas_call | solution.py:292
  15.7 5.0 %all-to-all-done = bf16[8,64,128]{2,1,0:T(8,128)(2,1)S(1)} async-done(((bf16[8,64,128]{2,1,0:T(8,128)(2,1)}), bf16[8,64,128]{2,1,0:T(8,128)(2,1)S(1)}, u32[]{:S(2)}, u32[]{:S(2)}) %all-to-all-start) | async-done | bytes 131104 | tf_op jit(solution)/shard_map/all_to_all | solution.py:266
  20.7 1.9 %collective-permute-start = (bf16[512,128]{1,0:T(8,128)(2,1)S(1)}, bf16[512,128]{1,0:T(8,128)(2,1)S(1)}, u32[]{:S(2)}, u32[]{:S(2)}) collective-permute-start(bf16[512,128]{1,0:T(8,128)(2,1)S(1)} %bitcast.10), channel_id=1, source_target_pairs={{0,64},{64,128},{128,192},{192,256},{256,320},{320,384},{384,448},... | collective-permute-start | bytes 393224 | tf_op jit(solution)/shard_map/ppermute | solution.py:254
  22.6 4.4 %all-to-all-start.1 = ((bf16[8,528,128]{2,1,0:T(8,128)(2,1)}), bf16[8,528,128]{2,1,0:T(8,128)(2,1)S(1)}, u32[]{:S(2)}, u32[]{:S(2)}) async-start(bf16[8,528,128]{2,1,0:T(8,128)(2,1)} %shard_map.94), calls=%async_computation.1 | async-start | bytes 2162688 | tf_op jit(solution)/shard_map/all_to_all | solution.py:266
  27.0 1.5 %collective-permute-done.older_ref = bf16[512,128]{1,0:T(8,128)(2,1)S(1)} collective-permute-done((bf16[512,128]{1,0:T(8,128)(2,1)S(1)}, bf16[512,128]{1,0:T(8,128)(2,1)S(1)}, u32[]{:S(2)}, u32[]{:S(2)}) %collective-permute-start) | collective-permute-done | bytes 131104 | tf_op jit(solution)/shard_map/ppermute | solution.py:254
  28.5 0.2 shard_map.96
  28.7 8.9 %collective-permute-start.3 = (bf16[512,128]{1,0:T(8,128)(2,1)S(1)}, bf16[512,128]{1,0:T(8,128)(2,1)S(1)}, u32[]{:S(2)}, u32[]{:S(2)}) collective-permute-start(bf16[512,128]{1,0:T(8,128)(2,1)S(1)} %get-tuple-element.24), channel_id=1, source_target_pairs={{0,48},{8,56},{16,0},{24,8},{32,16},{40,24},{48,32},{56,40},{1,49}... | collective-permute-start | bytes 393224 | tf_op jit(solution)/shard_map/ppermute | solution.py:254
  37.6 1.9 %collective-permute-start.4 = (bf16[512,128]{1,0:T(8,128)(2,1)S(1)}, bf16[512,128]{1,0:T(8,128)(2,1)S(1)}, u32[]{:S(2)}, u32[]{:S(2)}) collective-permute-start(bf16[512,128]{1,0:T(8,128)(2,1)S(1)} %get-tuple-element.25), channel_id=1, source_target_pairs={{0,32},{8,40},{16,48},{24,56},{32,0},{40,8},{48,16},{56,24},{1,33}... | collective-permute-start | bytes 393224 | tf_op jit(solution)/shard_map/ppermute | solution.py:254
  39.5 5.1 %collective-permute-start.5 = (bf16[512,128]{1,0:T(8,128)(2,1)S(1)}, bf16[512,128]{1,0:T(8,128)(2,1)S(1)}, u32[]{:S(2)}, u32[]{:S(2)}) collective-permute-start(bf16[512,128]{1,0:T(8,128)(2,1)S(1)} %get-tuple-element.26), channel_id=1, source_target_pairs={{0,24},{8,32},{16,40},{24,48},{32,56},{40,0},{48,8},{56,16},{1,25}... | collective-permute-start | bytes 393224 | tf_op jit(solution)/shard_map/ppermute | solution.py:254
  44.7 4.3 %collective-permute-start.6 = (bf16[512,128]{1,0:T(8,128)(2,1)S(1)}, bf16[512,128]{1,0:T(8,128)(2,1)S(1)}, u32[]{:S(2)}, u32[]{:S(2)}) collective-permute-start(bf16[512,128]{1,0:T(8,128)(2,1)S(1)} %get-tuple-element.27), channel_id=1, source_target_pairs={{0,8},{8,16},{16,24},{24,32},{32,40},{40,48},{48,56},{56,0},{1,9},... | collective-permute-start | bytes 393224 | tf_op jit(solution)/shard_map/ppermute | solution.py:254
  49.0 0.1 tile.20
  49.1 0.1 tile.24.pos_ref
  49.2 0.1 tile.22.low_ref
  49.3 1.9 %collective-permute-start.1 = (bf16[512,128]{1,0:T(8,128)(2,1)S(1)}, bf16[512,128]{1,0:T(8,128)(2,1)S(1)}, u32[]{:S(2)}, u32[]{:S(2)}) collective-permute-start(bf16[512,128]{1,0:T(8,128)(2,1)S(1)} %get-tuple-element.22), channel_id=1, source_target_pairs={{0,40},{8,48},{16,56},{24,0},{32,8},{40,16},{48,24},{56,32},{1,41}... | collective-permute-start | bytes 393224 | tf_op jit(solution)/shard_map/ppermute | solution.py:254
  51.2 4.2 %collective-permute-start.2 = (bf16[512,128]{1,0:T(8,128)(2,1)S(1)}, bf16[512,128]{1,0:T(8,128)(2,1)S(1)}, u32[]{:S(2)}, u32[]{:S(2)}) collective-permute-start(bf16[512,128]{1,0:T(8,128)(2,1)S(1)} %get-tuple-element.23), channel_id=1, source_target_pairs={{0,16},{8,24},{16,32},{24,40},{32,48},{40,56},{48,0},{56,8},{1,17}... | collective-permute-start | bytes 393224 | tf_op jit(solution)/shard_map/ppermute | solution.py:254
  55.4 2.9 %collective-permute-done.5.refs_2_ = bf16[512,128]{1,0:T(8,128)(2,1)S(1)} collective-permute-done((bf16[512,128]{1,0:T(8,128)(2,1)S(1)}, bf16[512,128]{1,0:T(8,128)(2,1)S(1)}, u32[]{:S(2)}, u32[]{:S(2)}) %collective-permute-start.5) | collective-permute-done | bytes 131104 | tf_op jit(solution)/shard_map/ppermute | solution.py:254
  58.4 3.5 %collective-permute-done.6.refs_3_ = bf16[512,128]{1,0:T(8,128)(2,1)S(1)} collective-permute-done((bf16[512,128]{1,0:T(8,128)(2,1)S(1)}, bf16[512,128]{1,0:T(8,128)(2,1)S(1)}, u32[]{:S(2)}, u32[]{:S(2)}) %collective-permute-start.6) | collective-permute-done | bytes 131104 | tf_op jit(solution)/shard_map/ppermute | solution.py:254
  61.8 4.7 %shard_map.97 = (f32[128,2048]{1,0:T(8,128)S(1)}, bf16[1024,128]{1,0:T(8,128)(2,1)S(1)}, bf16[1024,128]{1,0:T(8,128)(2,1)S(1)}) custom-call(s32[8,256]{1,0:T(8,128)S(1)} %tile.22.low_ref, s32[8,256]{1,0:T(8,128)S(1)} %tile.24.pos_ref, bf16[8,528,128]{2,1,0:T(8,128)(2,1)S(1)} %all-to-all-done.1.msg_ref, bf16[512,128]{1,0:T(8,128)(2,1)S(1)} %collective-permute-done.3.refs_0_, ...), custom_call_target="tpu_custom_call" | custom-call | flops 2684354560 | bytes 4194304 | tf_op jit(solution)/shard_map/pallas_call | solution.py:200
  66.6 1.9 %collective-permute-start.7 = (bf16[1024,128]{1,0:T(8,128)(2,1)S(1)}, bf16[1024,128]{1,0:T(8,128)(2,1)S(1)}, u32[]{:S(2)}, u32[]{:S(2)}) collective-permute-start(bf16[1024,128]{1,0:T(8,128)(2,1)S(1)} %get-tuple-element.31), channel_id=1, source_target_pairs={{0,8},{8,16},{16,24},{24,32},{32,40},{40,48},{48,56},{56,64},{64,7... | collective-permute-start | bytes 786440 | tf_op jit(solution)/shard_map/ppermute | solution.py:260
  68.5 7.6 %collective-permute-start.8 = (bf16[1024,128]{1,0:T(8,128)(2,1)S(1)}, bf16[1024,128]{1,0:T(8,128)(2,1)S(1)}, u32[]{:S(2)}, u32[]{:S(2)}) collective-permute-start(bf16[1024,128]{1,0:T(8,128)(2,1)S(1)} %get-tuple-element.32), channel_id=1, source_target_pairs={{0,504},{8,0},{16,8},{24,16},{32,24},{40,32},{48,40},{56,48},{64,5... | collective-permute-start | bytes 786440 | tf_op jit(solution)/shard_map/ppermute | solution.py:260
  76.1 0.0 collective-permute-done.1.refs_0_
  76.1 4.5 %shard_map.98 = (bf16[8,256,128]{2,1,0:T(8,128)(2,1)}, f32[512,128]{1,0:T(8,128)S(1)}, f32[512,128]{1,0:T(8,128)S(1)}, f32[512,128]{1,0:T(8,128)S(1)}) custom-call(s32[8,256]{1,0:T(8,128)S(1)} %tile.22.low_ref, s32[8,256]{1,0:T(8,128)S(1)} %tile.24.pos_ref, bf16[8,528,128]{2,1,0:T(8,128)(2,1)S(1)} %all-to-all-done.1.msg_ref, ...), custom_call_target="tpu_custom_call" | custom-call | flops 2013265920 | bytes 4194304 | tf_op jit(solution)/shard_map/pallas_call | solution.py:200
  80.6 8.9 %all-to-all-start.2 = ((bf16[8,256,128]{2,1,0:T(8,128)(2,1)}), bf16[8,256,128]{2,1,0:T(8,128)(2,1)S(1)}, u32[]{:S(2)}, u32[]{:S(2)}) async-start(bf16[8,256,128]{2,1,0:T(8,128)(2,1)} %get-tuple-element.29), calls=%async_computation.2 | async-start | bytes 1048576 | tf_op jit(solution)/shard_map/all_to_all | solution.py:266
  89.5 0.0 collective-permute-done.7.last_ref
  89.5 0.1 shard_map.99
  89.6 1.9 %collective-permute-start.9 = (bf16[512,128]{1,0:T(8,128)(2,1)S(1)}, bf16[512,128]{1,0:T(8,128)(2,1)S(1)}, u32[]{:S(2)}, u32[]{:S(2)}) collective-permute-start(bf16[512,128]{1,0:T(8,128)(2,1)S(1)} %get-tuple-element.35), channel_id=1, source_target_pairs={{0,496},{8,504},{16,0},{24,8},{32,16},{40,24},{48,32},{56,40},{64,... | collective-permute-start | bytes 393224 | tf_op jit(solution)/shard_map/ppermute | solution.py:260
  91.6 1.9 %collective-permute-start.10 = (bf16[512,128]{1,0:T(8,128)(2,1)S(1)}, bf16[512,128]{1,0:T(8,128)(2,1)S(1)}, u32[]{:S(2)}, u32[]{:S(2)}) collective-permute-start(bf16[512,128]{1,0:T(8,128)(2,1)S(1)} %get-tuple-element.36), channel_id=1, source_target_pairs={{0,472},{8,480},{16,488},{24,496},{32,504},{40,0},{48,8},{56,16},{... | collective-permute-start | bytes 393224 | tf_op jit(solution)/shard_map/ppermute | solution.py:260
  93.5 10.6 %collective-permute-done.9.near_ref = bf16[512,128]{1,0:T(8,128)(2,1)S(1)} collective-permute-done((bf16[512,128]{1,0:T(8,128)(2,1)S(1)}, bf16[512,128]{1,0:T(8,128)(2,1)S(1)}, u32[]{:S(2)}, u32[]{:S(2)}) %collective-permute-start.9) | collective-permute-done | bytes 131104 | tf_op jit(solution)/shard_map/ppermute | solution.py:260
  104.1 2.9 %collective-permute-done.10.far_ref = bf16[512,128]{1,0:T(8,128)(2,1)S(1)} collective-permute-done((bf16[512,128]{1,0:T(8,128)(2,1)S(1)}, bf16[512,128]{1,0:T(8,128)(2,1)S(1)}, u32[]{:S(2)}, u32[]{:S(2)}) %collective-permute-start.10) | collective-permute-done | bytes 131104 | tf_op jit(solution)/shard_map/ppermute | solution.py:260
  107.0 0.9 shard_map.100
  (12 shorter events, 0.0 us)
Async XLA Ops:
  2.2 18.5 %all-to-all-start = ((bf16[8,64,128]{2,1,0:T(8,128)(2,1)}), bf16[8,64,128]{2,1,0:T(8,128)(2,1)S(1)}, u32[]{:S(2)}, u32[]{:S(2)}) async-start(bf16[8,64,128]{2,1,0:T(8,128)(2,1)} %shard_map.95), calls=%async_computation | async-start | bytes 262144 | tf_op jit(solution)/shard_map/all_to_all | solution.py:266
  20.7 7.8 %collective-permute-start = (bf16[512,128]{1,0:T(8,128)(2,1)S(1)}, bf16[512,128]{1,0:T(8,128)(2,1)S(1)}, u32[]{:S(2)}, u32[]{:S(2)}) collective-permute-start(bf16[512,128]{1,0:T(8,128)(2,1)S(1)} %bitcast.10), channel_id=1, source_target_pairs={{0,64},{64,128},{128,192},{192,256},{256,320},{320,384},{384,448},... | collective-permute-start | bytes 393224 | tf_op jit(solution)/shard_map/ppermute | solution.py:254
  22.6 39.2 %all-to-all-start.1 = ((bf16[8,528,128]{2,1,0:T(8,128)(2,1)}), bf16[8,528,128]{2,1,0:T(8,128)(2,1)S(1)}, u32[]{:S(2)}, u32[]{:S(2)}) async-start(bf16[8,528,128]{2,1,0:T(8,128)(2,1)} %shard_map.94), calls=%async_computation.1 | async-start | bytes 2162688 | tf_op jit(solution)/shard_map/all_to_all | solution.py:266
  28.5 20.5 %copy-start = (s32[256]{0:T(256)S(1)}, s32[256]{0:T(256)}, u32[]{:S(2)}) copy-start(s32[256]{0:T(256)} %param.13) | copy-start | bytes 3076
  28.7 22.5 %collective-permute-start.3 = (bf16[512,128]{1,0:T(8,128)(2,1)S(1)}, bf16[512,128]{1,0:T(8,128)(2,1)S(1)}, u32[]{:S(2)}, u32[]{:S(2)}) collective-permute-start(bf16[512,128]{1,0:T(8,128)(2,1)S(1)} %get-tuple-element.24), channel_id=1, source_target_pairs={{0,48},{8,56},{16,0},{24,8},{32,16},{40,24},{48,32},{56,40},{1,49}... | collective-permute-start | bytes 393224 | tf_op jit(solution)/shard_map/ppermute | solution.py:254
  37.6 17.9 %collective-permute-start.4 = (bf16[512,128]{1,0:T(8,128)(2,1)S(1)}, bf16[512,128]{1,0:T(8,128)(2,1)S(1)}, u32[]{:S(2)}, u32[]{:S(2)}) collective-permute-start(bf16[512,128]{1,0:T(8,128)(2,1)S(1)} %get-tuple-element.25), channel_id=1, source_target_pairs={{0,32},{8,40},{16,48},{24,56},{32,0},{40,8},{48,16},{56,24},{1,33}... | collective-permute-start | bytes 393224 | tf_op jit(solution)/shard_map/ppermute | solution.py:254
  39.5 18.9 %collective-permute-start.5 = (bf16[512,128]{1,0:T(8,128)(2,1)S(1)}, bf16[512,128]{1,0:T(8,128)(2,1)S(1)}, u32[]{:S(2)}, u32[]{:S(2)}) collective-permute-start(bf16[512,128]{1,0:T(8,128)(2,1)S(1)} %get-tuple-element.26), channel_id=1, source_target_pairs={{0,24},{8,32},{16,40},{24,48},{32,56},{40,0},{48,8},{56,16},{1,25}... | collective-permute-start | bytes 393224 | tf_op jit(solution)/shard_map/ppermute | solution.py:254
  44.7 17.2 %collective-permute-start.6 = (bf16[512,128]{1,0:T(8,128)(2,1)S(1)}, bf16[512,128]{1,0:T(8,128)(2,1)S(1)}, u32[]{:S(2)}, u32[]{:S(2)}) collective-permute-start(bf16[512,128]{1,0:T(8,128)(2,1)S(1)} %get-tuple-element.27), channel_id=1, source_target_pairs={{0,8},{8,16},{16,24},{24,32},{32,40},{40,48},{48,56},{56,0},{1,9},... | collective-permute-start | bytes 393224 | tf_op jit(solution)/shard_map/ppermute | solution.py:254
  49.3 26.8 %collective-permute-start.1 = (bf16[512,128]{1,0:T(8,128)(2,1)S(1)}, bf16[512,128]{1,0:T(8,128)(2,1)S(1)}, u32[]{:S(2)}, u32[]{:S(2)}) collective-permute-start(bf16[512,128]{1,0:T(8,128)(2,1)S(1)} %get-tuple-element.22), channel_id=1, source_target_pairs={{0,40},{8,48},{16,56},{24,0},{32,8},{40,16},{48,24},{56,32},{1,41}... | collective-permute-start | bytes 393224 | tf_op jit(solution)/shard_map/ppermute | solution.py:254
  51.2 24.9 %collective-permute-start.2 = (bf16[512,128]{1,0:T(8,128)(2,1)S(1)}, bf16[512,128]{1,0:T(8,128)(2,1)S(1)}, u32[]{:S(2)}, u32[]{:S(2)}) collective-permute-start(bf16[512,128]{1,0:T(8,128)(2,1)S(1)} %get-tuple-element.23), channel_id=1, source_target_pairs={{0,16},{8,24},{16,32},{24,40},{32,48},{40,56},{48,0},{56,8},{1,17}... | collective-permute-start | bytes 393224 | tf_op jit(solution)/shard_map/ppermute | solution.py:254
  66.6 23.0 %collective-permute-start.7 = (bf16[1024,128]{1,0:T(8,128)(2,1)S(1)}, bf16[1024,128]{1,0:T(8,128)(2,1)S(1)}, u32[]{:S(2)}, u32[]{:S(2)}) collective-permute-start(bf16[1024,128]{1,0:T(8,128)(2,1)S(1)} %get-tuple-element.31), channel_id=1, source_target_pairs={{0,8},{8,16},{16,24},{24,32},{32,40},{40,48},{48,56},{56,64},{64,7... | collective-permute-start | bytes 786440 | tf_op jit(solution)/shard_map/ppermute | solution.py:260
  68.5 21.0 %collective-permute-start.8 = (bf16[1024,128]{1,0:T(8,128)(2,1)S(1)}, bf16[1024,128]{1,0:T(8,128)(2,1)S(1)}, u32[]{:S(2)}, u32[]{:S(2)}) collective-permute-start(bf16[1024,128]{1,0:T(8,128)(2,1)S(1)} %get-tuple-element.32), channel_id=1, source_target_pairs={{0,504},{8,0},{16,8},{24,16},{32,24},{40,32},{48,40},{56,48},{64,5... | collective-permute-start | bytes 786440 | tf_op jit(solution)/shard_map/ppermute | solution.py:260
  80.6 26.4 %all-to-all-start.2 = ((bf16[8,256,128]{2,1,0:T(8,128)(2,1)}), bf16[8,256,128]{2,1,0:T(8,128)(2,1)S(1)}, u32[]{:S(2)}, u32[]{:S(2)}) async-start(bf16[8,256,128]{2,1,0:T(8,128)(2,1)} %get-tuple-element.29), calls=%async_computation.2 | async-start | bytes 1048576 | tf_op jit(solution)/shard_map/all_to_all | solution.py:266
  89.6 14.5 %collective-permute-start.9 = (bf16[512,128]{1,0:T(8,128)(2,1)S(1)}, bf16[512,128]{1,0:T(8,128)(2,1)S(1)}, u32[]{:S(2)}, u32[]{:S(2)}) collective-permute-start(bf16[512,128]{1,0:T(8,128)(2,1)S(1)} %get-tuple-element.35), channel_id=1, source_target_pairs={{0,496},{8,504},{16,0},{24,8},{32,16},{40,24},{48,32},{56,40},{64,... | collective-permute-start | bytes 393224 | tf_op jit(solution)/shard_map/ppermute | solution.py:260
  91.6 15.5 %collective-permute-start.10 = (bf16[512,128]{1,0:T(8,128)(2,1)S(1)}, bf16[512,128]{1,0:T(8,128)(2,1)S(1)}, u32[]{:S(2)}, u32[]{:S(2)}) collective-permute-start(bf16[512,128]{1,0:T(8,128)(2,1)S(1)} %get-tuple-element.36), channel_id=1, source_target_pairs={{0,472},{8,480},{16,488},{24,496},{32,504},{40,0},{48,8},{56,16},{... | collective-permute-start | bytes 393224 | tf_op jit(solution)/shard_map/ppermute | solution.py:260

commit v4 on v3

--- a/solution.py
+++ b/solution.py
@@ -164,7 +164,7 @@
         if not first:
             dqt = dqt + before_ref[:, cols]
         if last:
-            dq_ref[j] = (dqt * scale).T.astype(BF16)
+            dq_ref[j] = (dqt * scale).astype(BF16).T
         else:
             dq_ref[:, cols] = dqt
 
@@ -229,7 +229,7 @@
         out[...] = (ref[...] + last_ref[part].astype(F32) + next_ref[part].astype(F32)).astype(BF16)
 
 
-def finish(groups, per, got_ref, own_ref, near_ref, far_ref, q_out, k_out, v_out, q_ref, k_ref, v_ref, sems):
+def finish(groups, per, got_ref, own_ref, far_ref, near_ref, q_out, k_out, v_out, q_ref, k_ref, v_ref, sems):
     rows, block = q_ref.shape[0], k_ref.shape[0]
     copies = []
     for n, (ref, out, at) in enumerate(((k_ref, k_out, 0), (v_ref, v_out, block))):
@@ -306,7 +306,7 @@
     got = exchange(message)
     z = lax.axis_index("z")
 
-    reach = (6, 4, 3, 1, 5, 2)
+    reach = (4, 3, 6, 1, 5, 2)
     sent = call(
         functools.partial(choose, reach),
         [shape((2 * block, HD), BF16)] * REACH,
@@ -324,7 +324,7 @@
     run = functools.partial(attend, scale, chunks, rows, per, low, pos, got)
 
     dq, g14, g36 = run(
-        (6, 4, 3, 1), [kv[s] for s in (6, 4, 3, 1)], [(n, 0) for n in range(4)], [(BF16, (1, 4)), (BF16, (3, 6))]
+        (6, 4, 3, 1), [kv[s] for s in (4, 3, 6, 1)], [(2, 0), (0, 0), (1, 0), (3, 0)], [(BF16, (1, 4)), (BF16, (3, 6))]
     )
     from_last, from_next = hop(g14, 1), hop(g36, -1)
     dq, g5, g2, g0 = run(
@@ -354,7 +354,7 @@
         moved=4 * rows * wide,
         in_specs=[vmem] * 4,
         out_specs=[hbm] * 3,
-    )(back_q, g0, g2, g5)
+    )(back_q, g0, g5, g2)
     return grad_q, grad_k, grad_v
 
 

time: 109 us -> 104 us (0.954)
  waiting for transfers between devices: 26.4 us -> 18.5 us
  starting transfers between devices: 65.1 us -> 68.3 us
    ppermute x7, waiting for transfers between devices: 7.91 us -> 1.53 us  [turn(): lax.ppermute(array, axis, [(i, (i + by) % size) for i in range(size)])]
    ppermute x4, starting transfers between devices: 13.3 us -> 15.6 us  [hop(): lax.ppermute(array, axes, [(i, (i + by) % size) for i in range(size)])]
    ppermute x4, waiting for transfers between devices: 13.6 us -> 12 us  [hop(): lax.ppermute(array, axes, [(i, (i + by) % size) for i in range(size)])]
    ppermute x7, starting transfers between devices: 28.3 us -> 29.5 us  [turn(): lax.ppermute(array, axis, [(i, (i + by) % size) for i in range(size)])]
  transfers between devices with their start and end apart: 14 -> 14, of which waited for: 6 -> 4; matrix products, arithmetic and copies ran while one was open for 0% -> 0% of each run, Pallas kernels for 12% -> 12%
where the time goes in v4:
time: 104 us; the launch traced here: 103 us
  starting transfers between devices  68.3 us (66%)
  waiting for transfers between devices  18.5 us (18%)
  Pallas kernels  15.3 us (15%)
    ppermute x7, starting transfers between devices, turn(): lax.ppermute(array, axis, [(i, (i + by) % size) for i in range(size)])  29.5 us
    all_to_all x3, starting transfers between devices, exchange(): lax.all_to_all(flat, 'head', split_axis=0, concat_axis=0, tiled=True)  23.2 us
    ppermute x4, starting transfers between devices, hop(): lax.ppermute(array, axes, [(i, (i + by) % size) for i in range(size)])  15.6 us
    ppermute x4, waiting for transfers between devices, hop(): lax.ppermute(array, axes, [(i, (i + by) % size) for i in range(size)])  12 us
    pallas_call x2, Pallas kernels, attend(): call(functools.partial(attention, scale, chunks, rows, per, blocks, sourc...  9.2 us
    all_to_all x3, waiting for transfers between devices, exchange(): lax.all_to_all(flat, 'head', split_axis=0, concat_axis=0, tiled=True)  4.97 us
    pallas_call x1, Pallas kernels, per_device(): call(functools.partial(pack_queries, groups, per), shape((groups, 2 * spa...  3.38 us
  transfers between devices with their start and end apart: 14, of which 4 were waited for; matrix products, arithmetic and copies ran while one was open for 0% of the time, Pallas kernels for 12%

profile of v4, /device:TPU:1, one launch (start us, length us, event | category | flops | bytes accessed | tf_op | source)
XLA Modules:
  0.0 103.2 jit_solution(4751058918753727516)
XLA Ops:
  0.6 1.5 %shard_map.95 = bf16[8,64,128]{2,1,0:T(8,128)(2,1)} custom-call(bf16[32,1024]{1,0:T(8,128)(2,1)} %key_hbm.1, bf16[32,1024]{1,0:T(8,128)(2,1)} %value_hbm.1), custom_call_target="tpu_custom_call" | custom-call | bytes 262144 | tf_op jit(solution)/shard_map/pallas_call | solution.py:282
  2.2 10.2 %all-to-all-start = ((bf16[8,64,128]{2,1,0:T(8,128)(2,1)}), bf16[8,64,128]{2,1,0:T(8,128)(2,1)S(1)}, u32[]{:S(2)}, u32[]{:S(2)}) async-start(bf16[8,64,128]{2,1,0:T(8,128)(2,1)} %shard_map.95), calls=%async_computation | async-start | bytes 262144 | tf_op jit(solution)/shard_map/all_to_all | solution.py:266
  12.3 3.4 %shard_map.94 = bf16[8,528,128]{2,1,0:T(8,128)(2,1)} custom-call(bf16[32,8192]{1,0:T(8,128)(2,1)} %query_hbm.1, bf16[32,8192]{1,0:T(8,128)(2,1)} %dout_hbm.1, bf16[32,8192]{1,0:T(8,128)(2,1)} %output_hbm.1, f32[32,64]{1,0:T(8,128)} %lse_hbm.1), custom_call_target="tpu_custom_call" | custom-call | bytes 2621440 | tf_op jit(solution)/shard_map/pallas_call | solution.py:292
  15.7 5.0 %all-to-all-done = bf16[8,64,128]{2,1,0:T(8,128)(2,1)S(1)} async-done(((bf16[8,64,128]{2,1,0:T(8,128)(2,1)}), bf16[8,64,128]{2,1,0:T(8,128)(2,1)S(1)}, u32[]{:S(2)}, u32[]{:S(2)}) %all-to-all-start) | async-done | bytes 131104 | tf_op jit(solution)/shard_map/all_to_all | solution.py:266
  20.7 1.9 %collective-permute-start = (bf16[512,128]{1,0:T(8,128)(2,1)S(1)}, bf16[512,128]{1,0:T(8,128)(2,1)S(1)}, u32[]{:S(2)}, u32[]{:S(2)}) collective-permute-start(bf16[512,128]{1,0:T(8,128)(2,1)S(1)} %bitcast.10), channel_id=1, source_target_pairs={{0,64},{64,128},{128,192},{192,256},{256,320},{320,384},{384,448},... | collective-permute-start | bytes 393224 | tf_op jit(solution)/shard_map/ppermute | solution.py:254
  22.6 4.4 %all-to-all-start.1 = ((bf16[8,528,128]{2,1,0:T(8,128)(2,1)}), bf16[8,528,128]{2,1,0:T(8,128)(2,1)S(1)}, u32[]{:S(2)}, u32[]{:S(2)}) async-start(bf16[8,528,128]{2,1,0:T(8,128)(2,1)} %shard_map.94), calls=%async_computation.1 | async-start | bytes 2162688 | tf_op jit(solution)/shard_map/all_to_all | solution.py:266
  27.0 1.5 %collective-permute-done.older_ref = bf16[512,128]{1,0:T(8,128)(2,1)S(1)} collective-permute-done((bf16[512,128]{1,0:T(8,128)(2,1)S(1)}, bf16[512,128]{1,0:T(8,128)(2,1)S(1)}, u32[]{:S(2)}, u32[]{:S(2)}) %collective-permute-start) | collective-permute-done | bytes 131104 | tf_op jit(solution)/shard_map/ppermute | solution.py:254
  28.5 0.2 shard_map.96
  28.7 8.9 %collective-permute-start.3 = (bf16[512,128]{1,0:T(8,128)(2,1)S(1)}, bf16[512,128]{1,0:T(8,128)(2,1)S(1)}, u32[]{:S(2)}, u32[]{:S(2)}) collective-permute-start(bf16[512,128]{1,0:T(8,128)(2,1)S(1)} %get-tuple-element.24), channel_id=1, source_target_pairs={{0,32},{8,40},{16,48},{24,56},{32,0},{40,8},{48,16},{56,24},{1,33}... | collective-permute-start | bytes 393224 | tf_op jit(solution)/shard_map/ppermute | solution.py:254
  37.5 4.9 %collective-permute-start.4 = (bf16[512,128]{1,0:T(8,128)(2,1)S(1)}, bf16[512,128]{1,0:T(8,128)(2,1)S(1)}, u32[]{:S(2)}, u32[]{:S(2)}) collective-permute-start(bf16[512,128]{1,0:T(8,128)(2,1)S(1)} %get-tuple-element.25), channel_id=1, source_target_pairs={{0,24},{8,32},{16,40},{24,48},{32,56},{40,0},{48,8},{56,16},{1,25}... | collective-permute-start | bytes 393224 | tf_op jit(solution)/shard_map/ppermute | solution.py:254
  42.5 3.4 %collective-permute-start.5 = (bf16[512,128]{1,0:T(8,128)(2,1)S(1)}, bf16[512,128]{1,0:T(8,128)(2,1)S(1)}, u32[]{:S(2)}, u32[]{:S(2)}) collective-permute-start(bf16[512,128]{1,0:T(8,128)(2,1)S(1)} %get-tuple-element.26), channel_id=1, source_target_pairs={{0,48},{8,56},{16,0},{24,8},{32,16},{40,24},{48,32},{56,40},{1,49}... | collective-permute-start | bytes 393224 | tf_op jit(solution)/shard_map/ppermute | solution.py:254
  45.9 3.1 %collective-permute-start.6 = (bf16[512,128]{1,0:T(8,128)(2,1)S(1)}, bf16[512,128]{1,0:T(8,128)(2,1)S(1)}, u32[]{:S(2)}, u32[]{:S(2)}) collective-permute-start(bf16[512,128]{1,0:T(8,128)(2,1)S(1)} %get-tuple-element.27), channel_id=1, source_target_pairs={{0,8},{8,16},{16,24},{24,32},{32,40},{40,48},{48,56},{56,0},{1,9},... | collective-permute-start | bytes 393224 | tf_op jit(solution)/shard_map/ppermute | solution.py:254
  49.0 0.1 tile.20
  49.1 0.1 tile.24.pos_ref
  49.2 0.1 tile.22.low_ref
  49.3 1.9 %collective-permute-start.1 = (bf16[512,128]{1,0:T(8,128)(2,1)S(1)}, bf16[512,128]{1,0:T(8,128)(2,1)S(1)}, u32[]{:S(2)}, u32[]{:S(2)}) collective-permute-start(bf16[512,128]{1,0:T(8,128)(2,1)S(1)} %get-tuple-element.22), channel_id=1, source_target_pairs={{0,40},{8,48},{16,56},{24,0},{32,8},{40,16},{48,24},{56,32},{1,41}... | collective-permute-start | bytes 393224 | tf_op jit(solution)/shard_map/ppermute | solution.py:254
  51.2 0.0 collective-permute-done.3.refs_0_
  51.2 5.5 %collective-permute-start.2 = (bf16[512,128]{1,0:T(8,128)(2,1)S(1)}, bf16[512,128]{1,0:T(8,128)(2,1)S(1)}, u32[]{:S(2)}, u32[]{:S(2)}) collective-permute-start(bf16[512,128]{1,0:T(8,128)(2,1)S(1)} %get-tuple-element.23), channel_id=1, source_target_pairs={{0,16},{8,24},{16,32},{24,40},{32,48},{40,56},{48,0},{56,8},{1,17}... | collective-permute-start | bytes 393224 | tf_op jit(solution)/shard_map/ppermute | solution.py:254
  56.7 0.0 collective-permute-done.6.refs_3_
  56.7 4.7 %shard_map.97 = (f32[128,2048]{1,0:T(8,128)S(1)}, bf16[1024,128]{1,0:T(8,128)(2,1)S(1)}, bf16[1024,128]{1,0:T(8,128)(2,1)S(1)}) custom-call(s32[8,256]{1,0:T(8,128)S(1)} %tile.22.low_ref, s32[8,256]{1,0:T(8,128)S(1)} %tile.24.pos_ref, bf16[8,528,128]{2,1,0:T(8,128)(2,1)S(1)} %all-to-all-done.1.msg_ref, bf16[512,128]{1,0:T(8,128)(2,1)S(1)} %collective-permute-done.3.refs_0_, ...), custom_call_target="tpu_custom_call" | custom-call | flops 2684354560 | bytes 4194304 | tf_op jit(solution)/shard_map/pallas_call | solution.py:200
  61.4 1.9 %collective-permute-start.7 = (bf16[1024,128]{1,0:T(8,128)(2,1)S(1)}, bf16[1024,128]{1,0:T(8,128)(2,1)S(1)}, u32[]{:S(2)}, u32[]{:S(2)}) collective-permute-start(bf16[1024,128]{1,0:T(8,128)(2,1)S(1)} %get-tuple-element.31), channel_id=1, source_target_pairs={{0,8},{8,16},{16,24},{24,32},{32,40},{40,48},{48,56},{56,64},{64,7... | collective-permute-start | bytes 786440 | tf_op jit(solution)/shard_map/ppermute | solution.py:260
  63.4 8.4 %collective-permute-start.8 = (bf16[1024,128]{1,0:T(8,128)(2,1)S(1)}, bf16[1024,128]{1,0:T(8,128)(2,1)S(1)}, u32[]{:S(2)}, u32[]{:S(2)}) collective-permute-start(bf16[1024,128]{1,0:T(8,128)(2,1)S(1)} %get-tuple-element.32), channel_id=1, source_target_pairs={{0,504},{8,0},{16,8},{24,16},{32,24},{40,32},{48,40},{56,48},{64,5... | collective-permute-start | bytes 786440 | tf_op jit(solution)/shard_map/ppermute | solution.py:260
  71.7 0.0 collective-permute-done.2.refs_1_
  71.8 4.5 %shard_map.98 = (bf16[8,256,128]{2,1,0:T(8,128)(2,1)}, f32[512,128]{1,0:T(8,128)S(1)}, f32[512,128]{1,0:T(8,128)S(1)}, f32[512,128]{1,0:T(8,128)S(1)}) custom-call(s32[8,256]{1,0:T(8,128)S(1)} %tile.22.low_ref, s32[8,256]{1,0:T(8,128)S(1)} %tile.24.pos_ref, bf16[8,528,128]{2,1,0:T(8,128)(2,1)S(1)} %all-to-all-done.1.msg_ref, ...), custom_call_target="tpu_custom_call" | custom-call | flops 2013265920 | bytes 4194304 | tf_op jit(solution)/shard_map/pallas_call | solution.py:200
  76.2 8.6 %all-to-all-start.2 = ((bf16[8,256,128]{2,1,0:T(8,128)(2,1)}), bf16[8,256,128]{2,1,0:T(8,128)(2,1)S(1)}, u32[]{:S(2)}, u32[]{:S(2)}) async-start(bf16[8,256,128]{2,1,0:T(8,128)(2,1)} %get-tuple-element.29), calls=%async_computation.2 | async-start | bytes 1048576 | tf_op jit(solution)/shard_map/all_to_all | solution.py:266
  84.9 0.1 shard_map.99
  85.0 1.9 %collective-permute-start.9 = (bf16[512,128]{1,0:T(8,128)(2,1)S(1)}, bf16[512,128]{1,0:T(8,128)(2,1)S(1)}, u32[]{:S(2)}, u32[]{:S(2)}) collective-permute-start(bf16[512,128]{1,0:T(8,128)(2,1)S(1)} %get-tuple-element.35), channel_id=1, source_target_pairs={{0,472},{8,480},{16,488},{24,496},{32,504},{40,0},{48,8},{56,16},{... | collective-permute-start | bytes 393224 | tf_op jit(solution)/shard_map/ppermute | solution.py:260
  86.9 3.4 %collective-permute-start.10 = (bf16[512,128]{1,0:T(8,128)(2,1)S(1)}, bf16[512,128]{1,0:T(8,128)(2,1)S(1)}, u32[]{:S(2)}, u32[]{:S(2)}) collective-permute-start(bf16[512,128]{1,0:T(8,128)(2,1)S(1)} %get-tuple-element.36), channel_id=1, source_target_pairs={{0,496},{8,504},{16,0},{24,8},{32,16},{40,24},{48,32},{56,40},{64,... | collective-permute-start | bytes 393224 | tf_op jit(solution)/shard_map/ppermute | solution.py:260
  90.3 9.2 %collective-permute-done.9.far_ref = bf16[512,128]{1,0:T(8,128)(2,1)S(1)} collective-permute-done((bf16[512,128]{1,0:T(8,128)(2,1)S(1)}, bf16[512,128]{1,0:T(8,128)(2,1)S(1)}, u32[]{:S(2)}, u32[]{:S(2)}) %collective-permute-start.9) | collective-permute-done | bytes 131104 | tf_op jit(solution)/shard_map/ppermute | solution.py:260
  99.5 2.8 %collective-permute-done.10.near_ref = bf16[512,128]{1,0:T(8,128)(2,1)S(1)} collective-permute-done((bf16[512,128]{1,0:T(8,128)(2,1)S(1)}, bf16[512,128]{1,0:T(8,128)(2,1)S(1)}, u32[]{:S(2)}, u32[]{:S(2)}) %collective-permute-start.10) | collective-permute-done | bytes 131104 | tf_op jit(solution)/shard_map/ppermute | solution.py:260
  102.3 0.0 all-to-all-done.2.got_ref
  102.3 0.9 shard_map.100
  (12 shorter events, 0.0 us)
Async XLA Ops:
  2.2 18.5 %all-to-all-start = ((bf16[8,64,128]{2,1,0:T(8,128)(2,1)}), bf16[8,64,128]{2,1,0:T(8,128)(2,1)S(1)}, u32[]{:S(2)}, u32[]{:S(2)}) async-start(bf16[8,64,128]{2,1,0:T(8,128)(2,1)} %shard_map.95), calls=%async_computation | async-start | bytes 262144 | tf_op jit(solution)/shard_map/all_to_all | solution.py:266
  20.7 7.8 %collective-permute-start = (bf16[512,128]{1,0:T(8,128)(2,1)S(1)}, bf16[512,128]{1,0:T(8,128)(2,1)S(1)}, u32[]{:S(2)}, u32[]{:S(2)}) collective-permute-start(bf16[512,128]{1,0:T(8,128)(2,1)S(1)} %bitcast.10), channel_id=1, source_target_pairs={{0,64},{64,128},{128,192},{192,256},{256,320},{320,384},{384,448},... | collective-permute-start | bytes 393224 | tf_op jit(solution)/shard_map/ppermute | solution.py:254
  22.6 34.1 %all-to-all-start.1 = ((bf16[8,528,128]{2,1,0:T(8,128)(2,1)}), bf16[8,528,128]{2,1,0:T(8,128)(2,1)S(1)}, u32[]{:S(2)}, u32[]{:S(2)}) async-start(bf16[8,528,128]{2,1,0:T(8,128)(2,1)} %shard_map.94), calls=%async_computation.1 | async-start | bytes 2162688 | tf_op jit(solution)/shard_map/all_to_all | solution.py:266
  28.5 20.5 %copy-start = (s32[256]{0:T(256)S(1)}, s32[256]{0:T(256)}, u32[]{:S(2)}) copy-start(s32[256]{0:T(256)} %param.13) | copy-start | bytes 3076
  28.7 22.5 %collective-permute-start.3 = (bf16[512,128]{1,0:T(8,128)(2,1)S(1)}, bf16[512,128]{1,0:T(8,128)(2,1)S(1)}, u32[]{:S(2)}, u32[]{:S(2)}) collective-permute-start(bf16[512,128]{1,0:T(8,128)(2,1)S(1)} %get-tuple-element.24), channel_id=1, source_target_pairs={{0,32},{8,40},{16,48},{24,56},{32,0},{40,8},{48,16},{56,24},{1,33}... | collective-permute-start | bytes 393224 | tf_op jit(solution)/shard_map/ppermute | solution.py:254
  37.5 19.1 %collective-permute-start.4 = (bf16[512,128]{1,0:T(8,128)(2,1)S(1)}, bf16[512,128]{1,0:T(8,128)(2,1)S(1)}, u32[]{:S(2)}, u32[]{:S(2)}) collective-permute-start(bf16[512,128]{1,0:T(8,128)(2,1)S(1)} %get-tuple-element.25), channel_id=1, source_target_pairs={{0,24},{8,32},{16,40},{24,48},{32,56},{40,0},{48,8},{56,16},{1,25}... | collective-permute-start | bytes 393224 | tf_op jit(solution)/shard_map/ppermute | solution.py:254
  42.5 14.2 %collective-permute-start.5 = (bf16[512,128]{1,0:T(8,128)(2,1)S(1)}, bf16[512,128]{1,0:T(8,128)(2,1)S(1)}, u32[]{:S(2)}, u32[]{:S(2)}) collective-permute-start(bf16[512,128]{1,0:T(8,128)(2,1)S(1)} %get-tuple-element.26), channel_id=1, source_target_pairs={{0,48},{8,56},{16,0},{24,8},{32,16},{40,24},{48,32},{56,40},{1,49}... | collective-permute-start | bytes 393224 | tf_op jit(solution)/shard_map/ppermute | solution.py:254
  45.9 10.8 %collective-permute-start.6 = (bf16[512,128]{1,0:T(8,128)(2,1)S(1)}, bf16[512,128]{1,0:T(8,128)(2,1)S(1)}, u32[]{:S(2)}, u32[]{:S(2)}) collective-permute-start(bf16[512,128]{1,0:T(8,128)(2,1)S(1)} %get-tuple-element.27), channel_id=1, source_target_pairs={{0,8},{8,16},{16,24},{24,32},{32,40},{40,48},{48,56},{56,0},{1,9},... | collective-permute-start | bytes 393224 | tf_op jit(solution)/shard_map/ppermute | solution.py:254
  49.3 22.5 %collective-permute-start.1 = (bf16[512,128]{1,0:T(8,128)(2,1)S(1)}, bf16[512,128]{1,0:T(8,128)(2,1)S(1)}, u32[]{:S(2)}, u32[]{:S(2)}) collective-permute-start(bf16[512,128]{1,0:T(8,128)(2,1)S(1)} %get-tuple-element.22), channel_id=1, source_target_pairs={{0,40},{8,48},{16,56},{24,0},{32,8},{40,16},{48,24},{56,32},{1,41}... | collective-permute-start | bytes 393224 | tf_op jit(solution)/shard_map/ppermute | solution.py:254
  51.2 20.6 %collective-permute-start.2 = (bf16[512,128]{1,0:T(8,128)(2,1)S(1)}, bf16[512,128]{1,0:T(8,128)(2,1)S(1)}, u32[]{:S(2)}, u32[]{:S(2)}) collective-permute-start(bf16[512,128]{1,0:T(8,128)(2,1)S(1)} %get-tuple-element.23), channel_id=1, source_target_pairs={{0,16},{8,24},{16,32},{24,40},{32,48},{40,56},{48,0},{56,8},{1,17}... | collective-permute-start | bytes 393224 | tf_op jit(solution)/shard_map/ppermute | solution.py:254
  61.4 23.4 %collective-permute-start.7 = (bf16[1024,128]{1,0:T(8,128)(2,1)S(1)}, bf16[1024,128]{1,0:T(8,128)(2,1)S(1)}, u32[]{:S(2)}, u32[]{:S(2)}) collective-permute-start(bf16[1024,128]{1,0:T(8,128)(2,1)S(1)} %get-tuple-element.31), channel_id=1, source_target_pairs={{0,8},{8,16},{16,24},{24,32},{32,40},{40,48},{48,56},{56,64},{64,7... | collective-permute-start | bytes 786440 | tf_op jit(solution)/shard_map/ppermute | solution.py:260
  63.4 21.5 %collective-permute-start.8 = (bf16[1024,128]{1,0:T(8,128)(2,1)S(1)}, bf16[1024,128]{1,0:T(8,128)(2,1)S(1)}, u32[]{:S(2)}, u32[]{:S(2)}) collective-permute-start(bf16[1024,128]{1,0:T(8,128)(2,1)S(1)} %get-tuple-element.32), channel_id=1, source_target_pairs={{0,504},{8,0},{16,8},{24,16},{32,24},{40,32},{48,40},{56,48},{64,5... | collective-permute-start | bytes 786440 | tf_op jit(solution)/shard_map/ppermute | solution.py:260
  76.2 26.1 %all-to-all-start.2 = ((bf16[8,256,128]{2,1,0:T(8,128)(2,1)}), bf16[8,256,128]{2,1,0:T(8,128)(2,1)S(1)}, u32[]{:S(2)}, u32[]{:S(2)}) async-start(bf16[8,256,128]{2,1,0:T(8,128)(2,1)} %get-tuple-element.29), calls=%async_computation.2 | async-start | bytes 1048576 | tf_op jit(solution)/shard_map/all_to_all | solution.py:266
  85.0 14.5 %collective-permute-start.9 = (bf16[512,128]{1,0:T(8,128)(2,1)S(1)}, bf16[512,128]{1,0:T(8,128)(2,1)S(1)}, u32[]{:S(2)}, u32[]{:S(2)}) collective-permute-start(bf16[512,128]{1,0:T(8,128)(2,1)S(1)} %get-tuple-element.35), channel_id=1, source_target_pairs={{0,472},{8,480},{16,488},{24,496},{32,504},{40,0},{48,8},{56,16},{... | collective-permute-start | bytes 393224 | tf_op jit(solution)/shard_map/ppermute | solution.py:260
  86.9 15.4 %collective-permute-start.10 = (bf16[512,128]{1,0:T(8,128)(2,1)S(1)}, bf16[512,128]{1,0:T(8,128)(2,1)S(1)}, u32[]{:S(2)}, u32[]{:S(2)}) collective-permute-start(bf16[512,128]{1,0:T(8,128)(2,1)S(1)} %get-tuple-element.36), channel_id=1, source_target_pairs={{0,496},{8,504},{16,0},{24,8},{32,16},{40,24},{48,32},{56,40},{64,... | collective-permute-start | bytes 393224 | tf_op jit(solution)/shard_map/ppermute | solution.py:260

commit v5 on v4

--- a/solution.py
+++ b/solution.py
@@ -229,24 +229,18 @@
         out[...] = (ref[...] + last_ref[part].astype(F32) + next_ref[part].astype(F32)).astype(BF16)
 
 
-def finish(groups, per, got_ref, own_ref, far_ref, near_ref, q_out, k_out, v_out, q_ref, k_ref, v_ref, sems):
-    rows, block = q_ref.shape[0], k_ref.shape[0]
-    copies = []
-    for n, (ref, out, at) in enumerate(((k_ref, k_out, 0), (v_ref, v_out, block))):
-        part = slice(at, at + block)
-        ref[...] = own_ref[part] + near_ref[part].astype(F32) + far_ref[part].astype(F32)
-        copies.append(pltpu.make_async_copy(ref, out, sems.at[n]))
-        copies[-1].start()
+def finish(own_ref, far_ref, near_ref, k_out, v_out):
+    block = k_out.shape[0]
+    for n, out in enumerate((k_out, v_out)):
+        part = slice(n * block, (n + 1) * block)
+        out[...] = own_ref[part] + far_ref[part].astype(F32) + near_ref[part].astype(F32)
+
+
+def unpack(groups, per, got_ref, out_ref):
+    rows = out_ref.shape[0]
     for g in range(groups):
         for h in range(per):
-            q_ref[:, (g * per + h) * HD : (g * per + h + 1) * HD] = got_ref[g, h * rows : (h + 1) * rows, :]
-    half = rows // 2
-    for n in range(2):
-        part = slice(n * half, (n + 1) * half)
-        copies.append(pltpu.make_async_copy(q_ref.at[part], q_out.at[part], sems.at[2 + n]))
-        copies[-1].start()
-    for copy in copies:
-        copy.wait()
+            out_ref[:, (g * per + h) * HD : (g * per + h + 1) * HD] = got_ref[g, h * rows : (h + 1) * rows, :]
 
 
 def turn(array, axis, by):
@@ -342,19 +336,19 @@
     )(from_last, from_next, g5, g2)
     g5, g2 = hop(g5, -5), hop(g2, -2)
 
-    grad_q, grad_k, grad_v = call(
-        functools.partial(finish, groups, per),
-        [shape((rows, wide), BF16), shape((block, HD), F32), shape((block, HD), F32)],
-        scratch=[
-            pltpu.VMEM((rows, wide), BF16),
-            pltpu.VMEM((block, HD), F32),
-            pltpu.VMEM((block, HD), F32),
-            pltpu.SemaphoreType.DMA((4,)),
-        ],
-        moved=4 * rows * wide,
-        in_specs=[vmem] * 4,
-        out_specs=[hbm] * 3,
-    )(back_q, g0, g5, g2)
+    grad_q = call(
+        functools.partial(unpack, groups, per),
+        shape((rows, wide), BF16),
+        flops=CHOOSE_FLOPS,
+        in_specs=[vmem],
+        out_specs=vmem,
+    )(back_q)
+    grad_k, grad_v = call(
+        finish,
+        [shape((block, HD), F32)] * 2,
+        in_specs=[vmem] * 3,
+        out_specs=[vmem] * 2,
+    )(g0, g5, g2)
     return grad_q, grad_k, grad_v
 
 

time: 104 us -> 105 us (level)
  transfers between devices with their start and end apart: 14 -> 14, of which waited for: 4 -> 4; matrix products, arithmetic and copies ran while one was open for 0% -> 0% of each run, Pallas kernels for 12% -> 13%
where the time goes in v5:
time: 105 us; the launch traced here: 104 us
  starting transfers between devices  68.3 us (65%)
  waiting for transfers between devices  18.5 us (18%)
  Pallas kernels  16 us (15%)
    ppermute x7, starting transfers between devices, turn(): lax.ppermute(array, axis, [(i, (i + by) % size) for i in range(size)])  29.5 us
    all_to_all x3, starting transfers between devices, exchange(): lax.all_to_all(flat, 'head', split_axis=0, concat_axis=0, tiled=True)  23.2 us
    ppermute x4, starting transfers between devices, hop(): lax.ppermute(array, axes, [(i, (i + by) % size) for i in range(size)])  15.6 us
    ppermute x4, waiting for transfers between devices, hop(): lax.ppermute(array, axes, [(i, (i + by) % size) for i in range(size)])  12 us
    pallas_call x2, Pallas kernels, attend(): call(functools.partial(attention, scale, chunks, rows, per, blocks, sourc...  9.2 us
    all_to_all x3, waiting for transfers between devices, exchange(): lax.all_to_all(flat, 'head', split_axis=0, concat_axis=0, tiled=True)  4.97 us
    pallas_call x1, Pallas kernels, per_device(): call(functools.partial(pack_queries, groups, per), shape((groups, 2 * spa...  3.38 us
  transfers between devices with their start and end apart: 14, of which 4 were waited for; matrix products, arithmetic and copies ran while one was open for 0% of the time, Pallas kernels for 13%

profile of v5, /device:TPU:1, one launch (start us, length us, event | category | flops | bytes accessed | tf_op | source)
XLA Modules:
  0.0 103.9 jit_solution(438757353521219064)
XLA Ops:
  0.6 1.5 %shard_map.95 = bf16[8,64,128]{2,1,0:T(8,128)(2,1)} custom-call(bf16[32,1024]{1,0:T(8,128)(2,1)} %key_hbm.1, bf16[32,1024]{1,0:T(8,128)(2,1)} %value_hbm.1), custom_call_target="tpu_custom_call" | custom-call | bytes 262144 | tf_op jit(solution)/shard_map/pallas_call | solution.py:276
  2.2 10.2 %all-to-all-start = ((bf16[8,64,128]{2,1,0:T(8,128)(2,1)}), bf16[8,64,128]{2,1,0:T(8,128)(2,1)S(1)}, u32[]{:S(2)}, u32[]{:S(2)}) async-start(bf16[8,64,128]{2,1,0:T(8,128)(2,1)} %shard_map.95), calls=%async_computation | async-start | bytes 262144 | tf_op jit(solution)/shard_map/all_to_all | solution.py:260
  12.3 3.4 %shard_map.94 = bf16[8,528,128]{2,1,0:T(8,128)(2,1)} custom-call(bf16[32,8192]{1,0:T(8,128)(2,1)} %query_hbm.1, bf16[32,8192]{1,0:T(8,128)(2,1)} %dout_hbm.1, bf16[32,8192]{1,0:T(8,128)(2,1)} %output_hbm.1, f32[32,64]{1,0:T(8,128)} %lse_hbm.1), custom_call_target="tpu_custom_call" | custom-call | bytes 2621440 | tf_op jit(solution)/shard_map/pallas_call | solution.py:286
  15.7 5.0 %all-to-all-done = bf16[8,64,128]{2,1,0:T(8,128)(2,1)S(1)} async-done(((bf16[8,64,128]{2,1,0:T(8,128)(2,1)}), bf16[8,64,128]{2,1,0:T(8,128)(2,1)S(1)}, u32[]{:S(2)}, u32[]{:S(2)}) %all-to-all-start) | async-done | bytes 131104 | tf_op jit(solution)/shard_map/all_to_all | solution.py:260
  20.7 1.9 %collective-permute-start = (bf16[512,128]{1,0:T(8,128)(2,1)S(1)}, bf16[512,128]{1,0:T(8,128)(2,1)S(1)}, u32[]{:S(2)}, u32[]{:S(2)}) collective-permute-start(bf16[512,128]{1,0:T(8,128)(2,1)S(1)} %bitcast.10), channel_id=1, source_target_pairs={{0,64},{64,128},{128,192},{192,256},{256,320},{320,384},{384,448},... | collective-permute-start | bytes 393224 | tf_op jit(solution)/shard_map/ppermute | solution.py:248
  22.6 4.4 %all-to-all-start.1 = ((bf16[8,528,128]{2,1,0:T(8,128)(2,1)}), bf16[8,528,128]{2,1,0:T(8,128)(2,1)S(1)}, u32[]{:S(2)}, u32[]{:S(2)}) async-start(bf16[8,528,128]{2,1,0:T(8,128)(2,1)} %shard_map.94), calls=%async_computation.1 | async-start | bytes 2162688 | tf_op jit(solution)/shard_map/all_to_all | solution.py:260
  27.0 1.5 %collective-permute-done.older_ref = bf16[512,128]{1,0:T(8,128)(2,1)S(1)} collective-permute-done((bf16[512,128]{1,0:T(8,128)(2,1)S(1)}, bf16[512,128]{1,0:T(8,128)(2,1)S(1)}, u32[]{:S(2)}, u32[]{:S(2)}) %collective-permute-start) | collective-permute-done | bytes 131104 | tf_op jit(solution)/shard_map/ppermute | solution.py:248
  28.5 0.2 shard_map.96
  28.7 8.9 %collective-permute-start.3 = (bf16[512,128]{1,0:T(8,128)(2,1)S(1)}, bf16[512,128]{1,0:T(8,128)(2,1)S(1)}, u32[]{:S(2)}, u32[]{:S(2)}) collective-permute-start(bf16[512,128]{1,0:T(8,128)(2,1)S(1)} %get-tuple-element.26), channel_id=1, source_target_pairs={{0,32},{8,40},{16,48},{24,56},{32,0},{40,8},{48,16},{56,24},{1,33}... | collective-permute-start | bytes 393224 | tf_op jit(solution)/shard_map/ppermute | solution.py:248
  37.5 4.9 %collective-permute-start.4 = (bf16[512,128]{1,0:T(8,128)(2,1)S(1)}, bf16[512,128]{1,0:T(8,128)(2,1)S(1)}, u32[]{:S(2)}, u32[]{:S(2)}) collective-permute-start(bf16[512,128]{1,0:T(8,128)(2,1)S(1)} %get-tuple-element.27), channel_id=1, source_target_pairs={{0,24},{8,32},{16,40},{24,48},{32,56},{40,0},{48,8},{56,16},{1,25}... | collective-permute-start | bytes 393224 | tf_op jit(solution)/shard_map/ppermute | solution.py:248
  42.5 3.4 %collective-permute-start.5 = (bf16[512,128]{1,0:T(8,128)(2,1)S(1)}, bf16[512,128]{1,0:T(8,128)(2,1)S(1)}, u32[]{:S(2)}, u32[]{:S(2)}) collective-permute-start(bf16[512,128]{1,0:T(8,128)(2,1)S(1)} %get-tuple-element.28), channel_id=1, source_target_pairs={{0,48},{8,56},{16,0},{24,8},{32,16},{40,24},{48,32},{56,40},{1,49}... | collective-permute-start | bytes 393224 | tf_op jit(solution)/shard_map/ppermute | solution.py:248
  45.9 3.1 %collective-permute-start.6 = (bf16[512,128]{1,0:T(8,128)(2,1)S(1)}, bf16[512,128]{1,0:T(8,128)(2,1)S(1)}, u32[]{:S(2)}, u32[]{:S(2)}) collective-permute-start(bf16[512,128]{1,0:T(8,128)(2,1)S(1)} %get-tuple-element.29), channel_id=1, source_target_pairs={{0,8},{8,16},{16,24},{24,32},{32,40},{40,48},{48,56},{56,0},{1,9},... | collective-permute-start | bytes 393224 | tf_op jit(solution)/shard_map/ppermute | solution.py:248
  49.0 0.1 tile.20
  49.1 0.1 tile.24.pos_ref
  49.2 0.1 tile.22.low_ref
  49.3 1.9 %collective-permute-start.1 = (bf16[512,128]{1,0:T(8,128)(2,1)S(1)}, bf16[512,128]{1,0:T(8,128)(2,1)S(1)}, u32[]{:S(2)}, u32[]{:S(2)}) collective-permute-start(bf16[512,128]{1,0:T(8,128)(2,1)S(1)} %get-tuple-element.24), channel_id=1, source_target_pairs={{0,40},{8,48},{16,56},{24,0},{32,8},{40,16},{48,24},{56,32},{1,41}... | collective-permute-start | bytes 393224 | tf_op jit(solution)/shard_map/ppermute | solution.py:248
  51.2 0.0 collective-permute-done.3.refs_0_
  51.2 5.5 %collective-permute-start.2 = (bf16[512,128]{1,0:T(8,128)(2,1)S(1)}, bf16[512,128]{1,0:T(8,128)(2,1)S(1)}, u32[]{:S(2)}, u32[]{:S(2)}) collective-permute-start(bf16[512,128]{1,0:T(8,128)(2,1)S(1)} %get-tuple-element.25), channel_id=1, source_target_pairs={{0,16},{8,24},{16,32},{24,40},{32,48},{40,56},{48,0},{56,8},{1,17}... | collective-permute-start | bytes 393224 | tf_op jit(solution)/shard_map/ppermute | solution.py:248
  56.6 0.0 collective-permute-done.4.refs_1_
  56.7 0.0 collective-permute-done.5.refs_2_
  56.7 4.7 %shard_map.97 = (f32[128,2048]{1,0:T(8,128)S(1)}, bf16[1024,128]{1,0:T(8,128)(2,1)S(1)}, bf16[1024,128]{1,0:T(8,128)(2,1)S(1)}) custom-call(s32[8,256]{1,0:T(8,128)S(1)} %tile.22.low_ref, s32[8,256]{1,0:T(8,128)S(1)} %tile.24.pos_ref, bf16[8,528,128]{2,1,0:T(8,128)(2,1)S(1)} %all-to-all-done.1.msg_ref, bf16[512,128]{1,0:T(8,128)(2,1)S(1)} %collective-permute-done.3.refs_0_, ...), custom_call_target="tpu_custom_call" | custom-call | flops 2684354560 | bytes 4194304 | tf_op jit(solution)/shard_map/pallas_call | solution.py:200
  61.4 1.9 %collective-permute-start.7 = (bf16[1024,128]{1,0:T(8,128)(2,1)S(1)}, bf16[1024,128]{1,0:T(8,128)(2,1)S(1)}, u32[]{:S(2)}, u32[]{:S(2)}) collective-permute-start(bf16[1024,128]{1,0:T(8,128)(2,1)S(1)} %get-tuple-element.33), channel_id=1, source_target_pairs={{0,8},{8,16},{16,24},{24,32},{32,40},{40,48},{48,56},{56,64},{64,7... | collective-permute-start | bytes 786440 | tf_op jit(solution)/shard_map/ppermute | solution.py:254
  63.4 8.4 %collective-permute-start.8 = (bf16[1024,128]{1,0:T(8,128)(2,1)S(1)}, bf16[1024,128]{1,0:T(8,128)(2,1)S(1)}, u32[]{:S(2)}, u32[]{:S(2)}) collective-permute-start(bf16[1024,128]{1,0:T(8,128)(2,1)S(1)} %get-tuple-element.34), channel_id=1, source_target_pairs={{0,504},{8,0},{16,8},{24,16},{32,24},{40,32},{48,40},{56,48},{64,5... | collective-permute-start | bytes 786440 | tf_op jit(solution)/shard_map/ppermute | solution.py:254
  71.8 4.5 %shard_map.98 = (bf16[8,256,128]{2,1,0:T(8,128)(2,1)}, f32[512,128]{1,0:T(8,128)S(1)}, f32[512,128]{1,0:T(8,128)S(1)}, f32[512,128]{1,0:T(8,128)S(1)}) custom-call(s32[8,256]{1,0:T(8,128)S(1)} %tile.22.low_ref, s32[8,256]{1,0:T(8,128)S(1)} %tile.24.pos_ref, bf16[8,528,128]{2,1,0:T(8,128)(2,1)S(1)} %all-to-all-done.1.msg_ref, ...), custom_call_target="tpu_custom_call" | custom-call | flops 2013265920 | bytes 4194304 | tf_op jit(solution)/shard_map/pallas_call | solution.py:200
  76.2 8.6 %all-to-all-start.2 = ((bf16[8,256,128]{2,1,0:T(8,128)(2,1)}), bf16[8,256,128]{2,1,0:T(8,128)(2,1)S(1)}, u32[]{:S(2)}, u32[]{:S(2)}) async-start(bf16[8,256,128]{2,1,0:T(8,128)(2,1)} %get-tuple-element.31), calls=%async_computation.2 | async-start | bytes 1048576 | tf_op jit(solution)/shard_map/all_to_all | solution.py:260
  84.9 0.1 shard_map.100
  85.0 1.9 %collective-permute-start.9 = (bf16[512,128]{1,0:T(8,128)(2,1)S(1)}, bf16[512,128]{1,0:T(8,128)(2,1)S(1)}, u32[]{:S(2)}, u32[]{:S(2)}) collective-permute-start(bf16[512,128]{1,0:T(8,128)(2,1)S(1)} %get-tuple-element.37), channel_id=1, source_target_pairs={{0,472},{8,480},{16,488},{24,496},{32,504},{40,0},{48,8},{56,16},{... | collective-permute-start | bytes 393224 | tf_op jit(solution)/shard_map/ppermute | solution.py:254
  86.9 3.4 %collective-permute-start.10 = (bf16[512,128]{1,0:T(8,128)(2,1)S(1)}, bf16[512,128]{1,0:T(8,128)(2,1)S(1)}, u32[]{:S(2)}, u32[]{:S(2)}) collective-permute-start(bf16[512,128]{1,0:T(8,128)(2,1)S(1)} %get-tuple-element.38), channel_id=1, source_target_pairs={{0,496},{8,504},{16,0},{24,8},{32,16},{40,24},{48,32},{56,40},{64,... | collective-permute-start | bytes 393224 | tf_op jit(solution)/shard_map/ppermute | solution.py:254
  90.3 9.2 %collective-permute-done.9.far_ref = bf16[512,128]{1,0:T(8,128)(2,1)S(1)} collective-permute-done((bf16[512,128]{1,0:T(8,128)(2,1)S(1)}, bf16[512,128]{1,0:T(8,128)(2,1)S(1)}, u32[]{:S(2)}, u32[]{:S(2)}) %collective-permute-start.9) | collective-permute-done | bytes 131104 | tf_op jit(solution)/shard_map/ppermute | solution.py:254
  99.5 2.8 %collective-permute-done.10.near_ref = bf16[512,128]{1,0:T(8,128)(2,1)S(1)} collective-permute-done((bf16[512,128]{1,0:T(8,128)(2,1)S(1)}, bf16[512,128]{1,0:T(8,128)(2,1)S(1)}, u32[]{:S(2)}, u32[]{:S(2)}) %collective-permute-start.10) | collective-permute-done | bytes 131104 | tf_op jit(solution)/shard_map/ppermute | solution.py:254
  102.3 0.7 shard_map.101
  103.0 0.9 shard_map.99
  (13 shorter events, 0.0 us)
Async XLA Ops:
  2.2 18.5 %all-to-all-start = ((bf16[8,64,128]{2,1,0:T(8,128)(2,1)}), bf16[8,64,128]{2,1,0:T(8,128)(2,1)S(1)}, u32[]{:S(2)}, u32[]{:S(2)}) async-start(bf16[8,64,128]{2,1,0:T(8,128)(2,1)} %shard_map.95), calls=%async_computation | async-start | bytes 262144 | tf_op jit(solution)/shard_map/all_to_all | solution.py:260
  20.7 7.8 %collective-permute-start = (bf16[512,128]{1,0:T(8,128)(2,1)S(1)}, bf16[512,128]{1,0:T(8,128)(2,1)S(1)}, u32[]{:S(2)}, u32[]{:S(2)}) collective-permute-start(bf16[512,128]{1,0:T(8,128)(2,1)S(1)} %bitcast.10), channel_id=1, source_target_pairs={{0,64},{64,128},{128,192},{192,256},{256,320},{320,384},{384,448},... | collective-permute-start | bytes 393224 | tf_op jit(solution)/shard_map/ppermute | solution.py:248
  22.6 34.1 %all-to-all-start.1 = ((bf16[8,528,128]{2,1,0:T(8,128)(2,1)}), bf16[8,528,128]{2,1,0:T(8,128)(2,1)S(1)}, u32[]{:S(2)}, u32[]{:S(2)}) async-start(bf16[8,528,128]{2,1,0:T(8,128)(2,1)} %shard_map.94), calls=%async_computation.1 | async-start | bytes 2162688 | tf_op jit(solution)/shard_map/all_to_all | solution.py:260
  28.5 20.5 %copy-start = (s32[256]{0:T(256)S(1)}, s32[256]{0:T(256)}, u32[]{:S(2)}) copy-start(s32[256]{0:T(256)} %param.13) | copy-start | bytes 3076
  28.7 22.5 %collective-permute-start.3 = (bf16[512,128]{1,0:T(8,128)(2,1)S(1)}, bf16[512,128]{1,0:T(8,128)(2,1)S(1)}, u32[]{:S(2)}, u32[]{:S(2)}) collective-permute-start(bf16[512,128]{1,0:T(8,128)(2,1)S(1)} %get-tuple-element.26), channel_id=1, source_target_pairs={{0,32},{8,40},{16,48},{24,56},{32,0},{40,8},{48,16},{56,24},{1,33}... | collective-permute-start | bytes 393224 | tf_op jit(solution)/shard_map/ppermute | solution.py:248
  37.5 19.1 %collective-permute-start.4 = (bf16[512,128]{1,0:T(8,128)(2,1)S(1)}, bf16[512,128]{1,0:T(8,128)(2,1)S(1)}, u32[]{:S(2)}, u32[]{:S(2)}) collective-permute-start(bf16[512,128]{1,0:T(8,128)(2,1)S(1)} %get-tuple-element.27), channel_id=1, source_target_pairs={{0,24},{8,32},{16,40},{24,48},{32,56},{40,0},{48,8},{56,16},{1,25}... | collective-permute-start | bytes 393224 | tf_op jit(solution)/shard_map/ppermute | solution.py:248
  42.5 14.2 %collective-permute-start.5 = (bf16[512,128]{1,0:T(8,128)(2,1)S(1)}, bf16[512,128]{1,0:T(8,128)(2,1)S(1)}, u32[]{:S(2)}, u32[]{:S(2)}) collective-permute-start(bf16[512,128]{1,0:T(8,128)(2,1)S(1)} %get-tuple-element.28), channel_id=1, source_target_pairs={{0,48},{8,56},{16,0},{24,8},{32,16},{40,24},{48,32},{56,40},{1,49}... | collective-permute-start | bytes 393224 | tf_op jit(solution)/shard_map/ppermute | solution.py:248
  45.9 10.8 %collective-permute-start.6 = (bf16[512,128]{1,0:T(8,128)(2,1)S(1)}, bf16[512,128]{1,0:T(8,128)(2,1)S(1)}, u32[]{:S(2)}, u32[]{:S(2)}) collective-permute-start(bf16[512,128]{1,0:T(8,128)(2,1)S(1)} %get-tuple-element.29), channel_id=1, source_target_pairs={{0,8},{8,16},{16,24},{24,32},{32,40},{40,48},{48,56},{56,0},{1,9},... | collective-permute-start | bytes 393224 | tf_op jit(solution)/shard_map/ppermute | solution.py:248
  49.3 22.5 %collective-permute-start.1 = (bf16[512,128]{1,0:T(8,128)(2,1)S(1)}, bf16[512,128]{1,0:T(8,128)(2,1)S(1)}, u32[]{:S(2)}, u32[]{:S(2)}) collective-permute-start(bf16[512,128]{1,0:T(8,128)(2,1)S(1)} %get-tuple-element.24), channel_id=1, source_target_pairs={{0,40},{8,48},{16,56},{24,0},{32,8},{40,16},{48,24},{56,32},{1,41}... | collective-permute-start | bytes 393224 | tf_op jit(solution)/shard_map/ppermute | solution.py:248
  51.2 20.6 %collective-permute-start.2 = (bf16[512,128]{1,0:T(8,128)(2,1)S(1)}, bf16[512,128]{1,0:T(8,128)(2,1)S(1)}, u32[]{:S(2)}, u32[]{:S(2)}) collective-permute-start(bf16[512,128]{1,0:T(8,128)(2,1)S(1)} %get-tuple-element.25), channel_id=1, source_target_pairs={{0,16},{8,24},{16,32},{24,40},{32,48},{40,56},{48,0},{56,8},{1,17}... | collective-permute-start | bytes 393224 | tf_op jit(solution)/shard_map/ppermute | solution.py:248
  61.4 23.4 %collective-permute-start.7 = (bf16[1024,128]{1,0:T(8,128)(2,1)S(1)}, bf16[1024,128]{1,0:T(8,128)(2,1)S(1)}, u32[]{:S(2)}, u32[]{:S(2)}) collective-permute-start(bf16[1024,128]{1,0:T(8,128)(2,1)S(1)} %get-tuple-element.33), channel_id=1, source_target_pairs={{0,8},{8,16},{16,24},{24,32},{32,40},{40,48},{48,56},{56,64},{64,7... | collective-permute-start | bytes 786440 | tf_op jit(solution)/shard_map/ppermute | solution.py:254
  63.4 21.5 %collective-permute-start.8 = (bf16[1024,128]{1,0:T(8,128)(2,1)S(1)}, bf16[1024,128]{1,0:T(8,128)(2,1)S(1)}, u32[]{:S(2)}, u32[]{:S(2)}) collective-permute-start(bf16[1024,128]{1,0:T(8,128)(2,1)S(1)} %get-tuple-element.34), channel_id=1, source_target_pairs={{0,504},{8,0},{16,8},{24,16},{32,24},{40,32},{48,40},{56,48},{64,5... | collective-permute-start | bytes 786440 | tf_op jit(solution)/shard_map/ppermute | solution.py:254
  76.2 26.8 %all-to-all-start.2 = ((bf16[8,256,128]{2,1,0:T(8,128)(2,1)}), bf16[8,256,128]{2,1,0:T(8,128)(2,1)S(1)}, u32[]{:S(2)}, u32[]{:S(2)}) async-start(bf16[8,256,128]{2,1,0:T(8,128)(2,1)} %get-tuple-element.31), calls=%async_computation.2 | async-start | bytes 1048576 | tf_op jit(solution)/shard_map/all_to_all | solution.py:260
  85.0 14.5 %collective-permute-start.9 = (bf16[512,128]{1,0:T(8,128)(2,1)S(1)}, bf16[512,128]{1,0:T(8,128)(2,1)S(1)}, u32[]{:S(2)}, u32[]{:S(2)}) collective-permute-start(bf16[512,128]{1,0:T(8,128)(2,1)S(1)} %get-tuple-element.37), channel_id=1, source_target_pairs={{0,472},{8,480},{16,488},{24,496},{32,504},{40,0},{48,8},{56,16},{... | collective-permute-start | bytes 393224 | tf_op jit(solution)/shard_map/ppermute | solution.py:254
  86.9 15.4 %collective-permute-start.10 = (bf16[512,128]{1,0:T(8,128)(2,1)S(1)}, bf16[512,128]{1,0:T(8,128)(2,1)S(1)}, u32[]{:S(2)}, u32[]{:S(2)}) collective-permute-start(bf16[512,128]{1,0:T(8,128)(2,1)S(1)} %get-tuple-element.38), channel_id=1, source_target_pairs={{0,496},{8,504},{16,0},{24,8},{32,16},{40,24},{48,32},{56,40},{64,... | collective-permute-start | bytes 393224 | tf_op jit(solution)/shard_map/ppermute | solution.py:254
